TPU v7x, 256 devices: a whole 4x4x8 slice. The times are simulated.
256 devices in a mesh: col: 32 (over x, y, core), rep: 8 (over z).
Axes of the slice: x: 4, y: 4, z: 8, core: 2. Of those that a mesh axis runs over, the one named last changes fastest.
Arguments:
- gradient: bfloat16 [8, 4096, 16384], P('rep', None, 'col'), as said below
- error: bfloat16 [8, 4096, 16384], P('rep', None, 'col'), may hold values from -3 to 3
- warm_start: bfloat16 [32, 16384], P(None, 'col'), as said below
Outputs:
- new_error: bfloat16 [8, 4096, 16384], P('rep', None, 'col')
- q_factor: float32 [32, 16384], P(None, 'col')
Inputs may be any that keep to these rules, and one draw needn't show every extreme that they name: `gradient`: finite values. `warm_start`: finite values.
All inputs are finite; a program needn't handle non-finite values.
Results may differ from a plain program's by a relative error of at most 0.012.
Values may be sent and summed in bfloat16 or wider, within the bound.
No kernel may reach another device: no remote copies, remote signals or barrier semaphores. Data moves between devices by JAX's collectives and lax.ppermute only.
A program may use at most 64 MiB of HBM per device.

v0:
```python
import jax
import jax.numpy as jnp
from jax import lax
from jax.sharding import PartitionSpec as P


def orthonormal(p_rows, gram):
    lower = jnp.linalg.cholesky(gram)
    return jax.scipy.linalg.solve_triangular(lower, p_rows, lower=True).astype(jnp.bfloat16)


def per_device(gradient, error, warm_start):
    merged = (gradient[0].astype(jnp.float32) + error[0].astype(jnp.float32)).astype(jnp.bfloat16)
    partial_value = lax.dot_general(
        warm_start, merged, (((1,), (1,)), ((), ())), preferred_element_type=jnp.float32
    )
    p_sum = lax.psum(partial_value, ("col", "rep"))
    basis = orthonormal(p_sum, jnp.dot(p_sum, p_sum.T, precision=lax.Precision.HIGHEST))
    q_part = jnp.dot(basis, merged, preferred_element_type=jnp.float32)
    q_factor = lax.psum(q_part, "rep") / lax.axis_size("rep")
    q_round = q_factor.astype(jnp.bfloat16)
    rebuilt = lax.dot_general(
        basis, q_round, (((0,), (0,)), ((), ())), preferred_element_type=jnp.float32
    )
    new_error = (merged.astype(jnp.float32) - rebuilt).astype(jnp.bfloat16)
    return (new_error[None], q_factor)


def solution(mesh):
    in_specs = (P("rep", None, "col"), P("rep", None, "col"), P(None, "col"))
    out_specs = (P("rep", None, "col"), P(None, "col"))
    return jax.shard_map(
        per_device, mesh=mesh, in_specs=in_specs, out_specs=out_specs, check_vma=False
    )
```

profile of v0, /device:TPU:1, one launch (start us, length us, event | category | flops | bytes accessed | tf_op | source)
XLA Modules:
  0.0 365.3 jit_solution(536407187986780595)
XLA Ops:
  7.2 0.0 copy-start
  7.2 0.0 all-reduce.3.cloned.1.call-start
  7.2 0.7 copy-done
  7.9 5.6 %convolution_bitcast_fusion = f32[32,4096]{1,0:T(8,128)} fusion(bf16[32,512]{1,0:T(8,128)(2,1)S(1)} %copy-done, bf16[1,4096,512]{2,1,0:T(8,128)(2,1)} %param.4, bf16[1,4096,512]{2,1,0:T(8,128)(2,1)} %param.3), kind=kOutput, calls=%fused_computation.3 | convolution fusion | flops 142606336 | bytes 8945664 | tf_op jit(solution)/shard_map/dot_general | solution.py:14
  13.5 0.0 all-reduce.3.cloned.1.call-update
  13.6 0.0 all-reduce.5.cloned.1.call-start
  13.6 254.9 %all-reduce.3.cloned.1.call-done = f32[32,4096]{1,0:T(8,128)} async-done(((f32[32,4096]{1,0:T(8,128)}), f32[32,4096]{1,0:T(8,128)}) %all-reduce.3.cloned.1.call-update) | async-done | bytes 524304 | tf_op jit(solution)/shard_map/psum | solution.py:17
  268.5 1.8 fusion.9
  270.3 0.1 copy.5
  270.4 2.9 cholesky.16
  273.3 0.6 compare_reduce_fusion
  274.0 0.7 fusion.3
  274.6 2.4 custom-call.7
  277.1 1.7 convolution_convert_fusion
  278.8 5.3 %fusion.6 = f32[32,512]{1,0:T(8,128)} fusion(bf16[32,4096]{1,0:T(8,128)(2,1)S(1)} %convolution_convert_fusion, bf16[1,4096,512]{2,1,0:T(8,128)(2,1)} %param.4, bf16[1,4096,512]{2,1,0:T(8,128)(2,1)} %param.3), kind=kOutput, calls=%fused_computation.17 | convolution fusion | flops 142606336 | bytes 8716288 | tf_op jit(solution)/shard_map/dot_general | solution.py:19
  284.1 0.0 all-reduce.5.cloned.1.call-update
  284.1 66.7 %all-reduce.5.cloned.1.call-done = f32[32,512]{1,0:T(8,128)} async-done(((f32[32,512]{1,0:T(8,128)}), f32[32,512]{1,0:T(8,128)}) %all-reduce.5.cloned.1.call-update) | async-done | bytes 65552 | tf_op jit(solution)/shard_map/psum | solution.py:20
  350.8 0.8 broadcast_multiply_fusion
  351.6 0.0 copy-start.1
  351.6 6.9 %fusion = bf16[1,4096,512]{2,1,0:T(8,128)(2,1)} fusion(bf16[32,4096]{1,0:T(8,128)(2,1)S(1)} %convolution_convert_fusion, f32[32,512]{1,0:T(8,128)S(1)} %broadcast_multiply_fusion, bf16[1,4096,512]{2,1,0:T(8,128)(2,1)} %param.4, bf16[1,4096,512]{2,1,0:T(8,128)(2,1)} %param.3), kind=kOutput, calls=%fused_computation.2 | convolution fusion | flops 148914176 | bytes 12910592 | tf_op jit(solution)/shard_map/dot_general | solution.py:22
  358.5 0.0 copy-done.1
  (2 shorter events, 0.0 us)
Async XLA Ops:
  7.2 0.8 copy-start
  7.2 261.4 %all-reduce.3.cloned.1.call-start = ((), (), s32[]{:S(2)}) async-start(), calls=%async_computation | async-start | bytes 1048576 | tf_op jit(solution)/shard_map/psum | solution.py:17
  13.6 337.2 %all-reduce.5.cloned.1.call-start = ((), (), s32[]{:S(2)}) async-start(), calls=%async_computation.1 | async-start | bytes 131072 | tf_op jit(solution)/shard_map/psum | solution.py:20
  351.6 6.9 %copy-start.1 = (f32[32,512]{1,0:T(8,128)}, f32[32,512]{1,0:T(8,128)S(1)}, u32[]{:S(2)}) copy-start(f32[32,512]{1,0:T(8,128)S(1)} %broadcast_multiply_fusion) | copy-start | bytes 196612
Sparse Core Ops, SparseCore 0:
  14.0 254.4 all-reduce.2
  284.2 66.5 all-reduce.4
where the time goes:
time: 370 us; the launch traced here: 365 us
  waiting for transfers between devices  322 us (87%)
  matrix products  21.2 us (6%)
  between operations  14.1 us (4%)
  other arithmetic  7.53 us (2%)
    psum x1, waiting for transfers between devices, per_device(): p_sum = lax.psum(partial_value, ('col', 'rep'))  255 us
    psum x1, waiting for transfers between devices, per_device(): q_factor = lax.psum(q_part, 'rep') / lax.axis_size('rep')  66.7 us
  transfers between devices with their start and end apart: 2, of which 2 were waited for; matrix products, arithmetic and copies ran while one was open for 0% of the time, Pallas kernels for 0%

commit v1 on v0

v1 whole, which is shorter than its diff:
```python
import jax
import jax.numpy as jnp
from jax import lax
from jax.sharding import PartitionSpec as P

BF16, F32 = jnp.bfloat16, jnp.float32
WIDTH = 128


def exchange(blocks, axis):
    return lax.all_to_all(blocks, axis, 0, 0, tiled=True)


def share(block, axis):
    return exchange(jnp.broadcast_to(block[None], (lax.axis_size(axis),) + block.shape), axis)


def total(blocks):
    return jnp.sum(blocks.astype(F32), axis=0)


def per_device(gradient, error, warm_start):
    rank, rows = warm_start.shape[0], gradient.shape[1]
    merged = (gradient[0].astype(F32) + error[0].astype(F32)).astype(BF16)
    part = lax.dot_general(warm_start, merged, (((1,), (1,)), ((), ())), preferred_element_type=F32)
    blocks = part.reshape(rank, rows // WIDTH, WIDTH).transpose(1, 0, 2)
    with jax.named_scope("left_factor"):
        own = total(exchange(blocks.astype(BF16), "col"))
        own = total(share(own, "rep"))
        p_sum = share(own.astype(BF16), "col").transpose(1, 0, 2).reshape(rank, rows)
    gram = lax.dot_general(p_sum, p_sum, (((1,), (1,)), ((), ())), preferred_element_type=F32)
    lower = jnp.linalg.cholesky(gram)
    inverse = jax.scipy.linalg.solve_triangular(lower, jnp.eye(rank, dtype=F32), lower=True)
    raw = jnp.dot(p_sum, merged, preferred_element_type=F32)
    raw = total(share(raw.astype(BF16), "rep"))
    q_factor = jnp.dot(inverse, raw, precision=lax.Precision.HIGHEST) / lax.axis_size("rep")
    q_round = q_factor.astype(BF16).astype(F32)
    solved = jnp.dot(inverse.T, q_round, precision=lax.Precision.HIGHEST)
    high = solved.astype(BF16)
    low = (solved - high.astype(F32)).astype(BF16)
    rebuilt = lax.dot_general(
        jnp.concatenate([p_sum, p_sum]), jnp.concatenate([high, low]), (((0,), (0,)), ((), ())), preferred_element_type=F32
    )
    new_error = (merged.astype(F32) - rebuilt).astype(BF16)
    return (new_error[None], q_factor)


def solution(mesh):
    in_specs = (P("rep", None, "col"), P("rep", None, "col"), P(None, "col"))
    out_specs = (P("rep", None, "col"), P(None, "col"))
    return jax.shard_map(
        per_device, mesh=mesh, in_specs=in_specs, out_specs=out_specs, check_vma=False
    )
```

time: 370 us -> 86 us (0.23); the launches traced: 365 us -> 85.6 us
  waiting for transfers between devices: 322 us -> 8.31 us
  blocking collectives: 0 us -> 47.4 us
  between operations: 14.1 us -> 0.74 us
  matrix products: 21.2 us -> 17.2 us
    psum x2 -> x0, waiting for transfers between devices: 322 us -> none  [the longest x1 255 us: per_device(): p_sum = lax.psum(partial_value, ('col', 'rep'))]
    all_to_all x0 -> x3, blocking collectives: none -> 47.4 us  [exchange(): return lax.all_to_all(blocks, axis, 0, 0, tiled=True)]
    all_to_all x0 -> x1, waiting for transfers between devices: none -> 8.31 us  [exchange(): return lax.all_to_all(blocks, axis, 0, 0, tiled=True)]
    dot_general x3 -> x5, matrix products: 13.9 us -> 12.2 us  [the longest x1 6.87 us: per_device(): lax.dot_general(jnp.concatenate([p_sum, p_sum]), jnp.concatenate([high, l...]
  transfers between devices with their start and end apart: 2 -> 1, of which waited for: 2 -> 1; matrix products, arithmetic and copies ran while one was open for 0% -> 5% of each run, Pallas kernels for 0% -> 0%
where the time goes in v1:
time: 86 us; the launch traced here: 85.6 us
  blocking collectives  47.4 us (55%)
  matrix products  17.2 us (20%)
  waiting for transfers between devices  8.31 us (10%)
  other arithmetic  6.78 us (8%)
  starting transfers between devices  3.41 us (4%)
  local copies, waits for them, and re-layouts  1.69 us (2%)
    all_to_all x3, blocking collectives, exchange(): return lax.all_to_all(blocks, axis, 0, 0, tiled=True)  47.4 us
    all_to_all x1, waiting for transfers between devices, exchange(): return lax.all_to_all(blocks, axis, 0, 0, tiled=True)  8.31 us
    dot_general x1, matrix products, per_device(): lax.dot_general(jnp.concatenate([p_sum, p_sum]), jnp.concatenate([high, l...  6.87 us
    dot_general x1, matrix products, per_device(): lax.dot_general(warm_start, merged, (((1,), (1,)), ((), ())), preferred_e...  4.82 us
    dot_general x1, matrix products, per_device(): raw = jnp.dot(p_sum, merged, preferred_element_type=F32)  4.7 us
    another operation x3, other arithmetic, per_device(): lower = jnp.linalg.cholesky(gram)  3.59 us
    all_to_all x1, starting transfers between devices, exchange(): return lax.all_to_all(blocks, axis, 0, 0, tiled=True)  3.41 us
    another operation x2, other arithmetic, per_device(): jax.scipy.linalg.solve_triangular(lower, jnp.eye(rank, dtype=F32), lower=...  3.09 us
  transfers between devices with their start and end apart: 1, of which 1 were waited for; matrix products, arithmetic and copies ran while one was open for 5% of the time, Pallas kernels for 0%

profile of v1, /device:TPU:1, one launch (start us, length us, event | category | flops | bytes accessed | tf_op | source)
XLA Modules:
  0.0 85.6 jit_solution(5318943983457680228)
XLA Ops:
  0.6 0.0 copy-start
  0.6 0.7 copy-done
  1.4 4.8 %fusion.2 = bf16[4,32,8,128]{3,2,1,0:T(8,128)(2,1)S(1)} fusion(bf16[32,512]{1,0:T(8,128)(2,1)S(1)} %copy-done, bf16[1,4096,512]{2,1,0:T(8,128)(2,1)} %param.4, bf16[1,4096,512]{2,1,0:T(8,128)(2,1)} %param.3), kind=kOutput, calls=%fused_computation.5 | convolution fusion | flops 142737408 | bytes 8683520 | tf_op jit(solution)/shard_map/dot_general | solution.py:25
  6.3 17.4 %all_to_all.20 = bf16[32,32,128]{2,1,0:T(8,128)(2,1)S(1)} all-to-all(bf16[32,32,128]{2,1,0:T(8,128)(2,1)S(1)} %bitcast.44), channel_id=1, replica_groups=mesh['col'=32,'rep'=8] {'col'}, dimensions={0} | all-to-all | bytes 524288 | tf_op jit(solution)/shard_map/left_factor/all_to_all | solution.py:11
  23.7 16.3 %all_to_all.21 = f32[8,32,128]{2,1,0:T(8,128)S(1)} all-to-all(f32[8,32,128]{2,1,0:T(8,128)S(1)} %broadcast_in_dim.10), channel_id=1, replica_groups=mesh['col'=32,'rep'=8] {'rep'}, dimensions={0} | all-to-all | bytes 262144 | tf_op jit(solution)/shard_map/left_factor/all_to_all | solution.py:11
  40.1 13.8 %all_to_all.22 = bf16[32,32,128]{2,1,0:T(8,128)(2,1)S(1)} all-to-all(bf16[32,32,128]{2,1,0:T(8,128)(2,1)S(1)} %broadcast_in_dim.11), channel_id=1, replica_groups=mesh['col'=32,'rep'=8] {'col'}, dimensions={0} | all-to-all | bytes 524288 | tf_op jit(solution)/shard_map/left_factor/all_to_all | solution.py:11
  53.9 0.2 convolution_bitcast_fusion
  54.0 0.1 copy.13
  54.1 2.9 %cholesky.17 = f32[32,32]{1,0:T(8,128)S(1)} custom-call(f32[32,32]{1,0:T(8,128)S(1)} %fusion.15), custom_call_target="Cholesky" | custom-call | tf_op jit(solution)/shard_map/jit(cholesky)/cholesky | solution.py:32
  57.1 4.7 %convolution_convert_fusion.1 = bf16[32,512]{1,0:T(8,128)(2,1)S(1)} fusion(bf16[1,4096,512]{2,1,0:T(8,128)(2,1)} %param.4, bf16[1,4096,512]{2,1,0:T(8,128)(2,1)} %param.3, bf16[32,32,128]{2,1,0:T(8,128)(2,1)S(1)} %all_to_all.22), kind=kOutput, calls=%fused_computation.7 | convolution fusion | flops 142622720 | bytes 8683520 | tf_op jit(solution)/shard_map/dot_general | solution.py:34
  61.8 0.7 broadcast_in_dim.12
  62.5 3.4 %all-to-all-start.3 = ((bf16[8,32,512]{2,1,0:T(8,128)(2,1)}), bf16[8,32,512]{2,1,0:T(8,128)(2,1)S(1)}, u32[]{:S(2)}, u32[]{:S(2)}) async-start(bf16[8,32,512]{2,1,0:T(8,128)(2,1)} %broadcast_in_dim.12), calls=%async_computation.3 | async-start | bytes 524288 | tf_op jit(solution)/shard_map/all_to_all | solution.py:11
  66.0 0.6 compare_reduce_fusion
  66.6 0.7 fusion.12
  67.3 2.4 %custom-call.7 = f32[1,32,32]{1,2,0:T(8,128)S(1)} custom-call(f32[1,32,32]{2,1,0:T(8,128)S(1)} %fusion.12), custom_call_target="InvertDiagBlocksLowerTriangular" | custom-call | tf_op jit(solution)/shard_map/jit(_solve_triangular)/triangular_solve | solution.py:33
  69.7 0.2 fusion.13
  69.9 8.3 %all-to-all-done.3 = bf16[8,32,512]{2,1,0:T(8,128)(2,1)S(1)} async-done(((bf16[8,32,512]{2,1,0:T(8,128)(2,1)}), bf16[8,32,512]{2,1,0:T(8,128)(2,1)S(1)}, u32[]{:S(2)}, u32[]{:S(2)}) %all-to-all-start.3) | async-done | bytes 262176 | tf_op jit(solution)/shard_map/all_to_all | solution.py:11
  78.3 0.2 convolution_multiply_fusion
  78.5 0.0 copy-start.1
  78.5 0.2 subtract_convert_fusion.1
  78.7 6.9 %fusion = bf16[1,4096,512]{2,1,0:T(8,128)(2,1)} fusion(bf16[32,4096]{1,0:T(8,128)(2,1)S(1)} %copy_bitcast_fusion, bf16[32,512]{1,0:T(8,128)(2,1)S(1)} %get-tuple-element.2, bf16[32,512]{1,0:T(8,128)(2,1)S(1)} %get-tuple-element.3, bf16[1,4096,512]{2,1,0:T(8,128)(2,1)} %param.4, bf16[1,4096,512]{2,1,0:T(8,128)(2,1)} %param.3), kind=kOutput, calls=%fused_computation.2 | convolution fusion | flops 284295168 | bytes 12910592 | tf_op jit(solution)/shard_map/dot_general | solution.py:41
  85.6 0.0 copy-done.1
  (9 shorter events, 0.3 us)
Async XLA Ops:
  0.6 0.8 copy-start
  62.5 15.7 %all-to-all-start.3 = ((bf16[8,32,512]{2,1,0:T(8,128)(2,1)}), bf16[8,32,512]{2,1,0:T(8,128)(2,1)S(1)}, u32[]{:S(2)}, u32[]{:S(2)}) async-start(bf16[8,32,512]{2,1,0:T(8,128)(2,1)} %broadcast_in_dim.12), calls=%async_computation.3 | async-start | bytes 524288 | tf_op jit(solution)/shard_map/all_to_all | solution.py:11
  78.5 7.1 %copy-start.1 = (f32[32,512]{1,0:T(8,128)}, f32[32,512]{1,0:T(8,128)S(1)}, u32[]{:S(2)}) copy-start(f32[32,512]{1,0:T(8,128)S(1)} %convolution_multiply_fusion) | copy-start | bytes 196612

commit v2 on v1

v2 whole, which is shorter than its diff:
```python
import jax
import jax.numpy as jnp
from jax import lax
from jax.experimental import pallas as pl
from jax.experimental.pallas import tpu as pltpu
from jax.sharding import PartitionSpec as P

BF16, F32 = jnp.bfloat16, jnp.float32
HIGHEST = lax.Precision.HIGHEST
LANES = 128
STEP = 512
WHOLE = pl.BlockSpec(memory_space=pltpu.VMEM)
ANYWHERE = pl.BlockSpec(memory_space=pl.ANY)


def params():
    return pltpu.CompilerParams(vmem_limit_bytes=40 << 20)


def in_vmem(array):
    return pltpu.with_memory_space_constraint(array, pltpu.VMEM)


def in_hbm(array):
    return pltpu.with_memory_space_constraint(array, pltpu.HBM)


def rows_of(chunk):
    return pl.ds(chunk * STEP, STEP)


def merge_kernel(gradient, error, warm, merged, part, gradient_in, error_in, warm_in, done):
    chunks = merged.shape[0] // STEP
    copies = [pltpu.make_async_copy(warm, warm_in, done.at[2 * chunks])]
    for chunk in range(chunks):
        here = rows_of(chunk)
        copies.append(pltpu.make_async_copy(gradient.at[0, here, :], gradient_in.at[here, :], done.at[2 * chunk]))
        copies.append(pltpu.make_async_copy(error.at[0, here, :], error_in.at[here, :], done.at[2 * chunk + 1]))
    for copy in copies:
        copy.start()
    copies[0].wait()
    for chunk in range(chunks):
        here = rows_of(chunk)
        copies[2 * chunk + 1].wait()
        copies[2 * chunk + 2].wait()
        value = (gradient_in[here, :].astype(F32) + error_in[here, :].astype(F32)).astype(BF16)
        merged[here, :] = value
        product = lax.dot_general(warm_in[...], value, (((1,), (1,)), ((), ())), preferred_element_type=F32)
        for block in range(STEP // LANES):
            part[chunk * (STEP // LANES) + block] = product[:, block * LANES : (block + 1) * LANES].astype(BF16)


def merge(gradient, error, warm):
    _, rows, columns = gradient.shape
    rank = warm.shape[0]
    return pl.pallas_call(
        merge_kernel,
        in_specs=[ANYWHERE] * 3,
        out_specs=[WHOLE, WHOLE],
        out_shape=[
            pltpu.VMEM((rows, columns), BF16),
            pltpu.VMEM((rows // LANES, rank, LANES), BF16),
        ],
        scratch_shapes=[
            pltpu.VMEM((rows, columns), BF16),
            pltpu.VMEM((rows, columns), BF16),
            pltpu.VMEM((rank, columns), BF16),
            pltpu.SemaphoreType.DMA((2 * (rows // STEP) + 1,)),
        ],
        compiler_params=params(),
        cost_estimate=pl.CostEstimate(flops=2 * rank * rows * columns, bytes_accessed=4 * rows * columns, transcendentals=0),
        name="merge",
    )(in_hbm(gradient), in_hbm(error), in_hbm(warm))


def side_by_side(blocks):
    return jnp.concatenate([blocks[i] for i in range(blocks.shape[0])], axis=1)


def raw_kernel(p_sum, merged, raw):
    value = jnp.dot(side_by_side(p_sum), merged[...], preferred_element_type=F32).astype(BF16)
    for copy in range(raw.shape[0]):
        raw[copy] = value


def raw_factor(p_sum, merged, copies):
    rows, columns = merged.shape
    rank = p_sum.shape[1]
    return pl.pallas_call(
        raw_kernel,
        in_specs=[WHOLE, WHOLE],
        out_specs=WHOLE,
        out_shape=pltpu.VMEM((copies, rank, columns), BF16),
        compiler_params=params(),
        cost_estimate=pl.CostEstimate(flops=2 * rank * rows * columns, bytes_accessed=2 * rows * columns, transcendentals=0),
        name="raw_factor",
    )(in_vmem(p_sum), in_vmem(merged))


def solve_kernel(p_sum, inverse, turned):
    rank = p_sum.shape[1]
    wide = side_by_side(p_sum)
    gram = lax.dot_general(wide, wide, (((1,), (1,)), ((), ())), preferred_element_type=F32)
    row = lax.broadcasted_iota(jnp.int32, (rank, rank), 0)
    col = lax.broadcasted_iota(jnp.int32, (rank, rank), 1)
    one = (row == col).astype(F32)
    table = jnp.concatenate([gram, one], axis=1)
    below = lax.broadcasted_iota(jnp.int32, (rank, 1), 0)
    for k in range(rank):
        pivot = table[k : k + 1, :]
        factor = jnp.where(below > k, table[:, k : k + 1] / pivot[:, k : k + 1], 0.0)
        table = table - factor * pivot
    diagonal = jnp.sum(table[:, :rank] * one, axis=1, keepdims=True)
    inverse[...] = table[:, rank:] * lax.rsqrt(diagonal)
    for block in range(p_sum.shape[0]):
        tall = p_sum[block].astype(F32).T.astype(BF16)
        turned[pl.ds(block * LANES, LANES), :] = jnp.concatenate([tall, tall], axis=1)


def solve(p_sum):
    blocks, rank, lanes = p_sum.shape
    return pl.pallas_call(
        solve_kernel,
        in_specs=[WHOLE],
        out_specs=[WHOLE, WHOLE],
        out_shape=[pltpu.VMEM((rank, rank), F32), pltpu.VMEM((blocks * lanes, 2 * rank), BF16)],
        compiler_params=params(),
        cost_estimate=pl.CostEstimate(flops=2 * rank * rank * blocks * lanes, bytes_accessed=2 << 20, transcendentals=0),
        name="solve",
    )(in_vmem(p_sum))


def finish_kernel(replicas, raw, inverse, turned, merged, new_error, q_factor, halves, result, done):
    total = jnp.sum(raw[...].astype(F32), axis=0)
    factor = jnp.dot(inverse[...], total, precision=HIGHEST, preferred_element_type=F32) * (1.0 / replicas)
    q_factor[...] = factor
    rounded = factor.astype(BF16).astype(F32)
    solved = lax.dot_general(
        inverse[...], rounded, (((0,), (0,)), ((), ())), precision=HIGHEST, preferred_element_type=F32
    )
    high = solved.astype(BF16)
    halves[...] = jnp.concatenate([high, (solved - high.astype(F32)).astype(BF16)], axis=0)
    copies = []
    for chunk in range(merged.shape[0] // STEP):
        here = rows_of(chunk)
        rebuilt = jnp.dot(turned[here, :], halves[...], preferred_element_type=F32)
        result[here, :] = (merged[here, :].astype(F32) - rebuilt).astype(BF16)
        copies.append(pltpu.make_async_copy(result.at[here, :], new_error.at[0, here, :], done.at[chunk]))
        copies[-1].start()
    for copy in copies:
        copy.wait()


def finish(raw, inverse, turned, merged, replicas):
    rows, columns = merged.shape
    rank = inverse.shape[0]
    return pl.pallas_call(
        lambda *refs: finish_kernel(replicas, *refs),
        in_specs=[WHOLE] * 4,
        out_specs=[ANYWHERE, WHOLE],
        out_shape=[
            pltpu.HBM((1, rows, columns), BF16),
            jax.ShapeDtypeStruct((rank, columns), F32),
        ],
        scratch_shapes=[
            pltpu.VMEM((2 * rank, columns), BF16),
            pltpu.VMEM((rows, columns), BF16),
            pltpu.SemaphoreType.DMA((rows // STEP,)),
        ],
        compiler_params=params(),
        cost_estimate=pl.CostEstimate(flops=4 * rank * rows * columns, bytes_accessed=4 * rows * columns, transcendentals=0),
        name="finish",
    )(in_vmem(raw), in_vmem(inverse), in_vmem(turned), in_vmem(merged))


def exchange(blocks, axis):
    return lax.all_to_all(blocks, axis, 0, 0, tiled=True)


def share(block, axis):
    return exchange(jnp.broadcast_to(block[None], (lax.axis_size(axis),) + block.shape), axis)


def total(blocks):
    return jnp.sum(blocks.astype(F32), axis=0)


def per_device(gradient, error, warm_start):
    replicas = lax.axis_size("rep")
    merged, part = merge(gradient, error, warm_start)
    own = total(exchange(part, "col"))
    own = total(share(own, "rep"))
    p_sum = share(own.astype(BF16), "col")
    raw = exchange(raw_factor(p_sum, merged, replicas), "rep")
    inverse, turned = solve(p_sum)
    return tuple(finish(raw, inverse, turned, merged, replicas))


def solution(mesh):
    in_specs = (P("rep", None, "col"), P("rep", None, "col"), P(None, "col"))
    out_specs = (P("rep", None, "col"), P(None, "col"))
    return jax.shard_map(
        per_device, mesh=mesh, in_specs=in_specs, out_specs=out_specs, check_vma=False
    )
```

time: 86 us -> 79.4 us (0.923)
  matrix products: 17.2 us -> 0 us
  Pallas kernels: 0 us -> 11.7 us
  other arithmetic: 6.78 us -> 0.06 us
  local copies, waits for them, and re-layouts: 1.69 us -> 6.43 us
  waiting for transfers between devices: 8.31 us -> 9.26 us
    dot_general x6 -> x0, matrix products: 17 us -> none  [the longest x1 6.87 us: per_device(): lax.dot_general(jnp.concatenate([p_sum, p_sum]), jnp.concatenate([high, l...]
    pallas_call x0 -> x4, Pallas kernels: none -> 11.7 us  [the longest x1 3.81 us: merge(): pl.pallas_call(merge_kernel, in_specs=[ANYWHERE] * 3, out_specs=[WHOLE, W...]
    another operation x5 -> x0, other arithmetic: 6.68 us -> none  [the longest x3 3.59 us: per_device(): lower = jnp.linalg.cholesky(gram)]
    unnamed x4 -> x6, local copies, waits for them, and re-layouts: 0.76 us -> 6.38 us
    all_to_all x1, waiting for transfers between devices: 8.31 us -> 9.26 us  [exchange(): return lax.all_to_all(blocks, axis, 0, 0, tiled=True)]
  transfers between devices with their start and end apart: 1 -> 1, of which waited for: 1 -> 1; matrix products, arithmetic and copies ran while one was open for 5% -> 0% of each run, Pallas kernels for 0% -> 4%
where the time goes in v2:
time: 79.4 us; the launch traced here: 79 us
  blocking collectives  47.4 us (60%)
  Pallas kernels  11.7 us (15%)
  waiting for transfers between devices  9.26 us (12%)
  local copies, waits for them, and re-layouts  6.43 us (8%)
  starting transfers between devices  3.41 us (4%)
    all_to_all x3, blocking collectives, exchange(): return lax.all_to_all(blocks, axis, 0, 0, tiled=True)  47.4 us
    all_to_all x1, waiting for transfers between devices, exchange(): return lax.all_to_all(blocks, axis, 0, 0, tiled=True)  9.26 us
    unnamed x6, local copies, waits for them, and re-layouts  6.38 us
    pallas_call x1, Pallas kernels, merge(): pl.pallas_call(merge_kernel, in_specs=[ANYWHERE] * 3, out_specs=[WHOLE, W...  3.81 us
    all_to_all x1, starting transfers between devices, exchange(): return lax.all_to_all(blocks, axis, 0, 0, tiled=True)  3.41 us
    pallas_call x1, Pallas kernels, finish(): pl.pallas_call(lambda *refs: finish_kernel(replicas, *refs), in_specs=[WH...  3.38 us
    pallas_call x1, Pallas kernels, solve(): pl.pallas_call(solve_kernel, in_specs=[WHOLE], out_specs=[WHOLE, WHOLE],...  3.02 us
  transfers between devices with their start and end apart: 1, of which 1 were waited for; matrix products, arithmetic and copies ran while one was open for 0% of the time, Pallas kernels for 4%

profile of v2, /device:TPU:1, one launch (start us, length us, event | category | flops | bytes accessed | tf_op | source)
XLA Modules:
  0.0 79.0 jit_solution(10400152826979774410)
XLA Ops:
  0.6 3.8 %merge.1 = (bf16[4096,512]{1,0:T(8,128)(2,1)S(1)}, bf16[32,32,128]{2,1,0:T(8,128)(2,1)S(1)}) custom-call(bf16[1,4096,512]{2,1,0:T(8,128)(2,1)} %gradient.1, bf16[1,4096,512]{2,1,0:T(8,128)(2,1)} %error.1, bf16[32,512]{1,0:T(8,128)(2,1)} %warm.1), custom_call_target="tpu_custom_call" | custom-call | flops 134217728 | bytes 8388608 | tf_op jit(solution)/shard_map/merge/pallas_call | solution.py:56
  4.4 0.0 copy-start
  4.5 2.0 %copy-done = bf16[4096,512]{1,0:T(8,128)(2,1)} copy-done((bf16[4096,512]{1,0:T(8,128)(2,1)}, bf16[4096,512]{1,0:T(8,128)(2,1)S(1)}, u32[]{:S(2)}) %copy-start) | copy-done | bytes 4194328
  6.5 17.4 %all_to_all.20 = bf16[32,32,128]{2,1,0:T(8,128)(2,1)S(1)} all-to-all(bf16[32,32,128]{2,1,0:T(8,128)(2,1)S(1)} %get-tuple-element.6), channel_id=1, replica_groups=mesh['col'=32,'rep'=8] {'col'}, dimensions={0} | all-to-all | bytes 524288 | tf_op jit(solution)/shard_map/all_to_all | solution.py:177
  23.9 16.3 %all_to_all.21 = f32[8,32,128]{2,1,0:T(8,128)S(1)} all-to-all(f32[8,32,128]{2,1,0:T(8,128)S(1)} %broadcast_in_dim.4), channel_id=1, replica_groups=mesh['col'=32,'rep'=8] {'rep'}, dimensions={0} | all-to-all | bytes 262144 | tf_op jit(solution)/shard_map/all_to_all | solution.py:177
  40.2 13.8 %all_to_all.22.p_sum = bf16[32,32,128]{2,1,0:T(8,128)(2,1)S(1)} all-to-all(bf16[32,32,128]{2,1,0:T(8,128)(2,1)S(1)} %broadcast_in_dim.5), channel_id=1, replica_groups=mesh['col'=32,'rep'=8] {'col'}, dimensions={0} | all-to-all | bytes 524288 | tf_op jit(solution)/shard_map/all_to_all | solution.py:177
  54.0 0.0 copy-start.1
  54.0 2.2 %copy-done.1 = bf16[4096,512]{1,0:T(8,128)(2,1)S(1)} copy-done((bf16[4096,512]{1,0:T(8,128)(2,1)S(1)}, bf16[4096,512]{1,0:T(8,128)(2,1)}, u32[]{:S(2)}) %copy-start.1) | copy-done | bytes 4194328
  56.2 1.5 %raw_factor.1 = bf16[8,32,512]{2,1,0:T(8,128)(2,1)} custom-call(bf16[32,32,128]{2,1,0:T(8,128)(2,1)S(1)} %all_to_all.22.p_sum, bf16[4096,512]{1,0:T(8,128)(2,1)S(1)} %copy-done.1), custom_call_target="tpu_custom_call" | custom-call | flops 134217728 | bytes 4194304 | tf_op jit(solution)/shard_map/raw_factor/pallas_call | solution.py:89
  57.7 3.4 %all-to-all-start.3 = ((bf16[8,32,512]{2,1,0:T(8,128)(2,1)}), bf16[8,32,512]{2,1,0:T(8,128)(2,1)S(1)}, u32[]{:S(2)}, u32[]{:S(2)}) async-start(bf16[8,32,512]{2,1,0:T(8,128)(2,1)} %raw_factor.1), calls=%async_computation.3 | async-start | bytes 524288 | tf_op jit(solution)/shard_map/all_to_all | solution.py:177
  61.2 3.0 %solve.1 = (f32[32,32]{1,0:T(8,128)S(1)}, bf16[4096,64]{1,0:T(8,128)(2,1)S(1)}) custom-call(bf16[32,32,128]{2,1,0:T(8,128)(2,1)S(1)} %all_to_all.22.p_sum), custom_call_target="tpu_custom_call" | custom-call | flops 8388608 | bytes 2097152 | tf_op jit(solution)/shard_map/solve/pallas_call | solution.py:122
  64.2 9.3 %all-to-all-done.3.refs_0_ = bf16[8,32,512]{2,1,0:T(8,128)(2,1)S(1)} async-done(((bf16[8,32,512]{2,1,0:T(8,128)(2,1)}), bf16[8,32,512]{2,1,0:T(8,128)(2,1)S(1)}, u32[]{:S(2)}, u32[]{:S(2)}) %all-to-all-start.3) | async-done | bytes 262176 | tf_op jit(solution)/shard_map/all_to_all | solution.py:177
  73.4 0.0 copy-start.2
  73.4 2.2 %copy-done.2 = bf16[4096,512]{1,0:T(8,128)(2,1)S(1)} copy-done((bf16[4096,512]{1,0:T(8,128)(2,1)S(1)}, bf16[4096,512]{1,0:T(8,128)(2,1)}, u32[]{:S(2)}) %copy-start.2) | copy-done | bytes 4194328
  75.6 3.4 %finish.1 = (bf16[1,4096,512]{2,1,0:T(8,128)(2,1)}, f32[32,512]{1,0:T(8,128)}) custom-call(bf16[8,32,512]{2,1,0:T(8,128)(2,1)S(1)} %all-to-all-done.3.refs_0_, f32[32,32]{1,0:T(8,128)S(1)} %get-tuple-element.8.refs_1_, bf16[4096,64]{1,0:T(8,128)(2,1)S(1)} %get-tuple-element.9.refs_2_, bf16[4096,512]{1,0:T(8,128)(2,1)S(1)} %copy-done.2), custom_call_target="tpu_custom_call" | custom-call | flops 268435456 | bytes 8388608 | tf_op jit(solution)/shard_map/finish/pallas_call | solution.py:157
  (4 shorter events, 0.1 us)
Async XLA Ops:
  4.4 2.0 %copy-start = (bf16[4096,512]{1,0:T(8,128)(2,1)}, bf16[4096,512]{1,0:T(8,128)(2,1)S(1)}, u32[]{:S(2)}) copy-start(bf16[4096,512]{1,0:T(8,128)(2,1)S(1)} %get-tuple-element.7.merged.refs_3_) | copy-start | bytes 12582916
  54.0 2.2 %copy-start.1 = (bf16[4096,512]{1,0:T(8,128)(2,1)S(1)}, bf16[4096,512]{1,0:T(8,128)(2,1)}, u32[]{:S(2)}) copy-start(bf16[4096,512]{1,0:T(8,128)(2,1)} %copy-done) | copy-start | bytes 12582916
  57.7 15.7 %all-to-all-start.3 = ((bf16[8,32,512]{2,1,0:T(8,128)(2,1)}), bf16[8,32,512]{2,1,0:T(8,128)(2,1)S(1)}, u32[]{:S(2)}, u32[]{:S(2)}) async-start(bf16[8,32,512]{2,1,0:T(8,128)(2,1)} %raw_factor.1), calls=%async_computation.3 | async-start | bytes 524288 | tf_op jit(solution)/shard_map/all_to_all | solution.py:177
  73.4 2.2 %copy-start.2 = (bf16[4096,512]{1,0:T(8,128)(2,1)S(1)}, bf16[4096,512]{1,0:T(8,128)(2,1)}, u32[]{:S(2)}) copy-start(bf16[4096,512]{1,0:T(8,128)(2,1)} %copy-done) | copy-start | bytes 12582916

commit v3 on v2

--- a/solution.py
+++ b/solution.py
@@ -77,30 +77,16 @@
     return jnp.concatenate([blocks[i] for i in range(blocks.shape[0])], axis=1)
 
 
-def raw_kernel(p_sum, merged, raw):
-    value = jnp.dot(side_by_side(p_sum), merged[...], preferred_element_type=F32).astype(BF16)
+def factor_kernel(p_sum, merged, raw, inverse, turned):
+    blocks, rank, lanes = p_sum.shape
+    wide = side_by_side(p_sum)
+    gram = lax.dot_general(wide, wide, (((1,), (1,)), ((), ())), preferred_element_type=F32)
+    value = jnp.dot(wide, merged[...], preferred_element_type=F32).astype(BF16)
     for copy in range(raw.shape[0]):
         raw[copy] = value
-
-
-def raw_factor(p_sum, merged, copies):
-    rows, columns = merged.shape
-    rank = p_sum.shape[1]
-    return pl.pallas_call(
-        raw_kernel,
-        in_specs=[WHOLE, WHOLE],
-        out_specs=WHOLE,
-        out_shape=pltpu.VMEM((copies, rank, columns), BF16),
-        compiler_params=params(),
-        cost_estimate=pl.CostEstimate(flops=2 * rank * rows * columns, bytes_accessed=2 * rows * columns, transcendentals=0),
-        name="raw_factor",
-    )(in_vmem(p_sum), in_vmem(merged))
-
-
-def solve_kernel(p_sum, inverse, turned):
-    rank = p_sum.shape[1]
-    wide = side_by_side(p_sum)
-    gram = lax.dot_general(wide, wide, (((1,), (1,)), ((), ())), preferred_element_type=F32)
+    for block in range(blocks):
+        tall = p_sum[block].astype(F32).T.astype(BF16)
+        turned[pl.ds(block * lanes, lanes), :] = jnp.concatenate([tall, tall], axis=1)
     row = lax.broadcasted_iota(jnp.int32, (rank, rank), 0)
     col = lax.broadcasted_iota(jnp.int32, (rank, rank), 1)
     one = (row == col).astype(F32)
@@ -112,22 +98,24 @@
         table = table - factor * pivot
     diagonal = jnp.sum(table[:, :rank] * one, axis=1, keepdims=True)
     inverse[...] = table[:, rank:] * lax.rsqrt(diagonal)
-    for block in range(p_sum.shape[0]):
-        tall = p_sum[block].astype(F32).T.astype(BF16)
-        turned[pl.ds(block * LANES, LANES), :] = jnp.concatenate([tall, tall], axis=1)
 
 
-def solve(p_sum):
-    blocks, rank, lanes = p_sum.shape
+def factor(p_sum, merged, copies):
+    rows, columns = merged.shape
+    rank = p_sum.shape[1]
     return pl.pallas_call(
-        solve_kernel,
-        in_specs=[WHOLE],
-        out_specs=[WHOLE, WHOLE],
-        out_shape=[pltpu.VMEM((rank, rank), F32), pltpu.VMEM((blocks * lanes, 2 * rank), BF16)],
+        factor_kernel,
+        in_specs=[WHOLE, WHOLE],
+        out_specs=[WHOLE] * 3,
+        out_shape=[
+            pltpu.VMEM((copies, rank, columns), BF16),
+            pltpu.VMEM((rank, rank), F32),
+            pltpu.VMEM((rows, 2 * rank), BF16),
+        ],
         compiler_params=params(),
-        cost_estimate=pl.CostEstimate(flops=2 * rank * rank * blocks * lanes, bytes_accessed=2 << 20, transcendentals=0),
-        name="solve",
-    )(in_vmem(p_sum))
+        cost_estimate=pl.CostEstimate(flops=2 * rank * rows * columns, bytes_accessed=2 * rows * columns, transcendentals=0),
+        name="factor",
+    )(in_vmem(p_sum), in_vmem(merged))
 
 
 def finish_kernel(replicas, raw, inverse, turned, merged, new_error, q_factor, halves, result, done):
@@ -182,7 +170,10 @@
 
 
 def total(blocks):
-    return jnp.sum(blocks.astype(F32), axis=0)
+    terms = [blocks[i].astype(F32) for i in range(blocks.shape[0])]
+    while len(terms) > 1:
+        terms = [a + b for a, b in zip(terms[::2], terms[1::2])]
+    return terms[0]
 
 
 def per_device(gradient, error, warm_start):
@@ -191,8 +182,8 @@
     own = total(exchange(part, "col"))
     own = total(share(own, "rep"))
     p_sum = share(own.astype(BF16), "col")
-    raw = exchange(raw_factor(p_sum, merged, replicas), "rep")
-    inverse, turned = solve(p_sum)
+    raw, inverse, turned = factor(p_sum, merged, replicas)
+    raw = exchange(raw, "rep")
     return tuple(finish(raw, inverse, turned, merged, replicas))
 
 

time: 79.4 us -> 73.7 us (0.928)
  blocking collectives: 47.4 us -> 62.2 us
  waiting for transfers between devices: 9.26 us -> 0 us
  local copies, waits for them, and re-layouts: 6.43 us -> 0.05 us
  starting transfers between devices: 3.41 us -> 0 us
  Pallas kernels: 11.7 us -> 10.5 us
    all_to_all x3 -> x4, blocking collectives: 47.4 us -> 62.2 us  [exchange(): return lax.all_to_all(blocks, axis, 0, 0, tiled=True)]
    all_to_all x1 -> x0, waiting for transfers between devices: 9.26 us -> none  [exchange(): return lax.all_to_all(blocks, axis, 0, 0, tiled=True)]
    unnamed x6 -> x0, local copies, waits for them, and re-layouts: 6.38 us -> none
    all_to_all x1 -> x0, starting transfers between devices: 3.41 us -> none  [exchange(): return lax.all_to_all(blocks, axis, 0, 0, tiled=True)]
    pallas_call x2 -> x1, Pallas kernels: 4.54 us -> 3.3 us  [factor(): pl.pallas_call(factor_kernel, in_specs=[WHOLE, WHOLE], out_specs=[WHOLE]...]
  transfers between devices with their start and end apart: 1 -> 0, of which waited for: 1 -> 0; matrix products, arithmetic and copies ran while one was open for 0% -> 0% of each run, Pallas kernels for 4% -> 0%
where the time goes in v3:
time: 73.7 us; the launch traced here: 73.5 us
  blocking collectives  62.2 us (84%)
  Pallas kernels  10.5 us (14%)
    all_to_all x4, blocking collectives, exchange(): return lax.all_to_all(blocks, axis, 0, 0, tiled=True)  62.2 us
    pallas_call x1, Pallas kernels, merge(): pl.pallas_call(merge_kernel, in_specs=[ANYWHERE] * 3, out_specs=[WHOLE, W...  3.81 us
    pallas_call x1, Pallas kernels, finish(): pl.pallas_call(lambda *refs: finish_kernel(replicas, *refs), in_specs=[WH...  3.38 us
    pallas_call x1, Pallas kernels, factor(): pl.pallas_call(factor_kernel, in_specs=[WHOLE, WHOLE], out_specs=[WHOLE]...  3.3 us

profile of v3, /device:TPU:1, one launch (start us, length us, event | category | flops | bytes accessed | tf_op | source)
XLA Modules:
  0.0 73.5 jit_solution(1123120928178107187)
XLA Ops:
  0.6 3.8 %merge.1 = (bf16[4096,512]{1,0:T(8,128)(2,1)S(1)}, bf16[32,32,128]{2,1,0:T(8,128)(2,1)S(1)}) custom-call(bf16[1,4096,512]{2,1,0:T(8,128)(2,1)} %gradient.1, bf16[1,4096,512]{2,1,0:T(8,128)(2,1)} %error.1, bf16[32,512]{1,0:T(8,128)(2,1)} %warm.1), custom_call_target="tpu_custom_call" | custom-call | flops 134217728 | bytes 8388608 | tf_op jit(solution)/shard_map/merge/pallas_call | solution.py:56
  4.4 17.4 %all_to_all.20 = bf16[32,32,128]{2,1,0:T(8,128)(2,1)S(1)} all-to-all(bf16[32,32,128]{2,1,0:T(8,128)(2,1)S(1)} %get-tuple-element.7), channel_id=1, replica_groups=mesh['col'=32,'rep'=8] {'col'}, dimensions={0} | all-to-all | bytes 524288 | tf_op jit(solution)/shard_map/all_to_all | solution.py:165
  21.9 16.3 %all_to_all.21 = f32[8,32,128]{2,1,0:T(8,128)S(1)} all-to-all(f32[8,32,128]{2,1,0:T(8,128)S(1)} %broadcast_in_dim.17), channel_id=1, replica_groups=mesh['col'=32,'rep'=8] {'rep'}, dimensions={0} | all-to-all | bytes 262144 | tf_op jit(solution)/shard_map/all_to_all | solution.py:165
  38.2 13.8 %all_to_all.22.p_sum = bf16[32,32,128]{2,1,0:T(8,128)(2,1)S(1)} all-to-all(bf16[32,32,128]{2,1,0:T(8,128)(2,1)S(1)} %broadcast_in_dim.19), channel_id=1, replica_groups=mesh['col'=32,'rep'=8] {'col'}, dimensions={0} | all-to-all | bytes 524288 | tf_op jit(solution)/shard_map/all_to_all | solution.py:165
  52.0 3.3 %factor.1 = (bf16[8,32,512]{2,1,0:T(8,128)(2,1)S(1)}, f32[32,32]{1,0:T(8,128)S(1)}, bf16[4096,64]{1,0:T(8,128)(2,1)S(1)}) custom-call(bf16[32,32,128]{2,1,0:T(8,128)(2,1)S(1)} %all_to_all.22.p_sum, bf16[4096,512]{1,0:T(8,128)(2,1)S(1)} %get-tuple-element.8.merged.refs_3_), custom_call_target="tpu_custom_call" | custom-call | flops 134217728 | bytes 4194304 | tf_op jit(solution)/shard_map/factor/pallas_call | solution.py:106
  55.3 14.8 %all_to_all.23.refs_0_ = bf16[8,32,512]{2,1,0:T(8,128)(2,1)S(1)} all-to-all(bf16[8,32,512]{2,1,0:T(8,128)(2,1)S(1)} %get-tuple-element.9), channel_id=1, replica_groups=mesh['col'=32,'rep'=8] {'rep'}, dimensions={0} | all-to-all | bytes 524288 | tf_op jit(solution)/shard_map/all_to_all | solution.py:165
  70.1 3.4 %finish.1 = (bf16[1,4096,512]{2,1,0:T(8,128)(2,1)}, f32[32,512]{1,0:T(8,128)}) custom-call(bf16[8,32,512]{2,1,0:T(8,128)(2,1)S(1)} %all_to_all.23.refs_0_, f32[32,32]{1,0:T(8,128)S(1)} %get-tuple-element.10.refs_1_, bf16[4096,64]{1,0:T(8,128)(2,1)S(1)} %get-tuple-element.11.refs_2_, bf16[4096,512]{1,0:T(8,128)(2,1)S(1)} %get-tuple-element.8.merged.refs_3_), custom_call_target="tpu_custom_call" | custom-call | flops 268435456 | bytes 8388608 | tf_op jit(solution)/shard_map/finish/pallas_call | solution.py:145
  (4 shorter events, 0.1 us)

commit v4 on v2

--- a/solution.py
+++ b/solution.py
@@ -78,19 +78,17 @@
 
 
 def raw_kernel(p_sum, merged, raw):
-    value = jnp.dot(side_by_side(p_sum), merged[...], preferred_element_type=F32).astype(BF16)
-    for copy in range(raw.shape[0]):
-        raw[copy] = value
-
-
-def raw_factor(p_sum, merged, copies):
+    raw[...] = jnp.dot(side_by_side(p_sum), merged[...], preferred_element_type=F32).astype(BF16)
+
+
+def raw_factor(p_sum, merged):
     rows, columns = merged.shape
     rank = p_sum.shape[1]
     return pl.pallas_call(
         raw_kernel,
         in_specs=[WHOLE, WHOLE],
         out_specs=WHOLE,
-        out_shape=pltpu.VMEM((copies, rank, columns), BF16),
+        out_shape=pltpu.VMEM((rank, columns), BF16),
         compiler_params=params(),
         cost_estimate=pl.CostEstimate(flops=2 * rank * rows * columns, bytes_accessed=2 * rows * columns, transcendentals=0),
         name="raw_factor",
@@ -98,9 +96,12 @@
 
 
 def solve_kernel(p_sum, inverse, turned):
-    rank = p_sum.shape[1]
+    blocks, rank, lanes = p_sum.shape
     wide = side_by_side(p_sum)
     gram = lax.dot_general(wide, wide, (((1,), (1,)), ((), ())), preferred_element_type=F32)
+    for block in range(blocks):
+        tall = p_sum[block].astype(F32).T.astype(BF16)
+        turned[pl.ds(block * lanes, lanes), :] = jnp.concatenate([tall, tall], axis=1)
     row = lax.broadcasted_iota(jnp.int32, (rank, rank), 0)
     col = lax.broadcasted_iota(jnp.int32, (rank, rank), 1)
     one = (row == col).astype(F32)
@@ -112,9 +113,6 @@
         table = table - factor * pivot
     diagonal = jnp.sum(table[:, :rank] * one, axis=1, keepdims=True)
     inverse[...] = table[:, rank:] * lax.rsqrt(diagonal)
-    for block in range(p_sum.shape[0]):
-        tall = p_sum[block].astype(F32).T.astype(BF16)
-        turned[pl.ds(block * LANES, LANES), :] = jnp.concatenate([tall, tall], axis=1)
 
 
 def solve(p_sum):
@@ -125,14 +123,14 @@
         out_specs=[WHOLE, WHOLE],
         out_shape=[pltpu.VMEM((rank, rank), F32), pltpu.VMEM((blocks * lanes, 2 * rank), BF16)],
         compiler_params=params(),
-        cost_estimate=pl.CostEstimate(flops=2 * rank * rank * blocks * lanes, bytes_accessed=2 << 20, transcendentals=0),
+        cost_estimate=pl.CostEstimate(flops=16 * rank * rank * blocks * lanes, bytes_accessed=4 << 20, transcendentals=0),
         name="solve",
     )(in_vmem(p_sum))
 
 
-def finish_kernel(replicas, raw, inverse, turned, merged, new_error, q_factor, halves, result, done):
-    total = jnp.sum(raw[...].astype(F32), axis=0)
-    factor = jnp.dot(inverse[...], total, precision=HIGHEST, preferred_element_type=F32) * (1.0 / replicas)
+def finish_kernel(replicas, mine, theirs, inverse, turned, merged, new_error, q_factor, halves, result, done):
+    raw = mine[...].astype(F32) + theirs[...].astype(F32)
+    factor = jnp.dot(inverse[...], raw, precision=HIGHEST, preferred_element_type=F32) * (1.0 / replicas)
     q_factor[...] = factor
     rounded = factor.astype(BF16).astype(F32)
     solved = lax.dot_general(
@@ -151,12 +149,12 @@
         copy.wait()
 
 
-def finish(raw, inverse, turned, merged, replicas):
+def finish(mine, theirs, inverse, turned, merged, replicas):
     rows, columns = merged.shape
     rank = inverse.shape[0]
     return pl.pallas_call(
         lambda *refs: finish_kernel(replicas, *refs),
-        in_specs=[WHOLE] * 4,
+        in_specs=[WHOLE] * 5,
         out_specs=[ANYWHERE, WHOLE],
         out_shape=[
             pltpu.HBM((1, rows, columns), BF16),
@@ -170,7 +168,7 @@
         compiler_params=params(),
         cost_estimate=pl.CostEstimate(flops=4 * rank * rows * columns, bytes_accessed=4 * rows * columns, transcendentals=0),
         name="finish",
-    )(in_vmem(raw), in_vmem(inverse), in_vmem(turned), in_vmem(merged))
+    )(in_vmem(mine), in_vmem(theirs), in_vmem(inverse), in_vmem(turned), in_vmem(merged))
 
 
 def exchange(blocks, axis):
@@ -182,7 +180,14 @@
 
 
 def total(blocks):
-    return jnp.sum(blocks.astype(F32), axis=0)
+    terms = [blocks[i].astype(F32) for i in range(blocks.shape[0])]
+    while len(terms) > 1:
+        terms = [a + b for a, b in zip(terms[::2], terms[1::2])]
+    return terms[0]
+
+
+def swap(block, axis, mask):
+    return lax.ppermute(block, axis, [(i, i ^ mask) for i in range(lax.axis_size(axis))])
 
 
 def per_device(gradient, error, warm_start):
@@ -191,9 +196,12 @@
     own = total(exchange(part, "col"))
     own = total(share(own, "rep"))
     p_sum = share(own.astype(BF16), "col")
-    raw = exchange(raw_factor(p_sum, merged, replicas), "rep")
+    raw = raw_factor(p_sum, merged)
     inverse, turned = solve(p_sum)
-    return tuple(finish(raw, inverse, turned, merged, replicas))
+    masks = [2**bit ^ (2 ** (bit - 1) if bit > 1 else 0) for bit in range(replicas.bit_length() - 1)]
+    for mask in masks[:-1]:
+        raw = (raw.astype(F32) + swap(raw, "rep", mask).astype(F32)).astype(BF16)
+    return tuple(finish(raw, swap(raw, "rep", masks[-1]), inverse, turned, merged, replicas))
 
 
 def solution(mesh):

time: 79.4 us -> 69.5 us (0.88)
  the two profiles are of different devices: /device:TPU:1 before, /device:TPU:2 now
where the time goes in v4:
time: 69.5 us; the launch traced here: 69.3 us
  blocking collectives  45.2 us (65%)
  waiting for transfers between devices  11.4 us (16%)
  Pallas kernels  11.1 us (16%)
  starting transfers between devices  0.77 us (1%)
    all_to_all x3, blocking collectives, exchange(): return lax.all_to_all(blocks, axis, 0, 0, tiled=True)  45.2 us
    ppermute x3, waiting for transfers between devices, swap(): lax.ppermute(block, axis, [(i, i ^ mask) for i in range(lax.axis_size(axi...  11.4 us
    pallas_call x1, Pallas kernels, merge(): pl.pallas_call(merge_kernel, in_specs=[ANYWHERE] * 3, out_specs=[WHOLE, W...  3.81 us
    pallas_call x1, Pallas kernels, finish(): pl.pallas_call(lambda *refs: finish_kernel(replicas, *refs), in_specs=[WH...  3.35 us
    pallas_call x1, Pallas kernels, solve(): pl.pallas_call(solve_kernel, in_specs=[WHOLE], out_specs=[WHOLE, WHOLE],...  3.16 us
  transfers between devices with their start and end apart: 3, of which 3 were waited for; matrix products, arithmetic and copies ran while one was open for 0% of the time, Pallas kernels for 5%

profile of v4, /device:TPU:2, one launch (start us, length us, event | category | flops | bytes accessed | tf_op | source)
XLA Modules:
  0.0 69.3 jit_solution(4276991938631535441)
XLA Ops:
  0.6 3.8 %merge.1 = (bf16[4096,512]{1,0:T(8,128)(2,1)S(1)}, bf16[32,32,128]{2,1,0:T(8,128)(2,1)S(1)}) custom-call(bf16[1,4096,512]{2,1,0:T(8,128)(2,1)} %gradient.1, bf16[1,4096,512]{2,1,0:T(8,128)(2,1)} %error.1, bf16[32,512]{1,0:T(8,128)(2,1)} %warm.1), custom_call_target="tpu_custom_call" | custom-call | flops 134217728 | bytes 8388608 | tf_op jit(solution)/shard_map/merge/pallas_call | solution.py:56
  4.4 15.1 %all_to_all.15 = bf16[32,32,128]{2,1,0:T(8,128)(2,1)S(1)} all-to-all(bf16[32,32,128]{2,1,0:T(8,128)(2,1)S(1)} %get-tuple-element.6), channel_id=1, replica_groups=mesh['col'=32,'rep'=8] {'col'}, dimensions={0} | all-to-all | bytes 524288 | tf_op jit(solution)/shard_map/all_to_all | solution.py:175
  19.7 17.8 %all_to_all.16 = f32[8,32,128]{2,1,0:T(8,128)S(1)} all-to-all(f32[8,32,128]{2,1,0:T(8,128)S(1)} %broadcast_in_dim.17), channel_id=1, replica_groups=mesh['col'=32,'rep'=8] {'rep'}, dimensions={0} | all-to-all | bytes 262144 | tf_op jit(solution)/shard_map/all_to_all | solution.py:175
  37.5 12.3 %all_to_all.17.p_sum = bf16[32,32,128]{2,1,0:T(8,128)(2,1)S(1)} all-to-all(bf16[32,32,128]{2,1,0:T(8,128)(2,1)S(1)} %broadcast_in_dim.19), channel_id=1, replica_groups=mesh['col'=32,'rep'=8] {'col'}, dimensions={0} | all-to-all | bytes 524288 | tf_op jit(solution)/shard_map/all_to_all | solution.py:175
  49.8 0.8 %raw_factor.1 = bf16[32,512]{1,0:T(8,128)(2,1)S(1)} custom-call(bf16[32,32,128]{2,1,0:T(8,128)(2,1)S(1)} %all_to_all.17.p_sum, bf16[4096,512]{1,0:T(8,128)(2,1)S(1)} %get-tuple-element.7.merged.refs_4_), custom_call_target="tpu_custom_call" | custom-call | flops 134217728 | bytes 4194304 | tf_op jit(solution)/shard_map/raw_factor/pallas_call | solution.py:87
  50.6 0.5 collective-permute-start
  51.1 3.4 %collective-permute-done = bf16[32,512]{1,0:T(8,128)(2,1)S(1)} collective-permute-done((bf16[32,512]{1,0:T(8,128)(2,1)S(1)}, bf16[32,512]{1,0:T(8,128)(2,1)S(1)}, u32[]{:S(2)}, u32[]{:S(2)}) %collective-permute-start) | collective-permute-done | bytes 32800 | tf_op jit(solution)/shard_map/ppermute | solution.py:190
  54.5 0.2 collective-permute-start.1
  54.7 5.1 %collective-permute-done.1 = bf16[32,512]{1,0:T(8,128)(2,1)S(1)} collective-permute-done((bf16[32,512]{1,0:T(8,128)(2,1)S(1)}, bf16[32,512]{1,0:T(8,128)(2,1)S(1)}, u32[]{:S(2)}, u32[]{:S(2)}) %collective-permute-start.1) | collective-permute-done | bytes 32800 | tf_op jit(solution)/shard_map/ppermute | solution.py:190
  59.8 0.1 collective-permute-start.2
  59.9 3.2 %solve.1 = (f32[32,32]{1,0:T(8,128)S(1)}, bf16[4096,64]{1,0:T(8,128)(2,1)S(1)}) custom-call(bf16[32,32,128]{2,1,0:T(8,128)(2,1)S(1)} %all_to_all.17.p_sum), custom_call_target="tpu_custom_call" | custom-call | flops 67108864 | bytes 4194304 | tf_op jit(solution)/shard_map/solve/pallas_call | solution.py:120
  63.1 2.8 %collective-permute-done.2.refs_1_ = bf16[32,512]{1,0:T(8,128)(2,1)S(1)} collective-permute-done((bf16[32,512]{1,0:T(8,128)(2,1)S(1)}, bf16[32,512]{1,0:T(8,128)(2,1)S(1)}, u32[]{:S(2)}, u32[]{:S(2)}) %collective-permute-start.2) | collective-permute-done | bytes 32800 | tf_op jit(solution)/shard_map/ppermute | solution.py:190
  65.9 3.4 %finish.1 = (bf16[1,4096,512]{2,1,0:T(8,128)(2,1)}, f32[32,512]{1,0:T(8,128)}) custom-call(bf16[32,512]{1,0:T(8,128)(2,1)S(1)} %add_convert_fusion.refs_0_, bf16[32,512]{1,0:T(8,128)(2,1)S(1)} %collective-permute-done.2.refs_1_, f32[32,32]{1,0:T(8,128)S(1)} %get-tuple-element.8.refs_2_, bf16[4096,64]{1,0:T(8,128)(2,1)S(1)} %get-tuple-element.9.refs_3_, ...), custom_call_target="tpu_custom_call" | custom-call | flops 268435456 | bytes 8388608 | tf_op jit(solution)/shard_map/finish/pallas_call | solution.py:155
  (6 shorter events, 0.1 us)
Async XLA Ops:
  50.6 3.9 %collective-permute-start = (bf16[32,512]{1,0:T(8,128)(2,1)S(1)}, bf16[32,512]{1,0:T(8,128)(2,1)S(1)}, u32[]{:S(2)}, u32[]{:S(2)}) collective-permute-start(bf16[32,512]{1,0:T(8,128)(2,1)S(1)} %raw_factor.1), channel_id=1, source_target_pairs={{0,1},{1,0},{2,3},{3,2},{4,5},{5,4},{6,7},{7,6},{8,9},{9,8},{10,11... | collective-permute-start | bytes 98312 | tf_op jit(solution)/shard_map/ppermute | solution.py:190
  54.5 5.3 %collective-permute-start.1 = (bf16[32,512]{1,0:T(8,128)(2,1)S(1)}, bf16[32,512]{1,0:T(8,128)(2,1)S(1)}, u32[]{:S(2)}, u32[]{:S(2)}) collective-permute-start(bf16[32,512]{1,0:T(8,128)(2,1)S(1)} %add_convert_fusion.1), channel_id=1, source_target_pairs={{0,2},{1,3},{2,0},{3,1},{4,6},{5,7},{6,4},{7,5},{8,10},{9,11},{10,... | collective-permute-start | bytes 98312 | tf_op jit(solution)/shard_map/ppermute | solution.py:190
  59.8 6.1 %collective-permute-start.2 = (bf16[32,512]{1,0:T(8,128)(2,1)S(1)}, bf16[32,512]{1,0:T(8,128)(2,1)S(1)}, u32[]{:S(2)}, u32[]{:S(2)}) collective-permute-start(bf16[32,512]{1,0:T(8,128)(2,1)S(1)} %add_convert_fusion.refs_0_), channel_id=1, source_target_pairs={{0,6},{1,7},{2,4},{3,5},{4,2},{5,3},{6,0},{7,1},{8,14},{9,15},{10,... | collective-permute-start | bytes 98312 | tf_op jit(solution)/shard_map/ppermute | solution.py:190

commit v5 on v4

--- a/solution.py
+++ b/solution.py
@@ -180,7 +180,7 @@
 
 
 def total(blocks):
-    terms = [blocks[i].astype(F32) for i in range(blocks.shape[0])]
+    terms = [block.astype(F32) for block in blocks]
     while len(terms) > 1:
         terms = [a + b for a, b in zip(terms[::2], terms[1::2])]
     return terms[0]
@@ -194,14 +194,12 @@
     replicas = lax.axis_size("rep")
     merged, part = merge(gradient, error, warm_start)
     own = total(exchange(part, "col"))
-    own = total(share(own, "rep"))
+    own = total(share(own.astype(BF16), "rep"))
     p_sum = share(own.astype(BF16), "col")
     raw = raw_factor(p_sum, merged)
     inverse, turned = solve(p_sum)
-    masks = [2**bit ^ (2 ** (bit - 1) if bit > 1 else 0) for bit in range(replicas.bit_length() - 1)]
-    for mask in masks[:-1]:
-        raw = (raw.astype(F32) + swap(raw, "rep", mask).astype(F32)).astype(BF16)
-    return tuple(finish(raw, swap(raw, "rep", masks[-1]), inverse, turned, merged, replicas))
+    raw = total([raw] + [swap(raw, "rep", mask) for mask in (1, 2, 3)]).astype(BF16)
+    return tuple(finish(raw, swap(raw, "rep", 6), inverse, turned, merged, replicas))
 
 
 def solution(mesh):

time: 69.5 us -> 66.6 us (0.958)
  the two profiles are of different devices: /device:TPU:2 before, /device:TPU:1 now
where the time goes in v5:
time: 66.6 us; the launch traced here: 65.7 us
  blocking collectives  46.5 us (70%)
  Pallas kernels  11.1 us (17%)
  starting transfers between devices  4.47 us (7%)
  waiting for transfers between devices  2.82 us (4%)
    all_to_all x3, blocking collectives, exchange(): return lax.all_to_all(blocks, axis, 0, 0, tiled=True)  46.5 us
    ppermute x4, starting transfers between devices, swap(): lax.ppermute(block, axis, [(i, i ^ mask) for i in range(lax.axis_size(axi...  4.47 us
    pallas_call x1, Pallas kernels, merge(): pl.pallas_call(merge_kernel, in_specs=[ANYWHERE] * 3, out_specs=[WHOLE, W...  3.81 us
    pallas_call x1, Pallas kernels, finish(): pl.pallas_call(lambda *refs: finish_kernel(replicas, *refs), in_specs=[WH...  3.35 us
    pallas_call x1, Pallas kernels, solve(): pl.pallas_call(solve_kernel, in_specs=[WHOLE], out_specs=[WHOLE, WHOLE],...  3.16 us
    ppermute x4, waiting for transfers between devices, swap(): lax.ppermute(block, axis, [(i, i ^ mask) for i in range(lax.axis_size(axi...  2.82 us
  transfers between devices with their start and end apart: 4, of which 3 were waited for; matrix products, arithmetic and copies ran while one was open for 0% of the time, Pallas kernels for 5%

profile of v5, /device:TPU:1, one launch (start us, length us, event | category | flops | bytes accessed | tf_op | source)
XLA Modules:
  0.0 65.7 jit_solution(7304951049394466056)
XLA Ops:
  0.6 3.8 %merge.1 = (bf16[4096,512]{1,0:T(8,128)(2,1)S(1)}, bf16[32,32,128]{2,1,0:T(8,128)(2,1)S(1)}) custom-call(bf16[1,4096,512]{2,1,0:T(8,128)(2,1)} %gradient.1, bf16[1,4096,512]{2,1,0:T(8,128)(2,1)} %error.1, bf16[32,512]{1,0:T(8,128)(2,1)} %warm.1), custom_call_target="tpu_custom_call" | custom-call | flops 134217728 | bytes 8388608 | tf_op jit(solution)/shard_map/merge/pallas_call | solution.py:56
  4.4 17.4 %all_to_all.15 = bf16[32,32,128]{2,1,0:T(8,128)(2,1)S(1)} all-to-all(bf16[32,32,128]{2,1,0:T(8,128)(2,1)S(1)} %get-tuple-element.6), channel_id=1, replica_groups=mesh['col'=32,'rep'=8] {'col'}, dimensions={0} | all-to-all | bytes 524288 | tf_op jit(solution)/shard_map/all_to_all | solution.py:175
  21.9 15.2 %all_to_all.16 = bf16[8,32,128]{2,1,0:T(8,128)(2,1)S(1)} all-to-all(bf16[8,32,128]{2,1,0:T(8,128)(2,1)S(1)} %broadcast_in_dim.17), channel_id=1, replica_groups=mesh['col'=32,'rep'=8] {'rep'}, dimensions={0} | all-to-all | bytes 131072 | tf_op jit(solution)/shard_map/all_to_all | solution.py:175
  37.1 13.9 %all_to_all.17.p_sum = bf16[32,32,128]{2,1,0:T(8,128)(2,1)S(1)} all-to-all(bf16[32,32,128]{2,1,0:T(8,128)(2,1)S(1)} %broadcast_in_dim.19), channel_id=1, replica_groups=mesh['col'=32,'rep'=8] {'col'}, dimensions={0} | all-to-all | bytes 524288 | tf_op jit(solution)/shard_map/all_to_all | solution.py:175
  51.0 0.8 %raw_factor.1 = bf16[32,512]{1,0:T(8,128)(2,1)S(1)} custom-call(bf16[32,32,128]{2,1,0:T(8,128)(2,1)S(1)} %all_to_all.17.p_sum, bf16[4096,512]{1,0:T(8,128)(2,1)S(1)} %get-tuple-element.7.merged.refs_4_), custom_call_target="tpu_custom_call" | custom-call | flops 134217728 | bytes 4194304 | tf_op jit(solution)/shard_map/raw_factor/pallas_call | solution.py:87
  51.9 0.2 collective-permute-start.2
  52.0 1.3 %collective-permute-start.1 = (bf16[32,512]{1,0:T(8,128)(2,1)S(1)}, bf16[32,512]{1,0:T(8,128)(2,1)S(1)}, u32[]{:S(2)}, u32[]{:S(2)}) collective-permute-start(bf16[32,512]{1,0:T(8,128)(2,1)S(1)} %raw_factor.1), channel_id=1, source_target_pairs={{0,2},{1,3},{2,0},{3,1},{4,6},{5,7},{6,4},{7,5},{8,10},{9,11},{10,... | collective-permute-start | bytes 98312 | tf_op jit(solution)/shard_map/ppermute | solution.py:190
  53.3 2.1 %collective-permute-start = (bf16[32,512]{1,0:T(8,128)(2,1)S(1)}, bf16[32,512]{1,0:T(8,128)(2,1)S(1)}, u32[]{:S(2)}, u32[]{:S(2)}) collective-permute-start(bf16[32,512]{1,0:T(8,128)(2,1)S(1)} %raw_factor.1), channel_id=1, source_target_pairs={{0,1},{1,0},{2,3},{3,2},{4,5},{5,4},{6,7},{7,6},{8,9},{9,8},{10,11... | collective-permute-start | bytes 98312 | tf_op jit(solution)/shard_map/ppermute | solution.py:190
  55.4 1.0 %collective-permute-done.2 = bf16[32,512]{1,0:T(8,128)(2,1)S(1)} collective-permute-done((bf16[32,512]{1,0:T(8,128)(2,1)S(1)}, bf16[32,512]{1,0:T(8,128)(2,1)S(1)}, u32[]{:S(2)}, u32[]{:S(2)}) %collective-permute-start.2) | collective-permute-done | bytes 32800 | tf_op jit(solution)/shard_map/ppermute | solution.py:190
  56.5 0.0 collective-permute-done.1
  56.5 0.8 %collective-permute-done = bf16[32,512]{1,0:T(8,128)(2,1)S(1)} collective-permute-done((bf16[32,512]{1,0:T(8,128)(2,1)S(1)}, bf16[32,512]{1,0:T(8,128)(2,1)S(1)}, u32[]{:S(2)}, u32[]{:S(2)}) %collective-permute-start) | collective-permute-done | bytes 32800 | tf_op jit(solution)/shard_map/ppermute | solution.py:190
  57.3 0.9 %collective-permute-start.3 = (bf16[32,512]{1,0:T(8,128)(2,1)S(1)}, bf16[32,512]{1,0:T(8,128)(2,1)S(1)}, u32[]{:S(2)}, u32[]{:S(2)}) collective-permute-start(bf16[32,512]{1,0:T(8,128)(2,1)S(1)} %add_convert_fusion.refs_0_), channel_id=1, source_target_pairs={{0,6},{1,7},{2,4},{3,5},{4,2},{5,3},{6,0},{7,1},{8,14},{9,15},{10,... | collective-permute-start | bytes 98312 | tf_op jit(solution)/shard_map/ppermute | solution.py:190
  58.2 3.2 %solve.1 = (f32[32,32]{1,0:T(8,128)S(1)}, bf16[4096,64]{1,0:T(8,128)(2,1)S(1)}) custom-call(bf16[32,32,128]{2,1,0:T(8,128)(2,1)S(1)} %all_to_all.17.p_sum), custom_call_target="tpu_custom_call" | custom-call | flops 67108864 | bytes 4194304 | tf_op jit(solution)/shard_map/solve/pallas_call | solution.py:120
  61.3 1.0 %collective-permute-done.3.refs_1_ = bf16[32,512]{1,0:T(8,128)(2,1)S(1)} collective-permute-done((bf16[32,512]{1,0:T(8,128)(2,1)S(1)}, bf16[32,512]{1,0:T(8,128)(2,1)S(1)}, u32[]{:S(2)}, u32[]{:S(2)}) %collective-permute-start.3) | collective-permute-done | bytes 32800 | tf_op jit(solution)/shard_map/ppermute | solution.py:190
  62.3 3.4 %finish.1 = (bf16[1,4096,512]{2,1,0:T(8,128)(2,1)}, f32[32,512]{1,0:T(8,128)}) custom-call(bf16[32,512]{1,0:T(8,128)(2,1)S(1)} %add_convert_fusion.refs_0_, bf16[32,512]{1,0:T(8,128)(2,1)S(1)} %collective-permute-done.3.refs_1_, f32[32,32]{1,0:T(8,128)S(1)} %get-tuple-element.8.refs_2_, bf16[4096,64]{1,0:T(8,128)(2,1)S(1)} %get-tuple-element.9.refs_3_, ...), custom_call_target="tpu_custom_call" | custom-call | flops 268435456 | bytes 8388608 | tf_op jit(solution)/shard_map/finish/pallas_call | solution.py:155
  (5 shorter events, 0.1 us)
Async XLA Ops:
  51.9 4.6 %collective-permute-start.2 = (bf16[32,512]{1,0:T(8,128)(2,1)S(1)}, bf16[32,512]{1,0:T(8,128)(2,1)S(1)}, u32[]{:S(2)}, u32[]{:S(2)}) collective-permute-start(bf16[32,512]{1,0:T(8,128)(2,1)S(1)} %raw_factor.1), channel_id=1, source_target_pairs={{0,3},{1,2},{2,1},{3,0},{4,7},{5,6},{6,5},{7,4},{8,11},{9,10},{10,... | collective-permute-start | bytes 98312 | tf_op jit(solution)/shard_map/ppermute | solution.py:190
  52.0 4.5 %collective-permute-start.1 = (bf16[32,512]{1,0:T(8,128)(2,1)S(1)}, bf16[32,512]{1,0:T(8,128)(2,1)S(1)}, u32[]{:S(2)}, u32[]{:S(2)}) collective-permute-start(bf16[32,512]{1,0:T(8,128)(2,1)S(1)} %raw_factor.1), channel_id=1, source_target_pairs={{0,2},{1,3},{2,0},{3,1},{4,6},{5,7},{6,4},{7,5},{8,10},{9,11},{10,... | collective-permute-start | bytes 98312 | tf_op jit(solution)/shard_map/ppermute | solution.py:190
  53.3 3.9 %collective-permute-start = (bf16[32,512]{1,0:T(8,128)(2,1)S(1)}, bf16[32,512]{1,0:T(8,128)(2,1)S(1)}, u32[]{:S(2)}, u32[]{:S(2)}) collective-permute-start(bf16[32,512]{1,0:T(8,128)(2,1)S(1)} %raw_factor.1), channel_id=1, source_target_pairs={{0,1},{1,0},{2,3},{3,2},{4,5},{5,4},{6,7},{7,6},{8,9},{9,8},{10,11... | collective-permute-start | bytes 98312 | tf_op jit(solution)/shard_map/ppermute | solution.py:190
  57.3 5.1 %collective-permute-start.3 = (bf16[32,512]{1,0:T(8,128)(2,1)S(1)}, bf16[32,512]{1,0:T(8,128)(2,1)S(1)}, u32[]{:S(2)}, u32[]{:S(2)}) collective-permute-start(bf16[32,512]{1,0:T(8,128)(2,1)S(1)} %add_convert_fusion.refs_0_), channel_id=1, source_target_pairs={{0,6},{1,7},{2,4},{3,5},{4,2},{5,3},{6,0},{7,1},{8,14},{9,15},{10,... | collective-permute-start | bytes 98312 | tf_op jit(solution)/shard_map/ppermute | solution.py:190

commit v6 on v5

v6 whole, which is shorter than its diff:
```python
import jax
import jax.numpy as jnp
from jax import lax
from jax.experimental import pallas as pl
from jax.experimental.pallas import tpu as pltpu
from jax.sharding import PartitionSpec as P

BF16, F32 = jnp.bfloat16, jnp.float32
HIGHEST = lax.Precision.HIGHEST
CORES = 2
LANES = 128
STEP = 512
WHOLE = pl.BlockSpec(memory_space=pltpu.VMEM)
ANYWHERE = pl.BlockSpec(memory_space=pl.ANY)


def params():
    return pltpu.CompilerParams(vmem_limit_bytes=40 << 20)


def in_vmem(array):
    return pltpu.with_memory_space_constraint(array, pltpu.VMEM)


def in_hbm(array):
    return pltpu.with_memory_space_constraint(array, pltpu.HBM)


def rows_of(chunk, first=0):
    return pl.ds(pl.multiple_of(first + chunk * STEP, STEP), STEP)


def core():
    return lax.rem(lax.axis_index("col"), CORES)


def merge_kernel(own, gradient, error, warm, merged, part, gradient_in, error_in, warm_in, done):
    chunks = merged.shape[0] // STEP
    first = (core() if own else 1 - core()) * merged.shape[0]
    copies = [pltpu.make_async_copy(warm, warm_in, done.at[2 * chunks])]
    for chunk in range(chunks):
        here, there = rows_of(chunk), rows_of(chunk, first)
        copies.append(pltpu.make_async_copy(gradient.at[0, there, :], gradient_in.at[here, :], done.at[2 * chunk]))
        copies.append(pltpu.make_async_copy(error.at[0, there, :], error_in.at[here, :], done.at[2 * chunk + 1]))
    for copy in copies:
        copy.start()
    copies[0].wait()
    for chunk in range(chunks):
        here = rows_of(chunk)
        copies[2 * chunk + 1].wait()
        copies[2 * chunk + 2].wait()
        value = (gradient_in[here, :].astype(F32) + error_in[here, :].astype(F32)).astype(BF16)
        merged[here, :] = value
        product = lax.dot_general(warm_in[...], value, (((1,), (1,)), ((), ())), preferred_element_type=F32)
        for block in range(STEP // LANES):
            part[chunk * (STEP // LANES) + block] = product[:, block * LANES : (block + 1) * LANES].astype(part.dtype)


def merge(gradient, error, warm, own):
    _, rows, columns = gradient.shape
    rank, half = warm.shape[0], rows // CORES
    return pl.pallas_call(
        lambda *refs: merge_kernel(own, *refs),
        in_specs=[ANYWHERE] * 3,
        out_specs=[WHOLE, WHOLE],
        out_shape=[
            pltpu.VMEM((half, columns), BF16),
            pltpu.VMEM((half // LANES, rank, LANES), F32 if own else BF16),
        ],
        scratch_shapes=[
            pltpu.VMEM((half, columns), BF16),
            pltpu.VMEM((half, columns), BF16),
            pltpu.VMEM((rank, columns), BF16),
            pltpu.SemaphoreType.DMA((2 * (half // STEP) + 1,)),
        ],
        compiler_params=params(),
        cost_estimate=pl.CostEstimate(flops=2 * rank * half * columns, bytes_accessed=4 * half * columns, transcendentals=0),
        name="merge_own" if own else "merge_other",
    )(in_hbm(gradient), in_hbm(error), in_hbm(warm))


def side_by_side(blocks):
    return jnp.concatenate([blocks[i] for i in range(blocks.shape[0])], axis=1)


def half_kernel(p_half, merged, raw):
    raw[...] = jnp.dot(side_by_side(p_half), merged[...], preferred_element_type=F32)


def rest_kernel(p_half, merged, begun, raw):
    raw[...] = (begun[...] + jnp.dot(side_by_side(p_half), merged[...], preferred_element_type=F32)).astype(BF16)


def raw_factor(p_half, merged, *begun):
    half, columns = merged.shape
    rank = p_half.shape[1]
    return pl.pallas_call(
        rest_kernel if begun else half_kernel,
        in_specs=[WHOLE] * (2 + len(begun)),
        out_specs=WHOLE,
        out_shape=pltpu.VMEM((rank, columns), BF16 if begun else F32),
        compiler_params=params(),
        cost_estimate=pl.CostEstimate(flops=2 * rank * half * columns, bytes_accessed=2 * half * columns, transcendentals=0),
        name="raw_rest" if begun else "raw_half",
    )(*(in_vmem(x) for x in (p_half, merged, *begun)))


def solve_kernel(*refs):
    *halves, inverse, turned = refs
    blocks, rank, lanes = halves[0].shape
    gram = 0.0
    for place, half in enumerate(halves):
        wide = side_by_side(half)
        gram += lax.dot_general(wide, wide, (((1,), (1,)), ((), ())), preferred_element_type=F32)
        for block in range(blocks):
            tall = half[block].astype(F32).T.astype(BF16)
            turned[pl.ds((place * blocks + block) * lanes, lanes), :] = jnp.concatenate([tall, tall], axis=1)
    row = lax.broadcasted_iota(jnp.int32, (rank, rank), 0)
    col = lax.broadcasted_iota(jnp.int32, (rank, rank), 1)
    one = (row == col).astype(F32)
    table = jnp.concatenate([gram, one], axis=1)
    below = lax.broadcasted_iota(jnp.int32, (rank, 1), 0)
    for k in range(rank):
        pivot = table[k : k + 1, :]
        factor = jnp.where(below > k, table[:, k : k + 1] / pivot[:, k : k + 1], 0.0)
        table = table - factor * pivot
    diagonal = jnp.sum(table[:, :rank] * one, axis=1, keepdims=True)
    inverse[...] = table[:, rank:] * lax.rsqrt(diagonal)


def solve(*halves):
    blocks, rank, lanes = halves[0].shape
    rows = len(halves) * blocks * lanes
    return pl.pallas_call(
        solve_kernel,
        in_specs=[WHOLE] * len(halves),
        out_specs=[WHOLE, WHOLE],
        out_shape=[pltpu.VMEM((rank, rank), F32), pltpu.VMEM((rows, 2 * rank), BF16)],
        compiler_params=params(),
        cost_estimate=pl.CostEstimate(flops=16 * rank * rank * rows, bytes_accessed=4 << 20, transcendentals=0),
        name="solve",
    )(*(in_vmem(half) for half in halves))


def finish_kernel(replicas, mine, theirs, inverse, turned, own, other, new_error, q_factor, halves, result, done):
    raw = mine[...].astype(F32) + theirs[...].astype(F32)
    factor = jnp.dot(inverse[...], raw, precision=HIGHEST, preferred_element_type=F32) * (1.0 / replicas)
    q_factor[...] = factor
    rounded = factor.astype(BF16).astype(F32)
    solved = lax.dot_general(
        inverse[...], rounded, (((0,), (0,)), ((), ())), precision=HIGHEST, preferred_element_type=F32
    )
    high = solved.astype(BF16)
    halves[...] = jnp.concatenate([high, (solved - high.astype(F32)).astype(BF16)], axis=0)
    copies = []
    half = own.shape[0]
    for merged, first, begin in ((own, core() * half, 0), (other, (1 - core()) * half, half)):
        for chunk in range(half // STEP):
            place = begin // STEP + chunk
            here = rows_of(place)
            rebuilt = jnp.dot(turned[here, :], halves[...], preferred_element_type=F32)
            result[here, :] = (merged[rows_of(chunk), :].astype(F32) - rebuilt).astype(BF16)
            copies.append(
                pltpu.make_async_copy(result.at[here, :], new_error.at[0, rows_of(chunk, first), :], done.at[place])
            )
            copies[-1].start()
    for copy in copies:
        copy.wait()


def finish(mine, theirs, inverse, turned, own, other, replicas):
    half, columns = own.shape
    rows, rank = 2 * half, inverse.shape[0]
    return pl.pallas_call(
        lambda *refs: finish_kernel(replicas, *refs),
        in_specs=[WHOLE] * 6,
        out_specs=[ANYWHERE, WHOLE],
        out_shape=[
            pltpu.HBM((1, rows, columns), BF16),
            jax.ShapeDtypeStruct((rank, columns), F32),
        ],
        scratch_shapes=[
            pltpu.VMEM((2 * rank, columns), BF16),
            pltpu.VMEM((rows, columns), BF16),
            pltpu.SemaphoreType.DMA((rows // STEP,)),
        ],
        compiler_params=params(),
        cost_estimate=pl.CostEstimate(flops=4 * rank * rows * columns, bytes_accessed=4 * rows * columns, transcendentals=0),
        name="finish",
    )(*(in_vmem(x) for x in (mine, theirs, inverse, turned, own, other)))


def exchange(blocks, axis, groups=None):
    return lax.all_to_all(blocks, axis, 0, 0, axis_index_groups=groups, tiled=True)


def share(block, axis, groups=None):
    count = len(groups[0]) if groups else lax.axis_size(axis)
    return exchange(jnp.broadcast_to(block[None], (count,) + block.shape), axis, groups)


def swap(block, axis, mask):
    return lax.ppermute(block, axis, [(i, i ^ mask) for i in range(lax.axis_size(axis))])


def total(blocks):
    terms = [block.astype(F32) for block in blocks]
    while len(terms) > 1:
        terms = [a + b for a, b in zip(terms[::2], terms[1::2])]
    return terms[0]


def per_device(gradient, error, warm_start):
    replicas = lax.axis_size("rep")
    chips = [list(range(c, lax.axis_size("col"), CORES)) for c in range(CORES)]
    other, part_other = merge(gradient, error, warm_start, own=False)
    part_other = swap(part_other, "col", 1)
    own, part = merge(gradient, error, warm_start, own=True)
    part = (part + part_other.astype(F32)).astype(BF16)
    block = total(exchange(part, "col", chips))
    block = total(share(block.astype(BF16), "rep"))
    p_own = share(block.astype(BF16), "col", chips)
    p_other = swap(p_own, "col", 1)
    raw = raw_factor(p_other, other, raw_factor(p_own, own))
    inverse, turned = solve(p_own, p_other)
    raw = total([raw] + [swap(raw, "rep", mask) for mask in (1, 2, 3)]).astype(BF16)
    return tuple(finish(raw, swap(raw, "rep", 6), inverse, turned, own, other, replicas))


def solution(mesh):
    in_specs = (P("rep", None, "col"), P("rep", None, "col"), P(None, "col"))
    out_specs = (P("rep", None, "col"), P(None, "col"))
    return jax.shard_map(
        per_device, mesh=mesh, in_specs=in_specs, out_specs=out_specs, check_vma=False
    )
```

time: 66.6 us -> 66.4 us (level)
  the two profiles are of different devices: /device:TPU:1 before, /device:TPU:32 now
where the time goes in v6:
time: 66.4 us; the launch traced here: 66.2 us
  blocking collectives  41.2 us (62%)
  Pallas kernels  12.4 us (19%)
  waiting for transfers between devices  7.75 us (12%)
  starting transfers between devices  4.03 us (6%)
  between operations  0.7 us (1%)
    all_to_all x3, blocking collectives, exchange(): lax.all_to_all(blocks, axis, 0, 0, axis_index_groups=groups, tiled=True)  41.2 us
    ppermute x6, waiting for transfers between devices, swap(): lax.ppermute(block, axis, [(i, i ^ mask) for i in range(lax.axis_size(axi...  7.75 us
    pallas_call x2, Pallas kernels, merge(): pl.pallas_call(lambda *refs: merge_kernel(own, *refs), in_specs=[ANYWHERE...  5.1 us
    ppermute x6, starting transfers between devices, swap(): lax.ppermute(block, axis, [(i, i ^ mask) for i in range(lax.axis_size(axi...  4.03 us
    pallas_call x1, Pallas kernels, finish(): pl.pallas_call(lambda *refs: finish_kernel(replicas, *refs), in_specs=[WH...  3.35 us
    pallas_call x1, Pallas kernels, solve(): pl.pallas_call(solve_kernel, in_specs=[WHOLE] * len(halves), out_specs=[W...  3.06 us
  transfers between devices with their start and end apart: 6, of which 5 were waited for; matrix products, arithmetic and copies ran while one was open for 0% of the time, Pallas kernels for 9%

profile of v6, /device:TPU:32, one launch (start us, length us, event | category | flops | bytes accessed | tf_op | source)
XLA Modules:
  0.0 66.2 jit_solution(11005168146850400975)
XLA Ops:
  0.6 2.6 %merge_other.1 = (bf16[2048,512]{1,0:T(8,128)(2,1)S(1)}, bf16[16,32,128]{2,1,0:T(8,128)(2,1)S(1)}) custom-call(bf16[1,4096,512]{2,1,0:T(8,128)(2,1)} %refs_0_.3, bf16[1,4096,512]{2,1,0:T(8,128)(2,1)} %refs_1_.3, bf16[32,512]{1,0:T(8,128)(2,1)} %refs_2_.3), custom_call_target="tpu_custom_call" | custom-call | flops 67108864 | bytes 4194304 | tf_op jit(solution)/shard_map/merge_other/pallas_call | solution.py:62
  3.2 0.1 collective-permute-start
  3.3 2.5 %merge_own.1 = (bf16[2048,512]{1,0:T(8,128)(2,1)S(1)}, f32[16,32,128]{2,1,0:T(8,128)S(1)}) custom-call(bf16[1,4096,512]{2,1,0:T(8,128)(2,1)} %refs_0_.3, bf16[1,4096,512]{2,1,0:T(8,128)(2,1)} %refs_1_.3, bf16[32,512]{1,0:T(8,128)(2,1)} %refs_2_.3), custom_call_target="tpu_custom_call" | custom-call | flops 67108864 | bytes 4194304 | tf_op jit(solution)/shard_map/merge_own/pallas_call | solution.py:62
  5.8 0.0 collective-permute-done
  5.9 14.8 %all_to_all.15 = bf16[16,32,128]{2,1,0:T(8,128)(2,1)S(1)} all-to-all(bf16[16,32,128]{2,1,0:T(8,128)(2,1)S(1)} %add_convert_fusion), channel_id=1, replica_groups={{0,16,32,48,64,80,96,112,128,144,160,176,192,208,224,240},{8,24,40,56,7..., dimensions={0} | all-to-all | bytes 262144 | tf_op jit(solution)/shard_map/all_to_all | solution.py:194
  20.8 15.3 %all_to_all.16 = bf16[8,32,128]{2,1,0:T(8,128)(2,1)S(1)} all-to-all(bf16[8,32,128]{2,1,0:T(8,128)(2,1)S(1)} %broadcast_in_dim.17), channel_id=1, replica_groups=mesh['col'=32,'rep'=8] {'rep'}, dimensions={0} | all-to-all | bytes 131072 | tf_op jit(solution)/shard_map/all_to_all | solution.py:194
  36.1 11.1 %all_to_all.17.p_half.refs_0_ = bf16[16,32,128]{2,1,0:T(8,128)(2,1)S(1)} all-to-all(bf16[16,32,128]{2,1,0:T(8,128)(2,1)S(1)} %broadcast_in_dim.19), channel_id=1, replica_groups={{0,16,32,48,64,80,96,112,128,144,160,176,192,208,224,240},{8,24,40,56,7..., dimensions={0} | all-to-all | bytes 262144 | tf_op jit(solution)/shard_map/all_to_all | solution.py:194
  47.2 0.0 collective-permute-start.1
  47.2 0.4 raw_half.1.begun
  47.6 0.9 %collective-permute-done.1.p_half.refs_1_ = bf16[16,32,128]{2,1,0:T(8,128)(2,1)S(1)} collective-permute-done((bf16[16,32,128]{2,1,0:T(8,128)(2,1)S(1)}, bf16[16,32,128]{2,1,0:T(8,128)(2,1)S(1)}, u32[]{:S(2)}, u32[]{:S(2)}) %collective-permute-start.1) | collective-permute-done | bytes 131104 | tf_op jit(solution)/shard_map/ppermute | solution.py:203
  48.5 0.5 raw_rest.1
  49.0 0.5 collective-permute-start.4
  49.5 3.3 %collective-permute-start.3 = (bf16[32,512]{1,0:T(8,128)(2,1)S(1)}, bf16[32,512]{1,0:T(8,128)(2,1)S(1)}, u32[]{:S(2)}, u32[]{:S(2)}) collective-permute-start(bf16[32,512]{1,0:T(8,128)(2,1)S(1)} %raw_rest.1), channel_id=1, source_target_pairs={{0,2},{1,3},{2,0},{3,1},{4,6},{5,7},{6,4},{7,5},{8,10},{9,11},{10,... | collective-permute-start | bytes 98312 | tf_op jit(solution)/shard_map/ppermute | solution.py:203
  52.8 0.0 collective-permute-start.2
  52.8 0.2 collective-permute-done.4
  53.1 2.2 %collective-permute-done.3 = bf16[32,512]{1,0:T(8,128)(2,1)S(1)} collective-permute-done((bf16[32,512]{1,0:T(8,128)(2,1)S(1)}, bf16[32,512]{1,0:T(8,128)(2,1)S(1)}, u32[]{:S(2)}, u32[]{:S(2)}) %collective-permute-start.3) | collective-permute-done | bytes 32800 | tf_op jit(solution)/shard_map/ppermute | solution.py:203
  55.3 1.4 %collective-permute-done.2 = bf16[32,512]{1,0:T(8,128)(2,1)S(1)} collective-permute-done((bf16[32,512]{1,0:T(8,128)(2,1)S(1)}, bf16[32,512]{1,0:T(8,128)(2,1)S(1)}, u32[]{:S(2)}, u32[]{:S(2)}) %collective-permute-start.2) | collective-permute-done | bytes 32800 | tf_op jit(solution)/shard_map/ppermute | solution.py:203
  56.8 0.1 collective-permute-start.5
  56.9 3.1 %solve.1 = (f32[32,32]{1,0:T(8,128)S(1)}, bf16[4096,64]{1,0:T(8,128)(2,1)S(1)}) custom-call(bf16[16,32,128]{2,1,0:T(8,128)(2,1)S(1)} %all_to_all.17.p_half.refs_0_, bf16[16,32,128]{2,1,0:T(8,128)(2,1)S(1)} %collective-permute-done.1.p_half.refs_1_), custom_call_target="tpu_custom_call" | custom-call | flops 67108864 | bytes 4194304 | tf_op jit(solution)/shard_map/solve/pallas_call | solution.py:134
  59.9 2.9 %collective-permute-done.5.refs_1_ = bf16[32,512]{1,0:T(8,128)(2,1)S(1)} collective-permute-done((bf16[32,512]{1,0:T(8,128)(2,1)S(1)}, bf16[32,512]{1,0:T(8,128)(2,1)S(1)}, u32[]{:S(2)}, u32[]{:S(2)}) %collective-permute-start.5) | collective-permute-done | bytes 32800 | tf_op jit(solution)/shard_map/ppermute | solution.py:203
  62.9 3.4 %finish.1 = (bf16[1,4096,512]{2,1,0:T(8,128)(2,1)}, f32[32,512]{1,0:T(8,128)}) custom-call(bf16[32,512]{1,0:T(8,128)(2,1)S(1)} %add_convert_fusion.1.refs_0_, bf16[32,512]{1,0:T(8,128)(2,1)S(1)} %collective-permute-done.5.refs_1_, f32[32,32]{1,0:T(8,128)S(1)} %get-tuple-element.12.refs_2_, bf16[4096,64]{1,0:T(8,128)(2,1)S(1)} %get-tuple-element.13.refs_3_, ...), custom_call_target="tpu_custom_call" | custom-call | flops 268435456 | bytes 8388608 | tf_op jit(solution)/shard_map/finish/pallas_call | solution.py:174
  (6 shorter events, 0.1 us)
Async XLA Ops:
  3.2 2.6 %collective-permute-start = (bf16[16,32,128]{2,1,0:T(8,128)(2,1)S(1)}, bf16[16,32,128]{2,1,0:T(8,128)(2,1)S(1)}, u32[]{:S(2)}, u32[]{:S(2)}) collective-permute-start(bf16[16,32,128]{2,1,0:T(8,128)(2,1)S(1)} %get-tuple-element.9), channel_id=1, source_target_pairs={{0,8},{8,0},{16,24},{24,16},{32,40},{40,32},{48,56},{56,48},{64,72... | collective-permute-start | bytes 393224 | tf_op jit(solution)/shard_map/ppermute | solution.py:203
  47.2 1.3 %collective-permute-start.1 = (bf16[16,32,128]{2,1,0:T(8,128)(2,1)S(1)}, bf16[16,32,128]{2,1,0:T(8,128)(2,1)S(1)}, u32[]{:S(2)}, u32[]{:S(2)}) collective-permute-start(bf16[16,32,128]{2,1,0:T(8,128)(2,1)S(1)} %all_to_all.17.p_half.refs_0_), channel_id=1, source_target_pairs={{0,8},{8,0},{16,24},{24,16},{32,40},{40,32},{48,56},{56,48},{64,72... | collective-permute-start | bytes 393224 | tf_op jit(solution)/shard_map/ppermute | solution.py:203
  49.0 4.1 %collective-permute-start.4 = (bf16[32,512]{1,0:T(8,128)(2,1)S(1)}, bf16[32,512]{1,0:T(8,128)(2,1)S(1)}, u32[]{:S(2)}, u32[]{:S(2)}) collective-permute-start(bf16[32,512]{1,0:T(8,128)(2,1)S(1)} %raw_rest.1), channel_id=1, source_target_pairs={{0,3},{1,2},{2,1},{3,0},{4,7},{5,6},{6,5},{7,4},{8,11},{9,10},{10,... | collective-permute-start | bytes 98312 | tf_op jit(solution)/shard_map/ppermute | solution.py:203
  49.5 5.8 %collective-permute-start.3 = (bf16[32,512]{1,0:T(8,128)(2,1)S(1)}, bf16[32,512]{1,0:T(8,128)(2,1)S(1)}, u32[]{:S(2)}, u32[]{:S(2)}) collective-permute-start(bf16[32,512]{1,0:T(8,128)(2,1)S(1)} %raw_rest.1), channel_id=1, source_target_pairs={{0,2},{1,3},{2,0},{3,1},{4,6},{5,7},{6,4},{7,5},{8,10},{9,11},{10,... | collective-permute-start | bytes 98312 | tf_op jit(solution)/shard_map/ppermute | solution.py:203
  52.8 3.9 %collective-permute-start.2 = (bf16[32,512]{1,0:T(8,128)(2,1)S(1)}, bf16[32,512]{1,0:T(8,128)(2,1)S(1)}, u32[]{:S(2)}, u32[]{:S(2)}) collective-permute-start(bf16[32,512]{1,0:T(8,128)(2,1)S(1)} %raw_rest.1), channel_id=1, source_target_pairs={{0,1},{1,0},{2,3},{3,2},{4,5},{5,4},{6,7},{7,6},{8,9},{9,8},{10,11... | collective-permute-start | bytes 98312 | tf_op jit(solution)/shard_map/ppermute | solution.py:203
  56.8 6.1 %collective-permute-start.5 = (bf16[32,512]{1,0:T(8,128)(2,1)S(1)}, bf16[32,512]{1,0:T(8,128)(2,1)S(1)}, u32[]{:S(2)}, u32[]{:S(2)}) collective-permute-start(bf16[32,512]{1,0:T(8,128)(2,1)S(1)} %add_convert_fusion.1.refs_0_), channel_id=1, source_target_pairs={{0,6},{1,7},{2,4},{3,5},{4,2},{5,3},{6,0},{7,1},{8,14},{9,15},{10,... | collective-permute-start | bytes 98312 | tf_op jit(solution)/shard_map/ppermute | solution.py:203

commit v7 on v5

--- a/solution.py
+++ b/solution.py
@@ -7,6 +7,7 @@
 
 BF16, F32 = jnp.bfloat16, jnp.float32
 HIGHEST = lax.Precision.HIGHEST
+CORES = 2
 LANES = 128
 STEP = 512
 WHOLE = pl.BlockSpec(memory_space=pltpu.VMEM)
@@ -25,56 +26,86 @@
     return pltpu.with_memory_space_constraint(array, pltpu.HBM)
 
 
-def rows_of(chunk):
-    return pl.ds(chunk * STEP, STEP)
-
-
-def merge_kernel(gradient, error, warm, merged, part, gradient_in, error_in, warm_in, done):
-    chunks = merged.shape[0] // STEP
-    copies = [pltpu.make_async_copy(warm, warm_in, done.at[2 * chunks])]
-    for chunk in range(chunks):
-        here = rows_of(chunk)
-        copies.append(pltpu.make_async_copy(gradient.at[0, here, :], gradient_in.at[here, :], done.at[2 * chunk]))
-        copies.append(pltpu.make_async_copy(error.at[0, here, :], error_in.at[here, :], done.at[2 * chunk + 1]))
+def rows_of(chunk, first=0):
+    return pl.ds(pl.multiple_of(first + chunk * STEP, STEP), STEP)
+
+
+def core():
+    return lax.rem(lax.axis_index("col"), CORES)
+
+
+def merge_chunks(steps, gradient, error, warm, merged, columns_in, warm_in, done):
+    copies = [pltpu.make_async_copy(warm, warm_in, done.at[2 * len(steps)])]
+    for place, (chunk, first, _) in enumerate(steps):
+        there = rows_of(chunk, first)
+        copies.append(pltpu.make_async_copy(gradient.at[0, there, :], columns_in.at[2 * place], done.at[2 * place]))
+        copies.append(pltpu.make_async_copy(error.at[0, there, :], columns_in.at[2 * place + 1], done.at[2 * place + 1]))
     for copy in copies:
         copy.start()
     copies[0].wait()
-    for chunk in range(chunks):
-        here = rows_of(chunk)
-        copies[2 * chunk + 1].wait()
-        copies[2 * chunk + 2].wait()
-        value = (gradient_in[here, :].astype(F32) + error_in[here, :].astype(F32)).astype(BF16)
-        merged[here, :] = value
+    for place, (chunk, first, blocks) in enumerate(steps):
+        copies[2 * place + 1].wait()
+        copies[2 * place + 2].wait()
+        value = (columns_in[2 * place].astype(F32) + columns_in[2 * place + 1].astype(F32)).astype(BF16)
+        merged[rows_of(chunk, first), :] = value
         product = lax.dot_general(warm_in[...], value, (((1,), (1,)), ((), ())), preferred_element_type=F32)
         for block in range(STEP // LANES):
-            part[chunk * (STEP // LANES) + block] = product[:, block * LANES : (block + 1) * LANES].astype(BF16)
+            blocks[chunk * (STEP // LANES) + block] = product[:, block * LANES : (block + 1) * LANES].astype(blocks.dtype)
+
+
+def begin_kernel(early, gradient, error, warm, merged, part_own, part_other, *scratch):
+    half = merged.shape[0] // CORES
+    own, other = core() * half, (1 - core()) * half
+    steps = [(chunk, other, part_other) for chunk in range(half // STEP)]
+    steps += [(chunk, own, part_own) for chunk in range(early)]
+    merge_chunks(steps, gradient, error, warm, merged, *scratch)
+
+
+def end_kernel(early, gradient, error, warm, merged_in, part_in, merged, part_own, *scratch):
+    half = merged.shape[0] // CORES
+    steps = [(chunk, core() * half, part_own) for chunk in range(early, half // STEP)]
+    merge_chunks(steps, gradient, error, warm, merged, *scratch)
+
+
+def merge_call(kernel, early, chunks, arrays, begun, out_shape, name):
+    _, _, columns = arrays[0].shape
+    rank = arrays[2].shape[0]
+    rows = chunks * STEP
+    return pl.pallas_call(
+        lambda *refs: kernel(early, *refs),
+        in_specs=[ANYWHERE] * len(arrays) + [WHOLE] * len(begun),
+        out_specs=[WHOLE] * len(out_shape),
+        out_shape=out_shape,
+        input_output_aliases={len(arrays) + i: i for i in range(len(begun))},
+        scratch_shapes=[
+            pltpu.VMEM((2 * chunks, STEP, columns), BF16),
+            pltpu.VMEM((rank, columns), BF16),
+            pltpu.SemaphoreType.DMA((2 * chunks + 1,)),
+        ],
+        compiler_params=params(),
+        cost_estimate=pl.CostEstimate(flops=2 * rank * rows * columns, bytes_accessed=4 * rows * columns, transcendentals=0),
+        name=name,
+    )(*(in_hbm(x) for x in arrays), *(in_vmem(x) for x in begun))
 
 
 def merge(gradient, error, warm):
+    arrays = (gradient, error, warm)
     _, rows, columns = gradient.shape
-    rank = warm.shape[0]
-    return pl.pallas_call(
-        merge_kernel,
-        in_specs=[ANYWHERE] * 3,
-        out_specs=[WHOLE, WHOLE],
-        out_shape=[
-            pltpu.VMEM((rows, columns), BF16),
-            pltpu.VMEM((rows // LANES, rank, LANES), BF16),
-        ],
-        scratch_shapes=[
-            pltpu.VMEM((rows, columns), BF16),
-            pltpu.VMEM((rows, columns), BF16),
-            pltpu.VMEM((rank, columns), BF16),
-            pltpu.SemaphoreType.DMA((2 * (rows // STEP) + 1,)),
-        ],
-        compiler_params=params(),
-        cost_estimate=pl.CostEstimate(flops=2 * rank * rows * columns, bytes_accessed=4 * rows * columns, transcendentals=0),
-        name="merge",
-    )(in_hbm(gradient), in_hbm(error), in_hbm(warm))
-
-
-def side_by_side(blocks):
-    return jnp.concatenate([blocks[i] for i in range(blocks.shape[0])], axis=1)
+    blocks = (rows // CORES // LANES, warm.shape[0], LANES)
+    chunks = rows // STEP
+    late = chunks // 4
+    shapes = [pltpu.VMEM((rows, columns), BF16), pltpu.VMEM(blocks, F32), pltpu.VMEM(blocks, BF16)]
+    early = chunks // CORES - late
+    *begun, part_other = merge_call(begin_kernel, early, chunks - late, arrays, (), shapes, "merge_begin")
+    part_other = swap(part_other, "col", 1)
+    merged, part = merge_call(end_kernel, early, late, arrays, begun, shapes[:2], "merge_end")
+    return merged, (part + part_other.astype(F32)).astype(BF16)
+
+
+def side_by_side(p_sum):
+    blocks = p_sum.shape[0]
+    chips = blocks // CORES
+    return jnp.concatenate([p_sum[i % chips * CORES + i // chips] for i in range(blocks)], axis=1)
 
 
 def raw_kernel(p_sum, merged, raw):
@@ -95,17 +126,34 @@
     )(in_vmem(p_sum), in_vmem(merged))
 
 
-def solve_kernel(p_sum, inverse, turned):
+def turn_kernel(p_sum, gram, turned):
     blocks, rank, lanes = p_sum.shape
     wide = side_by_side(p_sum)
-    gram = lax.dot_general(wide, wide, (((1,), (1,)), ((), ())), preferred_element_type=F32)
+    gram[...] = lax.dot_general(wide, wide, (((1,), (1,)), ((), ())), preferred_element_type=F32)
     for block in range(blocks):
-        tall = p_sum[block].astype(F32).T.astype(BF16)
+        tall = wide[:, block * lanes : (block + 1) * lanes].astype(F32).T.astype(BF16)
         turned[pl.ds(block * lanes, lanes), :] = jnp.concatenate([tall, tall], axis=1)
+
+
+def turn(p_sum):
+    blocks, rank, lanes = p_sum.shape
+    return pl.pallas_call(
+        turn_kernel,
+        in_specs=[WHOLE],
+        out_specs=[WHOLE, WHOLE],
+        out_shape=[pltpu.VMEM((rank, rank), F32), pltpu.VMEM((blocks * lanes, 2 * rank), BF16)],
+        compiler_params=params(),
+        cost_estimate=pl.CostEstimate(flops=8 * rank * rank * blocks * lanes, bytes_accessed=2 << 20, transcendentals=0),
+        name="turn",
+    )(in_vmem(p_sum))
+
+
+def solve_kernel(gram, inverse):
+    rank = gram.shape[0]
     row = lax.broadcasted_iota(jnp.int32, (rank, rank), 0)
     col = lax.broadcasted_iota(jnp.int32, (rank, rank), 1)
     one = (row == col).astype(F32)
-    table = jnp.concatenate([gram, one], axis=1)
+    table = jnp.concatenate([gram[...], one], axis=1)
     below = lax.broadcasted_iota(jnp.int32, (rank, 1), 0)
     for k in range(rank):
         pivot = table[k : k + 1, :]
@@ -115,17 +163,16 @@
     inverse[...] = table[:, rank:] * lax.rsqrt(diagonal)
 
 
-def solve(p_sum):
-    blocks, rank, lanes = p_sum.shape
+def solve(gram):
     return pl.pallas_call(
         solve_kernel,
         in_specs=[WHOLE],
-        out_specs=[WHOLE, WHOLE],
-        out_shape=[pltpu.VMEM((rank, rank), F32), pltpu.VMEM((blocks * lanes, 2 * rank), BF16)],
-        compiler_params=params(),
-        cost_estimate=pl.CostEstimate(flops=16 * rank * rank * blocks * lanes, bytes_accessed=4 << 20, transcendentals=0),
+        out_specs=WHOLE,
+        out_shape=pltpu.VMEM(gram.shape, F32),
+        compiler_params=params(),
+        cost_estimate=pl.CostEstimate(flops=8 << 20, bytes_accessed=4 << 20, transcendentals=0),
         name="solve",
-    )(in_vmem(p_sum))
+    )(in_vmem(gram))
 
 
 def finish_kernel(replicas, mine, theirs, inverse, turned, merged, new_error, q_factor, halves, result, done):
@@ -171,12 +218,16 @@
     )(in_vmem(mine), in_vmem(theirs), in_vmem(inverse), in_vmem(turned), in_vmem(merged))
 
 
-def exchange(blocks, axis):
-    return lax.all_to_all(blocks, axis, 0, 0, tiled=True)
+def exchange(blocks, axis, groups=None):
+    return lax.all_to_all(blocks, axis, 0, 0, axis_index_groups=groups, tiled=True)
 
 
 def share(block, axis):
     return exchange(jnp.broadcast_to(block[None], (lax.axis_size(axis),) + block.shape), axis)
+
+
+def swap(block, axis, mask):
+    return lax.ppermute(block, axis, [(i, i ^ mask) for i in range(lax.axis_size(axis))])
 
 
 def total(blocks):
@@ -186,19 +237,19 @@
     return terms[0]
 
 
-def swap(block, axis, mask):
-    return lax.ppermute(block, axis, [(i, i ^ mask) for i in range(lax.axis_size(axis))])
-
-
 def per_device(gradient, error, warm_start):
     replicas = lax.axis_size("rep")
+    chips = [list(range(c, lax.axis_size("col"), CORES)) for c in range(CORES)]
     merged, part = merge(gradient, error, warm_start)
-    own = total(exchange(part, "col"))
+    own = total(exchange(part, "col", chips))
     own = total(share(own.astype(BF16), "rep"))
     p_sum = share(own.astype(BF16), "col")
     raw = raw_factor(p_sum, merged)
-    inverse, turned = solve(p_sum)
-    raw = total([raw] + [swap(raw, "rep", mask) for mask in (1, 2, 3)]).astype(BF16)
+    gram, turned = turn(p_sum)
+    near = [swap(raw, "rep", mask) for mask in (1, 2, 3)]
+    raw, gram, *near = lax.optimization_barrier((raw, gram, *near))
+    raw = total([raw, *near]).astype(BF16)
+    inverse = solve(gram)
     return tuple(finish(raw, swap(raw, "rep", 6), inverse, turned, merged, replicas))
 
 

time: 66.6 us -> 66.8 us (level)
  blocking collectives: 46.5 us -> 42 us
  starting transfers between devices: 4.47 us -> 7.85 us
  Pallas kernels: 11.1 us -> 12.6 us
    all_to_all x3, blocking collectives: 46.5 us -> 42 us  [exchange(): lax.all_to_all(blocks, axis, 0, 0, axis_index_groups=groups, tiled=True)]
    ppermute x4 -> x5, starting transfers between devices: 4.47 us -> 7.85 us  [swap(): lax.ppermute(block, axis, [(i, i ^ mask) for i in range(lax.axis_size(axi...]
    pallas_call x2 -> x4, Pallas kernels: 6.97 us -> 8.43 us  [the longest x2 5.03 us: merge_call(): pl.pallas_call(lambda *refs: kernel(early, *refs), in_specs=[ANYWHERE] *...]
    ppermute x4 -> x5, waiting for transfers between devices: 2.82 us -> 2.55 us  [swap(): lax.ppermute(block, axis, [(i, i ^ mask) for i in range(lax.axis_size(axi...]
  transfers between devices with their start and end apart: 4 -> 5, of which waited for: 3 -> 3; matrix products, arithmetic and copies ran while one was open for 0% -> 0% of each run, Pallas kernels for 5% -> 8%
where the time goes in v7:
time: 66.8 us; the launch traced here: 65.8 us
  blocking collectives  42 us (63%)
  Pallas kernels  12.6 us (19%)
  starting transfers between devices  7.85 us (12%)
  waiting for transfers between devices  2.55 us (4%)
  between operations  0.69 us (1%)
    all_to_all x3, blocking collectives, exchange(): lax.all_to_all(blocks, axis, 0, 0, axis_index_groups=groups, tiled=True)  42 us
    ppermute x5, starting transfers between devices, swap(): lax.ppermute(block, axis, [(i, i ^ mask) for i in range(lax.axis_size(axi...  7.85 us
    pallas_call x2, Pallas kernels, merge_call(): pl.pallas_call(lambda *refs: kernel(early, *refs), in_specs=[ANYWHERE] *...  5.03 us
    pallas_call x1, Pallas kernels, finish(): pl.pallas_call(lambda *refs: finish_kernel(replicas, *refs), in_specs=[WH...  3.35 us
    pallas_call x1, Pallas kernels, solve(): pl.pallas_call(solve_kernel, in_specs=[WHOLE], out_specs=WHOLE, out_shape...  2.76 us
    ppermute x5, waiting for transfers between devices, swap(): lax.ppermute(block, axis, [(i, i ^ mask) for i in range(lax.axis_size(axi...  2.55 us
  transfers between devices with their start and end apart: 5, of which 3 were waited for; matrix products, arithmetic and copies ran while one was open for 0% of the time, Pallas kernels for 8%

profile of v7, /device:TPU:1, one launch (start us, length us, event | category | flops | bytes accessed | tf_op | source)
XLA Modules:
  0.0 65.8 jit_solution(10485514946682546203)
XLA Ops:
  0.6 3.2 %merge_begin.1 = (bf16[4096,512]{1,0:T(8,128)(2,1)S(1)}, f32[16,32,128]{2,1,0:T(8,128)S(1)}, bf16[16,32,128]{2,1,0:T(8,128)(2,1)S(1)}) custom-call(bf16[1,4096,512]{2,1,0:T(8,128)(2,1)} %refs_0_.3, bf16[1,4096,512]{2,1,0:T(8,128)(2,1)} %refs_1_.3, bf16[32,512]{1,0:T(8,128)(2,1)} %refs_2_.3), custom_call_target="tpu_custom_call" | custom-call | flops 100663296 | bytes 6291456 | tf_op jit(solution)/shard_map/merge_begin/pallas_call | solution.py:74
  3.8 3.4 %collective-permute-start = (bf16[16,32,128]{2,1,0:T(8,128)(2,1)S(1)}, bf16[16,32,128]{2,1,0:T(8,128)(2,1)S(1)}, u32[]{:S(2)}, u32[]{:S(2)}) collective-permute-start(bf16[16,32,128]{2,1,0:T(8,128)(2,1)S(1)} %get-tuple-element.17), channel_id=1, source_target_pairs={{0,8},{8,0},{16,24},{24,16},{32,40},{40,32},{48,56},{56,48},{64,72... | collective-permute-start | bytes 393224 | tf_op jit(solution)/shard_map/ppermute | solution.py:230
  7.2 1.8 %merge_end.1 = (bf16[4096,512]{1,0:T(8,128)(2,1)S(1)}, f32[16,32,128]{2,1,0:T(8,128)S(1)}) custom-call(bf16[1,4096,512]{2,1,0:T(8,128)(2,1)} %refs_0_.3, bf16[1,4096,512]{2,1,0:T(8,128)(2,1)} %refs_1_.3, bf16[32,512]{1,0:T(8,128)(2,1)} %refs_2_.3, bf16[4096,512]{1,0:T(8,128)(2,1)S(1)} %get-tuple-element.14.refs_3_, ...), custom_call_target="tpu_custom_call", output_to_operand_aliasing={{0}: (3, {}), {1}: (4, {})} | custom-call | flops 33554432 | bytes 2097152 | tf_op jit(solution)/shard_map/merge_end/pallas_call | solution.py:74
  9.0 0.0 collective-permute-done
  9.1 11.6 %all_to_all.15 = bf16[16,32,128]{2,1,0:T(8,128)(2,1)S(1)} all-to-all(bf16[16,32,128]{2,1,0:T(8,128)(2,1)S(1)} %add_convert_fusion), channel_id=1, replica_groups={{0,16,32,48,64,80,96,112,128,144,160,176,192,208,224,240},{8,24,40,56,7..., dimensions={0} | all-to-all | bytes 262144 | tf_op jit(solution)/shard_map/all_to_all | solution.py:222
  20.7 15.3 %all_to_all.16 = bf16[8,32,128]{2,1,0:T(8,128)(2,1)S(1)} all-to-all(bf16[8,32,128]{2,1,0:T(8,128)(2,1)S(1)} %broadcast_in_dim.17), channel_id=1, replica_groups=mesh['col'=32,'rep'=8] {'rep'}, dimensions={0} | all-to-all | bytes 131072 | tf_op jit(solution)/shard_map/all_to_all | solution.py:222
  36.0 15.2 %all_to_all.17.p_sum = bf16[32,32,128]{2,1,0:T(8,128)(2,1)S(1)} all-to-all(bf16[32,32,128]{2,1,0:T(8,128)(2,1)S(1)} %broadcast_in_dim.19), channel_id=1, replica_groups=mesh['col'=32,'rep'=8] {'col'}, dimensions={0} | all-to-all | bytes 524288 | tf_op jit(solution)/shard_map/all_to_all | solution.py:222
  51.2 0.8 %raw_factor.1 = bf16[32,512]{1,0:T(8,128)(2,1)S(1)} custom-call(bf16[32,32,128]{2,1,0:T(8,128)(2,1)S(1)} %all_to_all.17.p_sum, bf16[4096,512]{1,0:T(8,128)(2,1)S(1)} %get-tuple-element.18.merged.refs_4_), custom_call_target="tpu_custom_call" | custom-call | flops 134217728 | bytes 4194304 | tf_op jit(solution)/shard_map/raw_factor/pallas_call | solution.py:118
  52.0 0.2 collective-permute-start.3
  52.2 1.3 %collective-permute-start.2 = (bf16[32,512]{1,0:T(8,128)(2,1)S(1)}, bf16[32,512]{1,0:T(8,128)(2,1)S(1)}, u32[]{:S(2)}, u32[]{:S(2)}) collective-permute-start(bf16[32,512]{1,0:T(8,128)(2,1)S(1)} %raw_factor.1), channel_id=1, source_target_pairs={{0,2},{1,3},{2,0},{3,1},{4,6},{5,7},{6,4},{7,5},{8,10},{9,11},{10,... | collective-permute-start | bytes 98312 | tf_op jit(solution)/shard_map/ppermute | solution.py:230
  53.5 2.1 %collective-permute-start.1 = (bf16[32,512]{1,0:T(8,128)(2,1)S(1)}, bf16[32,512]{1,0:T(8,128)(2,1)S(1)}, u32[]{:S(2)}, u32[]{:S(2)}) collective-permute-start(bf16[32,512]{1,0:T(8,128)(2,1)S(1)} %raw_factor.1), channel_id=1, source_target_pairs={{0,1},{1,0},{2,3},{3,2},{4,5},{5,4},{6,7},{7,6},{8,9},{9,8},{10,11... | collective-permute-start | bytes 98312 | tf_op jit(solution)/shard_map/ppermute | solution.py:230
  55.6 0.6 turn.1
  56.2 0.4 collective-permute-done.3
  56.6 0.0 collective-permute-done.2
  56.6 0.8 %collective-permute-done.1 = bf16[32,512]{1,0:T(8,128)(2,1)S(1)} collective-permute-done((bf16[32,512]{1,0:T(8,128)(2,1)S(1)}, bf16[32,512]{1,0:T(8,128)(2,1)S(1)}, u32[]{:S(2)}, u32[]{:S(2)}) %collective-permute-start.1) | collective-permute-done | bytes 32800 | tf_op jit(solution)/shard_map/ppermute | solution.py:230
  57.4 0.9 %collective-permute-start.4 = (bf16[32,512]{1,0:T(8,128)(2,1)S(1)}, bf16[32,512]{1,0:T(8,128)(2,1)S(1)}, u32[]{:S(2)}, u32[]{:S(2)}) collective-permute-start(bf16[32,512]{1,0:T(8,128)(2,1)S(1)} %add_convert_fusion.1.refs_0_), channel_id=1, source_target_pairs={{0,6},{1,7},{2,4},{3,5},{4,2},{5,3},{6,0},{7,1},{8,14},{9,15},{10,... | collective-permute-start | bytes 98312 | tf_op jit(solution)/shard_map/ppermute | solution.py:230
  58.4 2.8 %solve.1.refs_2_ = f32[32,32]{1,0:T(8,128)S(1)} custom-call(f32[32,32]{1,0:T(8,128)S(1)} %get-tuple-element.24.gram), custom_call_target="tpu_custom_call" | custom-call | flops 8388608 | bytes 4194304 | tf_op jit(solution)/shard_map/solve/pallas_call | solution.py:167
  61.1 1.4 %collective-permute-done.4.refs_1_ = bf16[32,512]{1,0:T(8,128)(2,1)S(1)} collective-permute-done((bf16[32,512]{1,0:T(8,128)(2,1)S(1)}, bf16[32,512]{1,0:T(8,128)(2,1)S(1)}, u32[]{:S(2)}, u32[]{:S(2)}) %collective-permute-start.4) | collective-permute-done | bytes 32800 | tf_op jit(solution)/shard_map/ppermute | solution.py:230
  62.5 3.4 %finish.1 = (bf16[1,4096,512]{2,1,0:T(8,128)(2,1)}, f32[32,512]{1,0:T(8,128)}) custom-call(bf16[32,512]{1,0:T(8,128)(2,1)S(1)} %add_convert_fusion.1.refs_0_, bf16[32,512]{1,0:T(8,128)(2,1)S(1)} %collective-permute-done.4.refs_1_, f32[32,32]{1,0:T(8,128)S(1)} %solve.1.refs_2_, bf16[4096,64]{1,0:T(8,128)(2,1)S(1)} %get-tuple-element.25.refs_3_, ...), custom_call_target="tpu_custom_call" | custom-call | flops 268435456 | bytes 8388608 | tf_op jit(solution)/shard_map/finish/pallas_call | solution.py:202
  (6 shorter events, 0.1 us)
Async XLA Ops:
  3.8 5.2 %collective-permute-start = (bf16[16,32,128]{2,1,0:T(8,128)(2,1)S(1)}, bf16[16,32,128]{2,1,0:T(8,128)(2,1)S(1)}, u32[]{:S(2)}, u32[]{:S(2)}) collective-permute-start(bf16[16,32,128]{2,1,0:T(8,128)(2,1)S(1)} %get-tuple-element.17), channel_id=1, source_target_pairs={{0,8},{8,0},{16,24},{24,16},{32,40},{40,32},{48,56},{56,48},{64,72... | collective-permute-start | bytes 393224 | tf_op jit(solution)/shard_map/ppermute | solution.py:230
  52.0 4.6 %collective-permute-start.3 = (bf16[32,512]{1,0:T(8,128)(2,1)S(1)}, bf16[32,512]{1,0:T(8,128)(2,1)S(1)}, u32[]{:S(2)}, u32[]{:S(2)}) collective-permute-start(bf16[32,512]{1,0:T(8,128)(2,1)S(1)} %raw_factor.1), channel_id=1, source_target_pairs={{0,3},{1,2},{2,1},{3,0},{4,7},{5,6},{6,5},{7,4},{8,11},{9,10},{10,... | collective-permute-start | bytes 98312 | tf_op jit(solution)/shard_map/ppermute | solution.py:230
  52.2 4.5 %collective-permute-start.2 = (bf16[32,512]{1,0:T(8,128)(2,1)S(1)}, bf16[32,512]{1,0:T(8,128)(2,1)S(1)}, u32[]{:S(2)}, u32[]{:S(2)}) collective-permute-start(bf16[32,512]{1,0:T(8,128)(2,1)S(1)} %raw_factor.1), channel_id=1, source_target_pairs={{0,2},{1,3},{2,0},{3,1},{4,6},{5,7},{6,4},{7,5},{8,10},{9,11},{10,... | collective-permute-start | bytes 98312 | tf_op jit(solution)/shard_map/ppermute | solution.py:230
  53.5 3.9 %collective-permute-start.1 = (bf16[32,512]{1,0:T(8,128)(2,1)S(1)}, bf16[32,512]{1,0:T(8,128)(2,1)S(1)}, u32[]{:S(2)}, u32[]{:S(2)}) collective-permute-start(bf16[32,512]{1,0:T(8,128)(2,1)S(1)} %raw_factor.1), channel_id=1, source_target_pairs={{0,1},{1,0},{2,3},{3,2},{4,5},{5,4},{6,7},{7,6},{8,9},{9,8},{10,11... | collective-permute-start | bytes 98312 | tf_op jit(solution)/shard_map/ppermute | solution.py:230
  57.4 5.1 %collective-permute-start.4 = (bf16[32,512]{1,0:T(8,128)(2,1)S(1)}, bf16[32,512]{1,0:T(8,128)(2,1)S(1)}, u32[]{:S(2)}, u32[]{:S(2)}) collective-permute-start(bf16[32,512]{1,0:T(8,128)(2,1)S(1)} %add_convert_fusion.1.refs_0_), channel_id=1, source_target_pairs={{0,6},{1,7},{2,4},{3,5},{4,2},{5,3},{6,0},{7,1},{8,14},{9,15},{10,... | collective-permute-start | bytes 98312 | tf_op jit(solution)/shard_map/ppermute | solution.py:230

commit v8 on v5

--- a/solution.py
+++ b/solution.py
@@ -7,6 +7,7 @@
 
 BF16, F32 = jnp.bfloat16, jnp.float32
 HIGHEST = lax.Precision.HIGHEST
+CORES = 2
 LANES = 128
 STEP = 512
 WHOLE = pl.BlockSpec(memory_space=pltpu.VMEM)
@@ -14,7 +15,7 @@
 
 
 def params():
-    return pltpu.CompilerParams(vmem_limit_bytes=40 << 20)
+    return pltpu.CompilerParams(vmem_limit_bytes=32 << 20)
 
 
 def in_vmem(array):
@@ -77,22 +78,34 @@
     return jnp.concatenate([blocks[i] for i in range(blocks.shape[0])], axis=1)
 
 
-def raw_kernel(p_sum, merged, raw):
-    raw[...] = jnp.dot(side_by_side(p_sum), merged[...], preferred_element_type=F32).astype(BF16)
-
-
-def raw_factor(p_sum, merged):
-    rows, columns = merged.shape
+def leads():
+    return lax.rem(lax.axis_index("col"), CORES) == 1
+
+
+def raw_kernel(p_sum, own, other, raw):
+    @pl.when(leads())
+    def _():
+        wide = side_by_side(p_sum)
+        for place, merged in enumerate((own, other)):
+            raw[place] = jnp.dot(wide, merged[...], preferred_element_type=F32).astype(BF16)
+
+    @pl.when(jnp.logical_not(leads()))
+    def _():
+        raw[...] = jnp.zeros_like(raw)
+
+
+def raw_factors(p_sum, own, other):
+    rows, columns = own.shape
     rank = p_sum.shape[1]
     return pl.pallas_call(
         raw_kernel,
-        in_specs=[WHOLE, WHOLE],
+        in_specs=[WHOLE] * 3,
         out_specs=WHOLE,
-        out_shape=pltpu.VMEM((rank, columns), BF16),
-        compiler_params=params(),
-        cost_estimate=pl.CostEstimate(flops=2 * rank * rows * columns, bytes_accessed=2 * rows * columns, transcendentals=0),
-        name="raw_factor",
-    )(in_vmem(p_sum), in_vmem(merged))
+        out_shape=pltpu.VMEM((CORES, rank, columns), BF16),
+        compiler_params=params(),
+        cost_estimate=pl.CostEstimate(flops=4 * rank * rows * columns, bytes_accessed=4 * rows * columns, transcendentals=0),
+        name="raw_factors",
+    )(in_vmem(p_sum), in_vmem(own), in_vmem(other))
 
 
 def solve_kernel(p_sum, inverse, turned):
@@ -128,9 +141,8 @@
     )(in_vmem(p_sum))
 
 
-def finish_kernel(replicas, mine, theirs, inverse, turned, merged, new_error, q_factor, halves, result, done):
-    raw = mine[...].astype(F32) + theirs[...].astype(F32)
-    factor = jnp.dot(inverse[...], raw, precision=HIGHEST, preferred_element_type=F32) * (1.0 / replicas)
+def finish_rows(replicas, raw, inverse, turned, merged, new_error, q_factor, halves, result, done):
+    factor = jnp.dot(inverse[...], raw[...], precision=HIGHEST, preferred_element_type=F32) * (1.0 / replicas)
     q_factor[...] = factor
     rounded = factor.astype(BF16).astype(F32)
     solved = lax.dot_general(
@@ -149,17 +161,39 @@
         copy.wait()
 
 
-def finish(mine, theirs, inverse, turned, merged, replicas):
+def first_kernel(replicas, raw, inverse, turned, merged, new_error, q_factor, *scratch):
+    @pl.when(leads())
+    def _():
+        finish_rows(replicas, raw, inverse, turned, merged, new_error, q_factor, *scratch)
+
+    @pl.when(jnp.logical_not(leads()))
+    def _():
+        q_factor[...] = jnp.zeros_like(q_factor)
+
+
+def second_kernel(replicas, raw, inverse, turned, merged, _, q_begun, new_error, q_factor, *scratch):
+    @pl.when(leads())
+    def _():
+        q_factor[...] = q_begun[...]
+
+    @pl.when(jnp.logical_not(leads()))
+    def _():
+        finish_rows(replicas, raw, inverse, turned, merged, new_error, q_factor, *scratch)
+
+
+def finish(raw, inverse, turned, merged, replicas, *begun):
     rows, columns = merged.shape
     rank = inverse.shape[0]
-    return pl.pallas_call(
-        lambda *refs: finish_kernel(replicas, *refs),
-        in_specs=[WHOLE] * 5,
+    kernel = second_kernel if begun else first_kernel
+    return pl.pallas_call(
+        lambda *refs: kernel(replicas, *refs),
+        in_specs=[WHOLE] * 4 + [ANYWHERE, WHOLE][: len(begun)],
         out_specs=[ANYWHERE, WHOLE],
         out_shape=[
             pltpu.HBM((1, rows, columns), BF16),
             jax.ShapeDtypeStruct((rank, columns), F32),
         ],
+        input_output_aliases={4: 0} if begun else {},
         scratch_shapes=[
             pltpu.VMEM((2 * rank, columns), BF16),
             pltpu.VMEM((rows, columns), BF16),
@@ -167,16 +201,31 @@
         ],
         compiler_params=params(),
         cost_estimate=pl.CostEstimate(flops=4 * rank * rows * columns, bytes_accessed=4 * rows * columns, transcendentals=0),
-        name="finish",
-    )(in_vmem(mine), in_vmem(theirs), in_vmem(inverse), in_vmem(turned), in_vmem(merged))
-
-
-def exchange(blocks, axis):
-    return lax.all_to_all(blocks, axis, 0, 0, tiled=True)
-
-
-def share(block, axis):
-    return exchange(jnp.broadcast_to(block[None], (lax.axis_size(axis),) + block.shape), axis)
+        name="finish_other" if begun else "finish_leading",
+    )(*(in_vmem(x) for x in (raw, inverse, turned, merged)), *begun)
+
+
+def exchange(blocks, axis, groups=None):
+    return lax.all_to_all(blocks, axis, 0, 0, axis_index_groups=groups, tiled=True)
+
+
+def share(block, axis, groups=None):
+    count = len(groups[0]) if groups else lax.axis_size(axis)
+    return exchange(jnp.broadcast_to(block[None], (count,) + block.shape), axis, groups)
+
+
+def swap_cores(block):
+    return lax.ppermute(block, "col", [(i, i ^ 1) for i in range(lax.axis_size("col"))])
+
+
+def swap_chips(block, mask, idle):
+    columns, replicas = lax.axis_size("col"), lax.axis_size("rep")
+    pairs = []
+    for c in range(columns):
+        for r in range(replicas):
+            partner = (c, r ^ mask) if c % CORES else (c ^ idle[0], r ^ idle[1])
+            pairs.append((c * replicas + r, partner[0] * replicas + partner[1]))
+    return lax.ppermute(block, ("col", "rep"), pairs)
 
 
 def total(blocks):
@@ -186,20 +235,30 @@
     return terms[0]
 
 
-def swap(block, axis, mask):
-    return lax.ppermute(block, axis, [(i, i ^ mask) for i in range(lax.axis_size(axis))])
+def left_factor(part):
+    chips = [list(range(c, lax.axis_size("col"), CORES)) for c in range(CORES)]
+    count = len(chips[0])
+    blocks = exchange(part, "col", chips)
+    own = total(blocks.reshape((count, -1) + blocks.shape[1:])).astype(BF16)
+    own = total(share(own, "rep")).astype(BF16)
+    return share(own, "col", chips).reshape(part.shape)
 
 
 def per_device(gradient, error, warm_start):
     replicas = lax.axis_size("rep")
     merged, part = merge(gradient, error, warm_start)
-    own = total(exchange(part, "col"))
-    own = total(share(own.astype(BF16), "rep"))
-    p_sum = share(own.astype(BF16), "col")
-    raw = raw_factor(p_sum, merged)
+    handed, merged = lax.optimization_barrier((swap_cores(part), merged))
+    part = total([part, handed]).astype(BF16)
+    other = swap_cores(merged)
+    p_sum = left_factor(part)
+    raw = raw_factors(p_sum, merged, other)
     inverse, turned = solve(p_sum)
-    raw = total([raw] + [swap(raw, "rep", mask) for mask in (1, 2, 3)]).astype(BF16)
-    return tuple(finish(raw, swap(raw, "rep", 6), inverse, turned, merged, replicas))
+    near = [swap_chips(raw, 1, (0, 1)), swap_chips(raw, 2, (8, 0)), swap_chips(raw, 3, (2, 0))]
+    raw, inverse, *near = lax.optimization_barrier((raw, inverse, *near))
+    raw = total([raw, *near]).astype(BF16)
+    raw = total([raw, swap_chips(raw, 6, (0, 1))])
+    begun = finish(raw[0], inverse, turned, merged, replicas)
+    return tuple(finish(swap_cores(raw[1]), inverse, turned, merged, replicas, *begun))
 
 
 def solution(mesh):

time: 66.6 us -> 66.6 us (level)
  blocking collectives: 46.5 us -> 39.4 us
  waiting for transfers between devices: 2.82 us -> 6.39 us
  starting transfers between devices: 4.47 us -> 7.45 us
  Pallas kernels: 11.1 us -> 11.9 us
    all_to_all x3, blocking collectives: 46.5 us -> 39.4 us  [exchange(): lax.all_to_all(blocks, axis, 0, 0, axis_index_groups=groups, tiled=True)]
    ppermute x4 -> x7, waiting for transfers between devices: 2.82 us -> 6.39 us  [the longest x4 5.22 us: swap_chips(): return lax.ppermute(block, ('col', 'rep'), pairs)]
    ppermute x4 -> x7, starting transfers between devices: 4.47 us -> 7.45 us  [the longest x3 3.79 us: swap_cores(): lax.ppermute(block, 'col', [(i, i ^ 1) for i in range(lax.axis_size('col'...]
    pallas_call x2 -> x3, Pallas kernels: 4.15 us -> 4.97 us  [the longest x2 3.45 us: finish(): pl.pallas_call(lambda *refs: kernel(replicas, *refs), in_specs=[WHOLE] *...]
  transfers between devices with their start and end apart: 4 -> 7, of which waited for: 3 -> 2; matrix products, arithmetic and copies ran while one was open for 0% -> 0% of each run, Pallas kernels for 5% -> 9%
where the time goes in v8:
time: 66.6 us; the launch traced here: 66.2 us
  blocking collectives  39.4 us (59%)
  Pallas kernels  11.9 us (18%)
  starting transfers between devices  7.45 us (11%)
  waiting for transfers between devices  6.39 us (10%)
  between operations  0.73 us (1%)
    all_to_all x3, blocking collectives, exchange(): lax.all_to_all(blocks, axis, 0, 0, axis_index_groups=groups, tiled=True)  39.4 us
    ppermute x4, waiting for transfers between devices, swap_chips(): return lax.ppermute(block, ('col', 'rep'), pairs)  5.22 us
    pallas_call x1, Pallas kernels, merge(): pl.pallas_call(merge_kernel, in_specs=[ANYWHERE] * 3, out_specs=[WHOLE, W...  3.81 us
    ppermute x3, starting transfers between devices, swap_cores(): lax.ppermute(block, 'col', [(i, i ^ 1) for i in range(lax.axis_size('col'...  3.79 us
    ppermute x4, starting transfers between devices, swap_chips(): return lax.ppermute(block, ('col', 'rep'), pairs)  3.66 us
    pallas_call x2, Pallas kernels, finish(): pl.pallas_call(lambda *refs: kernel(replicas, *refs), in_specs=[WHOLE] *...  3.45 us
    pallas_call x1, Pallas kernels, solve(): pl.pallas_call(solve_kernel, in_specs=[WHOLE], out_specs=[WHOLE, WHOLE],...  3.16 us
    pallas_call x1, Pallas kernels, raw_factors(): pl.pallas_call(raw_kernel, in_specs=[WHOLE] * 3, out_specs=WHOLE, out_sha...  1.52 us
  transfers between devices with their start and end apart: 7, of which 2 were waited for; matrix products, arithmetic and copies ran while one was open for 0% of the time, Pallas kernels for 9%

profile of v8, /device:TPU:1, one launch (start us, length us, event | category | flops | bytes accessed | tf_op | source)
XLA Modules:
  0.0 66.2 jit_solution(745951094153145293)
XLA Ops:
  0.6 3.8 %merge.1 = (bf16[4096,512]{1,0:T(8,128)(2,1)S(1)}, bf16[32,32,128]{2,1,0:T(8,128)(2,1)S(1)}) custom-call(bf16[1,4096,512]{2,1,0:T(8,128)(2,1)} %gradient.1, bf16[1,4096,512]{2,1,0:T(8,128)(2,1)} %error.1, bf16[32,512]{1,0:T(8,128)(2,1)} %warm.1), custom_call_target="tpu_custom_call" | custom-call | flops 134217728 | bytes 8388608 | tf_op jit(solution)/shard_map/merge/pallas_call | solution.py:57
  4.4 3.3 %collective-permute-start = (bf16[32,32,128]{2,1,0:T(8,128)(2,1)S(1)}, bf16[32,32,128]{2,1,0:T(8,128)(2,1)S(1)}, u32[]{:S(2)}, u32[]{:S(2)}) collective-permute-start(bf16[32,32,128]{2,1,0:T(8,128)(2,1)S(1)} %get-tuple-element.15), channel_id=1, source_target_pairs={{0,8},{8,0},{16,24},{24,16},{32,40},{40,32},{48,56},{56,48},{64,72... | collective-permute-start | bytes 786440 | tf_op jit(solution)/shard_map/ppermute | solution.py:218
  7.8 1.2 %collective-permute-done = bf16[32,32,128]{2,1,0:T(8,128)(2,1)S(1)} collective-permute-done((bf16[32,32,128]{2,1,0:T(8,128)(2,1)S(1)}, bf16[32,32,128]{2,1,0:T(8,128)(2,1)S(1)}, u32[]{:S(2)}, u32[]{:S(2)}) %collective-permute-start) | collective-permute-done | bytes 262176 | tf_op jit(solution)/shard_map/ppermute | solution.py:218
  8.9 0.4 collective-permute-start.1
  9.3 0.1 add_convert_fusion
  9.4 12.6 %all_to_all.15 = bf16[32,32,128]{2,1,0:T(8,128)(2,1)S(1)} all-to-all(bf16[32,32,128]{2,1,0:T(8,128)(2,1)S(1)} %add_convert_fusion), channel_id=1, replica_groups={{0,16,32,48,64,80,96,112,128,144,160,176,192,208,224,240},{8,24,40,56,7..., dimensions={0} | all-to-all | bytes 524288 | tf_op jit(solution)/shard_map/all_to_all | solution.py:209
  22.1 16.0 %all_to_all.16 = bf16[8,2,32,128]{3,2,1,0:T(8,128)(2,1)S(1)} all-to-all(bf16[8,2,32,128]{3,2,1,0:T(8,128)(2,1)S(1)} %broadcast_in_dim.6), channel_id=1, replica_groups=mesh['col'=32,'rep'=8] {'rep'}, dimensions={0} | all-to-all | bytes 262144 | tf_op jit(solution)/shard_map/all_to_all | solution.py:209
  38.1 10.8 %all_to_all.17 = bf16[16,2,32,128]{3,2,1,0:T(8,128)(2,1)S(1)} all-to-all(bf16[16,2,32,128]{3,2,1,0:T(8,128)(2,1)S(1)} %broadcast_in_dim.16), channel_id=1, replica_groups={{0,16,32,48,64,80,96,112,128,144,160,176,192,208,224,240},{8,24,40,56,7..., dimensions={0} | all-to-all | bytes 524288 | tf_op jit(solution)/shard_map/all_to_all | solution.py:209
  49.0 0.0 collective-permute-done.1.other
  49.0 1.5 %raw_factors.1 = bf16[2,32,512]{2,1,0:T(8,128)(2,1)S(1)} custom-call(bf16[32,32,128]{2,1,0:T(8,128)(2,1)S(1)} %bitcast.7, bf16[4096,512]{1,0:T(8,128)(2,1)S(1)} %get-tuple-element.18.own.refs_3_, bf16[4096,512]{1,0:T(8,128)(2,1)S(1)} %collective-permute-done.1.other), custom_call_target="tpu_custom_call" | custom-call | flops 268435456 | bytes 8388608 | tf_op jit(solution)/shard_map/raw_factors/pallas_call | solution.py:100
  50.5 0.1 collective-permute-start.4
  50.6 1.4 %collective-permute-start.3 = (bf16[2,32,512]{2,1,0:T(8,128)(2,1)S(1)}, bf16[2,32,512]{2,1,0:T(8,128)(2,1)S(1)}, u32[]{:S(2)}, u32[]{:S(2)}) collective-permute-start(bf16[2,32,512]{2,1,0:T(8,128)(2,1)S(1)} %raw_factors.1), channel_id=1, source_target_pairs={{0,64},{1,65},{2,66},{3,67},{4,68},{5,69},{6,70},{7,71},{8,10},{9,... | collective-permute-start | bytes 196616 | tf_op jit(solution)/shard_map/ppermute | solution.py:228
  51.9 2.1 %collective-permute-start.2 = (bf16[2,32,512]{2,1,0:T(8,128)(2,1)S(1)}, bf16[2,32,512]{2,1,0:T(8,128)(2,1)S(1)}, u32[]{:S(2)}, u32[]{:S(2)}) collective-permute-start(bf16[2,32,512]{2,1,0:T(8,128)(2,1)S(1)} %raw_factors.1), channel_id=1, source_target_pairs={{0,1},{1,0},{2,3},{3,2},{4,5},{5,4},{6,7},{7,6},{8,9},{9,8},{10,11... | collective-permute-start | bytes 196616 | tf_op jit(solution)/shard_map/ppermute | solution.py:228
  54.1 3.2 %solve.1 = (f32[32,32]{1,0:T(8,128)S(1)}, bf16[4096,64]{1,0:T(8,128)(2,1)S(1)}) custom-call(bf16[32,32,128]{2,1,0:T(8,128)(2,1)S(1)} %bitcast.8), custom_call_target="tpu_custom_call" | custom-call | flops 67108864 | bytes 4194304 | tf_op jit(solution)/shard_map/solve/pallas_call | solution.py:133
  57.2 0.0 collective-permute-done.4
  57.2 0.0 collective-permute-done.3
  57.2 0.0 collective-permute-done.2
  57.3 0.1 collective-permute-start.5
  57.4 5.2 %collective-permute-done.5 = bf16[2,32,512]{2,1,0:T(8,128)(2,1)S(1)} collective-permute-done((bf16[2,32,512]{2,1,0:T(8,128)(2,1)S(1)}, bf16[2,32,512]{2,1,0:T(8,128)(2,1)S(1)}, u32[]{:S(2)}, u32[]{:S(2)}) %collective-permute-start.5) | collective-permute-done | bytes 65568 | tf_op jit(solution)/shard_map/ppermute | solution.py:228
  62.6 0.1 collective-permute-start.6
  62.7 2.7 %finish_leading.1 = (bf16[1,4096,512]{2,1,0:T(8,128)(2,1)}, f32[32,512]{1,0:T(8,128)S(1)}) custom-call(f32[32,512]{1,0:T(8,128)S(1)} %get-tuple-element.28.refs_0_, f32[32,32]{1,0:T(8,128)S(1)} %get-tuple-element.24.refs_1_, bf16[4096,64]{1,0:T(8,128)(2,1)S(1)} %get-tuple-element.25.refs_2_, bf16[4096,512]{1,0:T(8,128)(2,1)S(1)} %get-tuple-element.18.own.refs_3_), custom_call_target="tpu_custom_call" | custom-call | flops 268435456 | bytes 8388608 | tf_op jit(solution)/shard_map/finish_leading/pallas_call | solution.py:188
  65.5 0.0 collective-permute-done.6.refs_0_
  65.5 0.7 %finish_other.1 = (bf16[1,4096,512]{2,1,0:T(8,128)(2,1)}, f32[32,512]{1,0:T(8,128)}) custom-call(f32[32,512]{1,0:T(8,128)S(1)} %collective-permute-done.6.refs_0_, f32[32,32]{1,0:T(8,128)S(1)} %get-tuple-element.24.refs_1_, bf16[4096,64]{1,0:T(8,128)(2,1)S(1)} %get-tuple-element.25.refs_2_, ...), custom_call_target="tpu_custom_call", output_to_operand_aliasing={{0}: (4, {})} | custom-call | flops 268435456 | bytes 8388608 | tf_op jit(solution)/shard_map/finish_other/pallas_call | solution.py:188
  (7 shorter events, 0.2 us)
Async XLA Ops:
  4.4 4.5 %collective-permute-start = (bf16[32,32,128]{2,1,0:T(8,128)(2,1)S(1)}, bf16[32,32,128]{2,1,0:T(8,128)(2,1)S(1)}, u32[]{:S(2)}, u32[]{:S(2)}) collective-permute-start(bf16[32,32,128]{2,1,0:T(8,128)(2,1)S(1)} %get-tuple-element.15), channel_id=1, source_target_pairs={{0,8},{8,0},{16,24},{24,16},{32,40},{40,32},{48,56},{56,48},{64,72... | collective-permute-start | bytes 786440 | tf_op jit(solution)/shard_map/ppermute | solution.py:218
  8.9 40.0 %collective-permute-start.1 = (bf16[4096,512]{1,0:T(8,128)(2,1)S(1)}, bf16[4096,512]{1,0:T(8,128)(2,1)S(1)}, u32[]{:S(2)}, u32[]{:S(2)}) collective-permute-start(bf16[4096,512]{1,0:T(8,128)(2,1)S(1)} %get-tuple-element.18.own.refs_3_), channel_id=1, source_target_pairs={{0,8},{8,0},{16,24},{24,16},{32,40},{40,32},{48,56},{56,48},{64,72... | collective-permute-start | bytes 12582920 | tf_op jit(solution)/shard_map/ppermute | solution.py:218
  50.5 6.7 %collective-permute-start.4 = (bf16[2,32,512]{2,1,0:T(8,128)(2,1)S(1)}, bf16[2,32,512]{2,1,0:T(8,128)(2,1)S(1)}, u32[]{:S(2)}, u32[]{:S(2)}) collective-permute-start(bf16[2,32,512]{2,1,0:T(8,128)(2,1)S(1)} %raw_factors.1), channel_id=1, source_target_pairs={{0,16},{1,17},{2,18},{3,19},{4,20},{5,21},{6,22},{7,23},{8,11},{9,... | collective-permute-start | bytes 196616 | tf_op jit(solution)/shard_map/ppermute | solution.py:228
  50.6 6.6 %collective-permute-start.3 = (bf16[2,32,512]{2,1,0:T(8,128)(2,1)S(1)}, bf16[2,32,512]{2,1,0:T(8,128)(2,1)S(1)}, u32[]{:S(2)}, u32[]{:S(2)}) collective-permute-start(bf16[2,32,512]{2,1,0:T(8,128)(2,1)S(1)} %raw_factors.1), channel_id=1, source_target_pairs={{0,64},{1,65},{2,66},{3,67},{4,68},{5,69},{6,70},{7,71},{8,10},{9,... | collective-permute-start | bytes 196616 | tf_op jit(solution)/shard_map/ppermute | solution.py:228
  51.9 5.3 %collective-permute-start.2 = (bf16[2,32,512]{2,1,0:T(8,128)(2,1)S(1)}, bf16[2,32,512]{2,1,0:T(8,128)(2,1)S(1)}, u32[]{:S(2)}, u32[]{:S(2)}) collective-permute-start(bf16[2,32,512]{2,1,0:T(8,128)(2,1)S(1)} %raw_factors.1), channel_id=1, source_target_pairs={{0,1},{1,0},{2,3},{3,2},{4,5},{5,4},{6,7},{7,6},{8,9},{9,8},{10,11... | collective-permute-start | bytes 196616 | tf_op jit(solution)/shard_map/ppermute | solution.py:228
  57.3 5.3 %collective-permute-start.5 = (bf16[2,32,512]{2,1,0:T(8,128)(2,1)S(1)}, bf16[2,32,512]{2,1,0:T(8,128)(2,1)S(1)}, u32[]{:S(2)}, u32[]{:S(2)}) collective-permute-start(bf16[2,32,512]{2,1,0:T(8,128)(2,1)S(1)} %add_convert_fusion.1), channel_id=1, source_target_pairs={{0,1},{1,0},{2,3},{3,2},{4,5},{5,4},{6,7},{7,6},{8,14},{9,15},{10,... | collective-permute-start | bytes 196616 | tf_op jit(solution)/shard_map/ppermute | solution.py:228
  62.6 2.8 %collective-permute-start.6 = (f32[32,512]{1,0:T(8,128)S(1)}, f32[32,512]{1,0:T(8,128)S(1)}, u32[]{:S(2)}, u32[]{:S(2)}) collective-permute-start(f32[32,512]{1,0:T(8,128)S(1)} %get-tuple-element.29), channel_id=1, source_target_pairs={{0,8},{8,0},{16,24},{24,16},{32,40},{40,32},{48,56},{56,48},{64,72... | collective-permute-start | bytes 196616 | tf_op jit(solution)/shard_map/ppermute | solution.py:218

commit v9 on v8

--- a/solution.py
+++ b/solution.py
@@ -108,17 +108,34 @@
     )(in_vmem(p_sum), in_vmem(own), in_vmem(other))
 
 
-def solve_kernel(p_sum, inverse, turned):
+def turn_kernel(p_sum, gram, turned):
     blocks, rank, lanes = p_sum.shape
     wide = side_by_side(p_sum)
-    gram = lax.dot_general(wide, wide, (((1,), (1,)), ((), ())), preferred_element_type=F32)
+    gram[...] = lax.dot_general(wide, wide, (((1,), (1,)), ((), ())), preferred_element_type=F32)
     for block in range(blocks):
-        tall = p_sum[block].astype(F32).T.astype(BF16)
+        tall = wide[:, block * lanes : (block + 1) * lanes].astype(F32).T.astype(BF16)
         turned[pl.ds(block * lanes, lanes), :] = jnp.concatenate([tall, tall], axis=1)
+
+
+def turn(p_sum):
+    blocks, rank, lanes = p_sum.shape
+    return pl.pallas_call(
+        turn_kernel,
+        in_specs=[WHOLE],
+        out_specs=[WHOLE, WHOLE],
+        out_shape=[pltpu.VMEM((rank, rank), F32), pltpu.VMEM((blocks * lanes, 2 * rank), BF16)],
+        compiler_params=params(),
+        cost_estimate=pl.CostEstimate(flops=8 * rank * rank * blocks * lanes, bytes_accessed=2 << 20, transcendentals=0),
+        name="turn",
+    )(in_vmem(p_sum))
+
+
+def solve_kernel(gram, inverse):
+    rank = gram.shape[0]
     row = lax.broadcasted_iota(jnp.int32, (rank, rank), 0)
     col = lax.broadcasted_iota(jnp.int32, (rank, rank), 1)
     one = (row == col).astype(F32)
-    table = jnp.concatenate([gram, one], axis=1)
+    table = jnp.concatenate([gram[...], one], axis=1)
     below = lax.broadcasted_iota(jnp.int32, (rank, 1), 0)
     for k in range(rank):
         pivot = table[k : k + 1, :]
@@ -128,29 +145,29 @@
     inverse[...] = table[:, rank:] * lax.rsqrt(diagonal)
 
 
-def solve(p_sum):
-    blocks, rank, lanes = p_sum.shape
+def solve(gram):
     return pl.pallas_call(
         solve_kernel,
         in_specs=[WHOLE],
-        out_specs=[WHOLE, WHOLE],
-        out_shape=[pltpu.VMEM((rank, rank), F32), pltpu.VMEM((blocks * lanes, 2 * rank), BF16)],
-        compiler_params=params(),
-        cost_estimate=pl.CostEstimate(flops=16 * rank * rank * blocks * lanes, bytes_accessed=4 << 20, transcendentals=0),
+        out_specs=WHOLE,
+        out_shape=pltpu.VMEM(gram.shape, F32),
+        compiler_params=params(),
+        cost_estimate=pl.CostEstimate(flops=8 << 20, bytes_accessed=4 << 20, transcendentals=0),
         name="solve",
-    )(in_vmem(p_sum))
-
-
-def finish_rows(replicas, raw, inverse, turned, merged, new_error, q_factor, halves, result, done):
+    )(in_vmem(gram))
+
+
+def finish_rows(replicas, raw, inverse, turned, merged, new_error, q_factor, halves, result, factor_out, done):
     factor = jnp.dot(inverse[...], raw[...], precision=HIGHEST, preferred_element_type=F32) * (1.0 / replicas)
-    q_factor[...] = factor
+    factor_out[...] = factor
+    copies = [pltpu.make_async_copy(factor_out, q_factor, done.at[merged.shape[0] // STEP])]
+    copies[0].start()
     rounded = factor.astype(BF16).astype(F32)
     solved = lax.dot_general(
         inverse[...], rounded, (((0,), (0,)), ((), ())), precision=HIGHEST, preferred_element_type=F32
     )
     high = solved.astype(BF16)
     halves[...] = jnp.concatenate([high, (solved - high.astype(F32)).astype(BF16)], axis=0)
-    copies = []
     for chunk in range(merged.shape[0] // STEP):
         here = rows_of(chunk)
         rebuilt = jnp.dot(turned[here, :], halves[...], preferred_element_type=F32)
@@ -161,24 +178,16 @@
         copy.wait()
 
 
-def first_kernel(replicas, raw, inverse, turned, merged, new_error, q_factor, *scratch):
+def first_kernel(replicas, *refs):
     @pl.when(leads())
     def _():
-        finish_rows(replicas, raw, inverse, turned, merged, new_error, q_factor, *scratch)
-
+        finish_rows(replicas, *refs)
+
+
+def second_kernel(replicas, raw, inverse, turned, merged, new_error_in, q_factor_in, *refs):
     @pl.when(jnp.logical_not(leads()))
     def _():
-        q_factor[...] = jnp.zeros_like(q_factor)
-
-
-def second_kernel(replicas, raw, inverse, turned, merged, _, q_begun, new_error, q_factor, *scratch):
-    @pl.when(leads())
-    def _():
-        q_factor[...] = q_begun[...]
-
-    @pl.when(jnp.logical_not(leads()))
-    def _():
-        finish_rows(replicas, raw, inverse, turned, merged, new_error, q_factor, *scratch)
+        finish_rows(replicas, raw, inverse, turned, merged, *refs)
 
 
 def finish(raw, inverse, turned, merged, replicas, *begun):
@@ -187,22 +196,20 @@
     kernel = second_kernel if begun else first_kernel
     return pl.pallas_call(
         lambda *refs: kernel(replicas, *refs),
-        in_specs=[WHOLE] * 4 + [ANYWHERE, WHOLE][: len(begun)],
-        out_specs=[ANYWHERE, WHOLE],
-        out_shape=[
-            pltpu.HBM((1, rows, columns), BF16),
-            jax.ShapeDtypeStruct((rank, columns), F32),
-        ],
-        input_output_aliases={4: 0} if begun else {},
+        in_specs=[WHOLE] * 4 + [ANYWHERE] * len(begun),
+        out_specs=[ANYWHERE] * 2,
+        out_shape=[pltpu.HBM((1, rows, columns), BF16), pltpu.HBM((rank, columns), F32)],
+        input_output_aliases={4 + i: i for i in range(len(begun))},
         scratch_shapes=[
             pltpu.VMEM((2 * rank, columns), BF16),
             pltpu.VMEM((rows, columns), BF16),
-            pltpu.SemaphoreType.DMA((rows // STEP,)),
+            pltpu.VMEM((rank, columns), F32),
+            pltpu.SemaphoreType.DMA((rows // STEP + 1,)),
         ],
         compiler_params=params(),
         cost_estimate=pl.CostEstimate(flops=4 * rank * rows * columns, bytes_accessed=4 * rows * columns, transcendentals=0),
         name="finish_other" if begun else "finish_leading",
-    )(*(in_vmem(x) for x in (raw, inverse, turned, merged)), *begun)
+    )(*(in_vmem(x) for x in (raw, inverse, turned, merged)), *(in_hbm(x) for x in begun))
 
 
 def exchange(blocks, axis, groups=None):
@@ -252,11 +259,12 @@
     other = swap_cores(merged)
     p_sum = left_factor(part)
     raw = raw_factors(p_sum, merged, other)
-    inverse, turned = solve(p_sum)
+    gram, turned = turn(p_sum)
     near = [swap_chips(raw, 1, (0, 1)), swap_chips(raw, 2, (8, 0)), swap_chips(raw, 3, (2, 0))]
-    raw, inverse, *near = lax.optimization_barrier((raw, inverse, *near))
+    raw, gram, *near = lax.optimization_barrier((raw, gram, *near))
     raw = total([raw, *near]).astype(BF16)
-    raw = total([raw, swap_chips(raw, 6, (0, 1))])
+    far, inverse = lax.optimization_barrier((swap_chips(raw, 6, (0, 1)), solve(gram)))
+    raw = total([raw, far])
     begun = finish(raw[0], inverse, turned, merged, replicas)
     return tuple(finish(swap_cores(raw[1]), inverse, turned, merged, replicas, *begun))
 

time: 66.6 us -> 65.8 us (0.988)
  waiting for transfers between devices: 6.39 us -> 5.6 us
    ppermute x4, waiting for transfers between devices: 5.22 us -> 4.43 us  [swap_chips(): return lax.ppermute(block, ('col', 'rep'), pairs)]
    pallas_call x1 -> x2, Pallas kernels: 3.16 us -> 3.4 us  [the longest x1 2.76 us: solve(): pl.pallas_call(solve_kernel, in_specs=[WHOLE], out_specs=WHOLE, out_shape...]
  transfers between devices with their start and end apart: 7 -> 7, of which waited for: 2 -> 4; matrix products, arithmetic and copies ran while one was open for 0% -> 0% of each run, Pallas kernels for 9% -> 9%
where the time goes in v9:
time: 65.8 us; the launch traced here: 65.5 us
  blocking collectives  39.4 us (60%)
  Pallas kernels  11.6 us (18%)
  starting transfers between devices  7.91 us (12%)
  waiting for transfers between devices  5.6 us (9%)
  between operations  0.71 us (1%)
    all_to_all x3, blocking collectives, exchange(): lax.all_to_all(blocks, axis, 0, 0, axis_index_groups=groups, tiled=True)  39.4 us
    ppermute x4, waiting for transfers between devices, swap_chips(): return lax.ppermute(block, ('col', 'rep'), pairs)  4.43 us
    ppermute x4, starting transfers between devices, swap_chips(): return lax.ppermute(block, ('col', 'rep'), pairs)  4.06 us
    ppermute x3, starting transfers between devices, swap_cores(): lax.ppermute(block, 'col', [(i, i ^ 1) for i in range(lax.axis_size('col'...  3.85 us
    pallas_call x1, Pallas kernels, merge(): pl.pallas_call(merge_kernel, in_specs=[ANYWHERE] * 3, out_specs=[WHOLE, W...  3.81 us
    pallas_call x2, Pallas kernels, finish(): pl.pallas_call(lambda *refs: kernel(replicas, *refs), in_specs=[WHOLE] *...  2.83 us
    pallas_call x1, Pallas kernels, solve(): pl.pallas_call(solve_kernel, in_specs=[WHOLE], out_specs=WHOLE, out_shape...  2.76 us
    pallas_call x1, Pallas kernels, raw_factors(): pl.pallas_call(raw_kernel, in_specs=[WHOLE] * 3, out_specs=WHOLE, out_sha...  1.52 us
  transfers between devices with their start and end apart: 7, of which 4 were waited for; matrix products, arithmetic and copies ran while one was open for 0% of the time, Pallas kernels for 9%

profile of v9, /device:TPU:1, one launch (start us, length us, event | category | flops | bytes accessed | tf_op | source)
XLA Modules:
  0.0 65.5 jit_solution(8737022396533758262)
XLA Ops:
  0.6 3.8 %merge.1 = (bf16[4096,512]{1,0:T(8,128)(2,1)S(1)}, bf16[32,32,128]{2,1,0:T(8,128)(2,1)S(1)}) custom-call(bf16[1,4096,512]{2,1,0:T(8,128)(2,1)} %gradient.1, bf16[1,4096,512]{2,1,0:T(8,128)(2,1)} %error.1, bf16[32,512]{1,0:T(8,128)(2,1)} %warm.1), custom_call_target="tpu_custom_call" | custom-call | flops 134217728 | bytes 8388608 | tf_op jit(solution)/shard_map/merge/pallas_call | solution.py:57
  4.4 3.3 %collective-permute-start = (bf16[32,32,128]{2,1,0:T(8,128)(2,1)S(1)}, bf16[32,32,128]{2,1,0:T(8,128)(2,1)S(1)}, u32[]{:S(2)}, u32[]{:S(2)}) collective-permute-start(bf16[32,32,128]{2,1,0:T(8,128)(2,1)S(1)} %get-tuple-element.17), channel_id=1, source_target_pairs={{0,8},{8,0},{16,24},{24,16},{32,40},{40,32},{48,56},{56,48},{64,72... | collective-permute-start | bytes 786440 | tf_op jit(solution)/shard_map/ppermute | solution.py:225
  7.8 1.2 %collective-permute-done = bf16[32,32,128]{2,1,0:T(8,128)(2,1)S(1)} collective-permute-done((bf16[32,32,128]{2,1,0:T(8,128)(2,1)S(1)}, bf16[32,32,128]{2,1,0:T(8,128)(2,1)S(1)}, u32[]{:S(2)}, u32[]{:S(2)}) %collective-permute-start) | collective-permute-done | bytes 262176 | tf_op jit(solution)/shard_map/ppermute | solution.py:225
  8.9 0.4 collective-permute-start.1
  9.3 0.1 add_convert_fusion
  9.4 12.6 %all_to_all.15 = bf16[32,32,128]{2,1,0:T(8,128)(2,1)S(1)} all-to-all(bf16[32,32,128]{2,1,0:T(8,128)(2,1)S(1)} %add_convert_fusion), channel_id=1, replica_groups={{0,16,32,48,64,80,96,112,128,144,160,176,192,208,224,240},{8,24,40,56,7..., dimensions={0} | all-to-all | bytes 524288 | tf_op jit(solution)/shard_map/all_to_all | solution.py:216
  22.1 16.0 %all_to_all.16 = bf16[8,2,32,128]{3,2,1,0:T(8,128)(2,1)S(1)} all-to-all(bf16[8,2,32,128]{3,2,1,0:T(8,128)(2,1)S(1)} %broadcast_in_dim.6), channel_id=1, replica_groups=mesh['col'=32,'rep'=8] {'rep'}, dimensions={0} | all-to-all | bytes 262144 | tf_op jit(solution)/shard_map/all_to_all | solution.py:216
  38.1 10.8 %all_to_all.17 = bf16[16,2,32,128]{3,2,1,0:T(8,128)(2,1)S(1)} all-to-all(bf16[16,2,32,128]{3,2,1,0:T(8,128)(2,1)S(1)} %broadcast_in_dim.16), channel_id=1, replica_groups={{0,16,32,48,64,80,96,112,128,144,160,176,192,208,224,240},{8,24,40,56,7..., dimensions={0} | all-to-all | bytes 524288 | tf_op jit(solution)/shard_map/all_to_all | solution.py:216
  49.0 0.0 collective-permute-done.1.other
  49.0 1.5 %raw_factors.1 = bf16[2,32,512]{2,1,0:T(8,128)(2,1)S(1)} custom-call(bf16[32,32,128]{2,1,0:T(8,128)(2,1)S(1)} %bitcast.7, bf16[4096,512]{1,0:T(8,128)(2,1)S(1)} %get-tuple-element.20.own.refs_3_, bf16[4096,512]{1,0:T(8,128)(2,1)S(1)} %collective-permute-done.1.other), custom_call_target="tpu_custom_call" | custom-call | flops 268435456 | bytes 8388608 | tf_op jit(solution)/shard_map/raw_factors/pallas_call | solution.py:100
  50.5 0.1 collective-permute-start.4
  50.6 1.4 %collective-permute-start.3 = (bf16[2,32,512]{2,1,0:T(8,128)(2,1)S(1)}, bf16[2,32,512]{2,1,0:T(8,128)(2,1)S(1)}, u32[]{:S(2)}, u32[]{:S(2)}) collective-permute-start(bf16[2,32,512]{2,1,0:T(8,128)(2,1)S(1)} %raw_factors.1), channel_id=1, source_target_pairs={{0,64},{1,65},{2,66},{3,67},{4,68},{5,69},{6,70},{7,71},{8,10},{9,... | collective-permute-start | bytes 196616 | tf_op jit(solution)/shard_map/ppermute | solution.py:235
  51.9 2.1 %collective-permute-start.2 = (bf16[2,32,512]{2,1,0:T(8,128)(2,1)S(1)}, bf16[2,32,512]{2,1,0:T(8,128)(2,1)S(1)}, u32[]{:S(2)}, u32[]{:S(2)}) collective-permute-start(bf16[2,32,512]{2,1,0:T(8,128)(2,1)S(1)} %raw_factors.1), channel_id=1, source_target_pairs={{0,1},{1,0},{2,3},{3,2},{4,5},{5,4},{6,7},{7,6},{8,9},{9,8},{10,11... | collective-permute-start | bytes 196616 | tf_op jit(solution)/shard_map/ppermute | solution.py:235
  54.1 0.6 turn.1
  54.7 0.8 %collective-permute-done.4 = bf16[2,32,512]{2,1,0:T(8,128)(2,1)S(1)} collective-permute-done((bf16[2,32,512]{2,1,0:T(8,128)(2,1)S(1)}, bf16[2,32,512]{2,1,0:T(8,128)(2,1)S(1)}, u32[]{:S(2)}, u32[]{:S(2)}) %collective-permute-start.4) | collective-permute-done | bytes 65568 | tf_op jit(solution)/shard_map/ppermute | solution.py:235
  55.5 0.0 collective-permute-done.3
  55.5 0.9 %collective-permute-done.2 = bf16[2,32,512]{2,1,0:T(8,128)(2,1)S(1)} collective-permute-done((bf16[2,32,512]{2,1,0:T(8,128)(2,1)S(1)}, bf16[2,32,512]{2,1,0:T(8,128)(2,1)S(1)}, u32[]{:S(2)}, u32[]{:S(2)}) %collective-permute-start.2) | collective-permute-done | bytes 65568 | tf_op jit(solution)/shard_map/ppermute | solution.py:235
  56.5 0.5 collective-permute-start.5
  56.9 2.8 %solve.1.refs_1_ = f32[32,32]{1,0:T(8,128)S(1)} custom-call(f32[32,32]{1,0:T(8,128)S(1)} %get-tuple-element.26.gram), custom_call_target="tpu_custom_call" | custom-call | flops 8388608 | bytes 4194304 | tf_op jit(solution)/shard_map/solve/pallas_call | solution.py:149
  59.7 2.7 %collective-permute-done.5 = bf16[2,32,512]{2,1,0:T(8,128)(2,1)S(1)} collective-permute-done((bf16[2,32,512]{2,1,0:T(8,128)(2,1)S(1)}, bf16[2,32,512]{2,1,0:T(8,128)(2,1)S(1)}, u32[]{:S(2)}, u32[]{:S(2)}) %collective-permute-start.5) | collective-permute-done | bytes 65568 | tf_op jit(solution)/shard_map/ppermute | solution.py:235
  62.5 0.1 collective-permute-start.6
  62.6 2.7 %finish_leading.1 = (bf16[1,4096,512]{2,1,0:T(8,128)(2,1)}, f32[32,512]{1,0:T(8,128)}) custom-call(f32[32,512]{1,0:T(8,128)S(1)} %get-tuple-element.32.refs_0_, f32[32,32]{1,0:T(8,128)S(1)} %solve.1.refs_1_, bf16[4096,64]{1,0:T(8,128)(2,1)S(1)} %get-tuple-element.29.refs_2_, bf16[4096,512]{1,0:T(8,128)(2,1)S(1)} %get-tuple-element.20.own.refs_3_), custom_call_target="tpu_custom_call" | custom-call | flops 268435456 | bytes 8388608 | tf_op jit(solution)/shard_map/finish_leading/pallas_call | solution.py:197
  65.3 0.0 collective-permute-done.6.refs_0_
  65.4 0.1 finish_other.1
  (7 shorter events, 0.2 us)
Async XLA Ops:
  4.4 4.5 %collective-permute-start = (bf16[32,32,128]{2,1,0:T(8,128)(2,1)S(1)}, bf16[32,32,128]{2,1,0:T(8,128)(2,1)S(1)}, u32[]{:S(2)}, u32[]{:S(2)}) collective-permute-start(bf16[32,32,128]{2,1,0:T(8,128)(2,1)S(1)} %get-tuple-element.17), channel_id=1, source_target_pairs={{0,8},{8,0},{16,24},{24,16},{32,40},{40,32},{48,56},{56,48},{64,72... | collective-permute-start | bytes 786440 | tf_op jit(solution)/shard_map/ppermute | solution.py:225
  8.9 40.0 %collective-permute-start.1 = (bf16[4096,512]{1,0:T(8,128)(2,1)S(1)}, bf16[4096,512]{1,0:T(8,128)(2,1)S(1)}, u32[]{:S(2)}, u32[]{:S(2)}) collective-permute-start(bf16[4096,512]{1,0:T(8,128)(2,1)S(1)} %get-tuple-element.20.own.refs_3_), channel_id=1, source_target_pairs={{0,8},{8,0},{16,24},{24,16},{32,40},{40,32},{48,56},{56,48},{64,72... | collective-permute-start | bytes 12582920 | tf_op jit(solution)/shard_map/ppermute | solution.py:225
  50.5 5.0 %collective-permute-start.4 = (bf16[2,32,512]{2,1,0:T(8,128)(2,1)S(1)}, bf16[2,32,512]{2,1,0:T(8,128)(2,1)S(1)}, u32[]{:S(2)}, u32[]{:S(2)}) collective-permute-start(bf16[2,32,512]{2,1,0:T(8,128)(2,1)S(1)} %raw_factors.1), channel_id=1, source_target_pairs={{0,16},{1,17},{2,18},{3,19},{4,20},{5,21},{6,22},{7,23},{8,11},{9,... | collective-permute-start | bytes 196616 | tf_op jit(solution)/shard_map/ppermute | solution.py:235
  50.6 4.9 %collective-permute-start.3 = (bf16[2,32,512]{2,1,0:T(8,128)(2,1)S(1)}, bf16[2,32,512]{2,1,0:T(8,128)(2,1)S(1)}, u32[]{:S(2)}, u32[]{:S(2)}) collective-permute-start(bf16[2,32,512]{2,1,0:T(8,128)(2,1)S(1)} %raw_factors.1), channel_id=1, source_target_pairs={{0,64},{1,65},{2,66},{3,67},{4,68},{5,69},{6,70},{7,71},{8,10},{9,... | collective-permute-start | bytes 196616 | tf_op jit(solution)/shard_map/ppermute | solution.py:235
  51.9 4.5 %collective-permute-start.2 = (bf16[2,32,512]{2,1,0:T(8,128)(2,1)S(1)}, bf16[2,32,512]{2,1,0:T(8,128)(2,1)S(1)}, u32[]{:S(2)}, u32[]{:S(2)}) collective-permute-start(bf16[2,32,512]{2,1,0:T(8,128)(2,1)S(1)} %raw_factors.1), channel_id=1, source_target_pairs={{0,1},{1,0},{2,3},{3,2},{4,5},{5,4},{6,7},{7,6},{8,9},{9,8},{10,11... | collective-permute-start | bytes 196616 | tf_op jit(solution)/shard_map/ppermute | solution.py:235
  56.5 6.0 %collective-permute-start.5 = (bf16[2,32,512]{2,1,0:T(8,128)(2,1)S(1)}, bf16[2,32,512]{2,1,0:T(8,128)(2,1)S(1)}, u32[]{:S(2)}, u32[]{:S(2)}) collective-permute-start(bf16[2,32,512]{2,1,0:T(8,128)(2,1)S(1)} %add_convert_fusion.1), channel_id=1, source_target_pairs={{0,1},{1,0},{2,3},{3,2},{4,5},{5,4},{6,7},{7,6},{8,14},{9,15},{10,... | collective-permute-start | bytes 196616 | tf_op jit(solution)/shard_map/ppermute | solution.py:235
  62.5 2.9 %collective-permute-start.6 = (f32[32,512]{1,0:T(8,128)S(1)}, f32[32,512]{1,0:T(8,128)S(1)}, u32[]{:S(2)}, u32[]{:S(2)}) collective-permute-start(f32[32,512]{1,0:T(8,128)S(1)} %get-tuple-element.33), channel_id=1, source_target_pairs={{0,8},{8,0},{16,24},{24,16},{32,40},{40,32},{48,56},{56,48},{64,72... | collective-permute-start | bytes 196616 | tf_op jit(solution)/shard_map/ppermute | solution.py:225

commit v10 on v9

--- a/solution.py
+++ b/solution.py
@@ -225,12 +225,13 @@
     return lax.ppermute(block, "col", [(i, i ^ 1) for i in range(lax.axis_size("col"))])
 
 
-def swap_chips(block, mask, idle):
+def swap_chips(block, mask):
     columns, replicas = lax.axis_size("col"), lax.axis_size("rep")
+    beside = columns // 4
     pairs = []
     for c in range(columns):
         for r in range(replicas):
-            partner = (c, r ^ mask) if c % CORES else (c ^ idle[0], r ^ idle[1])
+            partner = (c, r ^ mask) if c % CORES else (c ^ beside, r)
             pairs.append((c * replicas + r, partner[0] * replicas + partner[1]))
     return lax.ppermute(block, ("col", "rep"), pairs)
 
@@ -260,10 +261,10 @@
     p_sum = left_factor(part)
     raw = raw_factors(p_sum, merged, other)
     gram, turned = turn(p_sum)
-    near = [swap_chips(raw, 1, (0, 1)), swap_chips(raw, 2, (8, 0)), swap_chips(raw, 3, (2, 0))]
+    near = [swap_chips(raw, mask) for mask in (1, 2, 3)]
     raw, gram, *near = lax.optimization_barrier((raw, gram, *near))
     raw = total([raw, *near]).astype(BF16)
-    far, inverse = lax.optimization_barrier((swap_chips(raw, 6, (0, 1)), solve(gram)))
+    far, inverse = lax.optimization_barrier((swap_chips(raw, 6), solve(gram)))
     raw = total([raw, far])
     begun = finish(raw[0], inverse, turned, merged, replicas)
     return tuple(finish(swap_cores(raw[1]), inverse, turned, merged, replicas, *begun))

time: 65.8 us -> 67 us (1.018)
  starting transfers between devices: 7.91 us -> 9.81 us
    ppermute x3, starting transfers between devices: 3.85 us -> 5.76 us  [swap_cores(): lax.ppermute(block, 'col', [(i, i ^ 1) for i in range(lax.axis_size('col'...]
where the time goes in v10:
time: 67 us; the launch traced here: 66.8 us
  blocking collectives  39.4 us (59%)
  Pallas kernels  11.6 us (17%)
  starting transfers between devices  9.81 us (15%)
  waiting for transfers between devices  5.04 us (8%)
  between operations  0.71 us (1%)
    all_to_all x3, blocking collectives, exchange(): lax.all_to_all(blocks, axis, 0, 0, axis_index_groups=groups, tiled=True)  39.4 us
    ppermute x3, starting transfers between devices, swap_cores(): lax.ppermute(block, 'col', [(i, i ^ 1) for i in range(lax.axis_size('col'...  5.76 us
    ppermute x4, starting transfers between devices, swap_chips(): return lax.ppermute(block, ('col', 'rep'), pairs)  4.06 us
    ppermute x4, waiting for transfers between devices, swap_chips(): return lax.ppermute(block, ('col', 'rep'), pairs)  3.87 us
    pallas_call x1, Pallas kernels, merge(): pl.pallas_call(merge_kernel, in_specs=[ANYWHERE] * 3, out_specs=[WHOLE, W...  3.81 us
    pallas_call x2, Pallas kernels, finish(): pl.pallas_call(lambda *refs: kernel(replicas, *refs), in_specs=[WHOLE] *...  2.83 us
    pallas_call x1, Pallas kernels, solve(): pl.pallas_call(solve_kernel, in_specs=[WHOLE], out_specs=WHOLE, out_shape...  2.76 us
    pallas_call x1, Pallas kernels, raw_factors(): pl.pallas_call(raw_kernel, in_specs=[WHOLE] * 3, out_specs=WHOLE, out_sha...  1.52 us
  transfers between devices with their start and end apart: 7, of which 4 were waited for; matrix products, arithmetic and copies ran while one was open for 0% of the time, Pallas kernels for 9%

profile of v10, /device:TPU:1, one launch (start us, length us, event | category | flops | bytes accessed | tf_op | source)
XLA Modules:
  0.0 66.8 jit_solution(11766991221054863839)
XLA Ops:
  0.6 3.8 %merge.1 = (bf16[4096,512]{1,0:T(8,128)(2,1)S(1)}, bf16[32,32,128]{2,1,0:T(8,128)(2,1)S(1)}) custom-call(bf16[1,4096,512]{2,1,0:T(8,128)(2,1)} %gradient.1, bf16[1,4096,512]{2,1,0:T(8,128)(2,1)} %error.1, bf16[32,512]{1,0:T(8,128)(2,1)} %warm.1), custom_call_target="tpu_custom_call" | custom-call | flops 134217728 | bytes 8388608 | tf_op jit(solution)/shard_map/merge/pallas_call | solution.py:57
  4.4 3.3 %collective-permute-start = (bf16[32,32,128]{2,1,0:T(8,128)(2,1)S(1)}, bf16[32,32,128]{2,1,0:T(8,128)(2,1)S(1)}, u32[]{:S(2)}, u32[]{:S(2)}) collective-permute-start(bf16[32,32,128]{2,1,0:T(8,128)(2,1)S(1)} %get-tuple-element.17), channel_id=1, source_target_pairs={{0,8},{8,0},{16,24},{24,16},{32,40},{40,32},{48,56},{56,48},{64,72... | collective-permute-start | bytes 786440 | tf_op jit(solution)/shard_map/ppermute | solution.py:225
  7.8 1.2 %collective-permute-done = bf16[32,32,128]{2,1,0:T(8,128)(2,1)S(1)} collective-permute-done((bf16[32,32,128]{2,1,0:T(8,128)(2,1)S(1)}, bf16[32,32,128]{2,1,0:T(8,128)(2,1)S(1)}, u32[]{:S(2)}, u32[]{:S(2)}) %collective-permute-start) | collective-permute-done | bytes 262176 | tf_op jit(solution)/shard_map/ppermute | solution.py:225
  8.9 0.4 collective-permute-start.1
  9.3 0.1 add_convert_fusion
  9.4 12.6 %all_to_all.15 = bf16[32,32,128]{2,1,0:T(8,128)(2,1)S(1)} all-to-all(bf16[32,32,128]{2,1,0:T(8,128)(2,1)S(1)} %add_convert_fusion), channel_id=1, replica_groups={{0,16,32,48,64,80,96,112,128,144,160,176,192,208,224,240},{8,24,40,56,7..., dimensions={0} | all-to-all | bytes 524288 | tf_op jit(solution)/shard_map/all_to_all | solution.py:216
  22.1 16.0 %all_to_all.16 = bf16[8,2,32,128]{3,2,1,0:T(8,128)(2,1)S(1)} all-to-all(bf16[8,2,32,128]{3,2,1,0:T(8,128)(2,1)S(1)} %broadcast_in_dim.6), channel_id=1, replica_groups=mesh['col'=32,'rep'=8] {'rep'}, dimensions={0} | all-to-all | bytes 262144 | tf_op jit(solution)/shard_map/all_to_all | solution.py:216
  38.1 10.8 %all_to_all.17 = bf16[16,2,32,128]{3,2,1,0:T(8,128)(2,1)S(1)} all-to-all(bf16[16,2,32,128]{3,2,1,0:T(8,128)(2,1)S(1)} %broadcast_in_dim.16), channel_id=1, replica_groups={{0,16,32,48,64,80,96,112,128,144,160,176,192,208,224,240},{8,24,40,56,7..., dimensions={0} | all-to-all | bytes 524288 | tf_op jit(solution)/shard_map/all_to_all | solution.py:216
  49.0 0.0 collective-permute-done.1.other
  49.0 1.5 %raw_factors.1 = bf16[2,32,512]{2,1,0:T(8,128)(2,1)S(1)} custom-call(bf16[32,32,128]{2,1,0:T(8,128)(2,1)S(1)} %bitcast.7, bf16[4096,512]{1,0:T(8,128)(2,1)S(1)} %get-tuple-element.20.own.refs_3_, bf16[4096,512]{1,0:T(8,128)(2,1)S(1)} %collective-permute-done.1.other), custom_call_target="tpu_custom_call" | custom-call | flops 268435456 | bytes 8388608 | tf_op jit(solution)/shard_map/raw_factors/pallas_call | solution.py:100
  50.5 0.1 collective-permute-start.4
  50.6 1.4 %collective-permute-start.3 = (bf16[2,32,512]{2,1,0:T(8,128)(2,1)S(1)}, bf16[2,32,512]{2,1,0:T(8,128)(2,1)S(1)}, u32[]{:S(2)}, u32[]{:S(2)}) collective-permute-start(bf16[2,32,512]{2,1,0:T(8,128)(2,1)S(1)} %raw_factors.1), channel_id=1, source_target_pairs={{0,64},{1,65},{2,66},{3,67},{4,68},{5,69},{6,70},{7,71},{8,10},{9,... | collective-permute-start | bytes 196616 | tf_op jit(solution)/shard_map/ppermute | solution.py:236
  51.9 2.1 %collective-permute-start.2 = (bf16[2,32,512]{2,1,0:T(8,128)(2,1)S(1)}, bf16[2,32,512]{2,1,0:T(8,128)(2,1)S(1)}, u32[]{:S(2)}, u32[]{:S(2)}) collective-permute-start(bf16[2,32,512]{2,1,0:T(8,128)(2,1)S(1)} %raw_factors.1), channel_id=1, source_target_pairs={{0,64},{1,65},{2,66},{3,67},{4,68},{5,69},{6,70},{7,71},{8,9},{9,8... | collective-permute-start | bytes 196616 | tf_op jit(solution)/shard_map/ppermute | solution.py:236
  54.1 0.6 turn.1
  54.7 0.8 %collective-permute-done.4 = bf16[2,32,512]{2,1,0:T(8,128)(2,1)S(1)} collective-permute-done((bf16[2,32,512]{2,1,0:T(8,128)(2,1)S(1)}, bf16[2,32,512]{2,1,0:T(8,128)(2,1)S(1)}, u32[]{:S(2)}, u32[]{:S(2)}) %collective-permute-start.4) | collective-permute-done | bytes 65568 | tf_op jit(solution)/shard_map/ppermute | solution.py:236
  55.5 0.0 collective-permute-done.3
  55.5 0.9 %collective-permute-done.2 = bf16[2,32,512]{2,1,0:T(8,128)(2,1)S(1)} collective-permute-done((bf16[2,32,512]{2,1,0:T(8,128)(2,1)S(1)}, bf16[2,32,512]{2,1,0:T(8,128)(2,1)S(1)}, u32[]{:S(2)}, u32[]{:S(2)}) %collective-permute-start.2) | collective-permute-done | bytes 65568 | tf_op jit(solution)/shard_map/ppermute | solution.py:236
  56.5 0.5 collective-permute-start.5
  56.9 2.8 %solve.1.refs_1_ = f32[32,32]{1,0:T(8,128)S(1)} custom-call(f32[32,32]{1,0:T(8,128)S(1)} %get-tuple-element.26.gram), custom_call_target="tpu_custom_call" | custom-call | flops 8388608 | bytes 4194304 | tf_op jit(solution)/shard_map/solve/pallas_call | solution.py:149
  59.7 2.2 %collective-permute-done.5 = bf16[2,32,512]{2,1,0:T(8,128)(2,1)S(1)} collective-permute-done((bf16[2,32,512]{2,1,0:T(8,128)(2,1)S(1)}, bf16[2,32,512]{2,1,0:T(8,128)(2,1)S(1)}, u32[]{:S(2)}, u32[]{:S(2)}) %collective-permute-start.5) | collective-permute-done | bytes 65568 | tf_op jit(solution)/shard_map/ppermute | solution.py:236
  61.9 2.1 %collective-permute-start.6 = (f32[32,512]{1,0:T(8,128)S(1)}, f32[32,512]{1,0:T(8,128)S(1)}, u32[]{:S(2)}, u32[]{:S(2)}) collective-permute-start(f32[32,512]{1,0:T(8,128)S(1)} %get-tuple-element.33), channel_id=1, source_target_pairs={{0,8},{8,0},{16,24},{24,16},{32,40},{40,32},{48,56},{56,48},{64,72... | collective-permute-start | bytes 196616 | tf_op jit(solution)/shard_map/ppermute | solution.py:225
  64.0 2.7 %finish_leading.1 = (bf16[1,4096,512]{2,1,0:T(8,128)(2,1)}, f32[32,512]{1,0:T(8,128)}) custom-call(f32[32,512]{1,0:T(8,128)S(1)} %get-tuple-element.32.refs_0_, f32[32,32]{1,0:T(8,128)S(1)} %solve.1.refs_1_, bf16[4096,64]{1,0:T(8,128)(2,1)S(1)} %get-tuple-element.29.refs_2_, bf16[4096,512]{1,0:T(8,128)(2,1)S(1)} %get-tuple-element.20.own.refs_3_), custom_call_target="tpu_custom_call" | custom-call | flops 268435456 | bytes 8388608 | tf_op jit(solution)/shard_map/finish_leading/pallas_call | solution.py:197
  66.7 0.0 collective-permute-done.6.refs_0_
  66.7 0.1 finish_other.1
  (7 shorter events, 0.2 us)
Async XLA Ops:
  4.4 4.5 %collective-permute-start = (bf16[32,32,128]{2,1,0:T(8,128)(2,1)S(1)}, bf16[32,32,128]{2,1,0:T(8,128)(2,1)S(1)}, u32[]{:S(2)}, u32[]{:S(2)}) collective-permute-start(bf16[32,32,128]{2,1,0:T(8,128)(2,1)S(1)} %get-tuple-element.17), channel_id=1, source_target_pairs={{0,8},{8,0},{16,24},{24,16},{32,40},{40,32},{48,56},{56,48},{64,72... | collective-permute-start | bytes 786440 | tf_op jit(solution)/shard_map/ppermute | solution.py:225
  8.9 40.0 %collective-permute-start.1 = (bf16[4096,512]{1,0:T(8,128)(2,1)S(1)}, bf16[4096,512]{1,0:T(8,128)(2,1)S(1)}, u32[]{:S(2)}, u32[]{:S(2)}) collective-permute-start(bf16[4096,512]{1,0:T(8,128)(2,1)S(1)} %get-tuple-element.20.own.refs_3_), channel_id=1, source_target_pairs={{0,8},{8,0},{16,24},{24,16},{32,40},{40,32},{48,56},{56,48},{64,72... | collective-permute-start | bytes 12582920 | tf_op jit(solution)/shard_map/ppermute | solution.py:225
  50.5 5.0 %collective-permute-start.4 = (bf16[2,32,512]{2,1,0:T(8,128)(2,1)S(1)}, bf16[2,32,512]{2,1,0:T(8,128)(2,1)S(1)}, u32[]{:S(2)}, u32[]{:S(2)}) collective-permute-start(bf16[2,32,512]{2,1,0:T(8,128)(2,1)S(1)} %raw_factors.1), channel_id=1, source_target_pairs={{0,64},{1,65},{2,66},{3,67},{4,68},{5,69},{6,70},{7,71},{8,11},{9,... | collective-permute-start | bytes 196616 | tf_op jit(solution)/shard_map/ppermute | solution.py:236
  50.6 4.9 %collective-permute-start.3 = (bf16[2,32,512]{2,1,0:T(8,128)(2,1)S(1)}, bf16[2,32,512]{2,1,0:T(8,128)(2,1)S(1)}, u32[]{:S(2)}, u32[]{:S(2)}) collective-permute-start(bf16[2,32,512]{2,1,0:T(8,128)(2,1)S(1)} %raw_factors.1), channel_id=1, source_target_pairs={{0,64},{1,65},{2,66},{3,67},{4,68},{5,69},{6,70},{7,71},{8,10},{9,... | collective-permute-start | bytes 196616 | tf_op jit(solution)/shard_map/ppermute | solution.py:236
  51.9 4.5 %collective-permute-start.2 = (bf16[2,32,512]{2,1,0:T(8,128)(2,1)S(1)}, bf16[2,32,512]{2,1,0:T(8,128)(2,1)S(1)}, u32[]{:S(2)}, u32[]{:S(2)}) collective-permute-start(bf16[2,32,512]{2,1,0:T(8,128)(2,1)S(1)} %raw_factors.1), channel_id=1, source_target_pairs={{0,64},{1,65},{2,66},{3,67},{4,68},{5,69},{6,70},{7,71},{8,9},{9,8... | collective-permute-start | bytes 196616 | tf_op jit(solution)/shard_map/ppermute | solution.py:236
  56.5 5.4 %collective-permute-start.5 = (bf16[2,32,512]{2,1,0:T(8,128)(2,1)S(1)}, bf16[2,32,512]{2,1,0:T(8,128)(2,1)S(1)}, u32[]{:S(2)}, u32[]{:S(2)}) collective-permute-start(bf16[2,32,512]{2,1,0:T(8,128)(2,1)S(1)} %add_convert_fusion.1), channel_id=1, source_target_pairs={{0,64},{1,65},{2,66},{3,67},{4,68},{5,69},{6,70},{7,71},{8,14},{9,... | collective-permute-start | bytes 196616 | tf_op jit(solution)/shard_map/ppermute | solution.py:236
  61.9 4.8 %collective-permute-start.6 = (f32[32,512]{1,0:T(8,128)S(1)}, f32[32,512]{1,0:T(8,128)S(1)}, u32[]{:S(2)}, u32[]{:S(2)}) collective-permute-start(f32[32,512]{1,0:T(8,128)S(1)} %get-tuple-element.33), channel_id=1, source_target_pairs={{0,8},{8,0},{16,24},{24,16},{32,40},{40,32},{48,56},{56,48},{64,72... | collective-permute-start | bytes 196616 | tf_op jit(solution)/shard_map/ppermute | solution.py:225

commit v11 on v5

--- a/solution.py
+++ b/solution.py
@@ -95,17 +95,34 @@
     )(in_vmem(p_sum), in_vmem(merged))
 
 
-def solve_kernel(p_sum, inverse, turned):
+def turn_kernel(p_sum, gram, turned):
     blocks, rank, lanes = p_sum.shape
     wide = side_by_side(p_sum)
-    gram = lax.dot_general(wide, wide, (((1,), (1,)), ((), ())), preferred_element_type=F32)
+    gram[...] = lax.dot_general(wide, wide, (((1,), (1,)), ((), ())), preferred_element_type=F32)
     for block in range(blocks):
-        tall = p_sum[block].astype(F32).T.astype(BF16)
+        tall = wide[:, block * lanes : (block + 1) * lanes].astype(F32).T.astype(BF16)
         turned[pl.ds(block * lanes, lanes), :] = jnp.concatenate([tall, tall], axis=1)
+
+
+def turn(p_sum):
+    blocks, rank, lanes = p_sum.shape
+    return pl.pallas_call(
+        turn_kernel,
+        in_specs=[WHOLE],
+        out_specs=[WHOLE, WHOLE],
+        out_shape=[pltpu.VMEM((rank, rank), F32), pltpu.VMEM((blocks * lanes, 2 * rank), BF16)],
+        compiler_params=params(),
+        cost_estimate=pl.CostEstimate(flops=8 * rank * rank * blocks * lanes, bytes_accessed=2 << 20, transcendentals=0),
+        name="turn",
+    )(in_vmem(p_sum))
+
+
+def solve_kernel(gram, inverse):
+    rank = gram.shape[0]
     row = lax.broadcasted_iota(jnp.int32, (rank, rank), 0)
     col = lax.broadcasted_iota(jnp.int32, (rank, rank), 1)
     one = (row == col).astype(F32)
-    table = jnp.concatenate([gram, one], axis=1)
+    table = jnp.concatenate([gram[...], one], axis=1)
     below = lax.broadcasted_iota(jnp.int32, (rank, 1), 0)
     for k in range(rank):
         pivot = table[k : k + 1, :]
@@ -115,30 +132,30 @@
     inverse[...] = table[:, rank:] * lax.rsqrt(diagonal)
 
 
-def solve(p_sum):
-    blocks, rank, lanes = p_sum.shape
+def solve(gram):
     return pl.pallas_call(
         solve_kernel,
         in_specs=[WHOLE],
-        out_specs=[WHOLE, WHOLE],
-        out_shape=[pltpu.VMEM((rank, rank), F32), pltpu.VMEM((blocks * lanes, 2 * rank), BF16)],
-        compiler_params=params(),
-        cost_estimate=pl.CostEstimate(flops=16 * rank * rank * blocks * lanes, bytes_accessed=4 << 20, transcendentals=0),
+        out_specs=WHOLE,
+        out_shape=pltpu.VMEM(gram.shape, F32),
+        compiler_params=params(),
+        cost_estimate=pl.CostEstimate(flops=8 << 20, bytes_accessed=4 << 20, transcendentals=0),
         name="solve",
-    )(in_vmem(p_sum))
-
-
-def finish_kernel(replicas, mine, theirs, inverse, turned, merged, new_error, q_factor, halves, result, done):
+    )(in_vmem(gram))
+
+
+def finish_kernel(replicas, mine, theirs, inverse, turned, merged, new_error, q_factor, halves, result, factor_out, done):
     raw = mine[...].astype(F32) + theirs[...].astype(F32)
     factor = jnp.dot(inverse[...], raw, precision=HIGHEST, preferred_element_type=F32) * (1.0 / replicas)
-    q_factor[...] = factor
+    factor_out[...] = factor
+    copies = [pltpu.make_async_copy(factor_out, q_factor, done.at[merged.shape[0] // STEP])]
+    copies[0].start()
     rounded = factor.astype(BF16).astype(F32)
     solved = lax.dot_general(
         inverse[...], rounded, (((0,), (0,)), ((), ())), precision=HIGHEST, preferred_element_type=F32
     )
     high = solved.astype(BF16)
     halves[...] = jnp.concatenate([high, (solved - high.astype(F32)).astype(BF16)], axis=0)
-    copies = []
     for chunk in range(merged.shape[0] // STEP):
         here = rows_of(chunk)
         rebuilt = jnp.dot(turned[here, :], halves[...], preferred_element_type=F32)
@@ -155,20 +172,18 @@
     return pl.pallas_call(
         lambda *refs: finish_kernel(replicas, *refs),
         in_specs=[WHOLE] * 5,
-        out_specs=[ANYWHERE, WHOLE],
-        out_shape=[
-            pltpu.HBM((1, rows, columns), BF16),
-            jax.ShapeDtypeStruct((rank, columns), F32),
-        ],
+        out_specs=[ANYWHERE] * 2,
+        out_shape=[pltpu.HBM((1, rows, columns), BF16), pltpu.HBM((rank, columns), F32)],
         scratch_shapes=[
             pltpu.VMEM((2 * rank, columns), BF16),
             pltpu.VMEM((rows, columns), BF16),
-            pltpu.SemaphoreType.DMA((rows // STEP,)),
+            pltpu.VMEM((rank, columns), F32),
+            pltpu.SemaphoreType.DMA((rows // STEP + 1,)),
         ],
         compiler_params=params(),
         cost_estimate=pl.CostEstimate(flops=4 * rank * rows * columns, bytes_accessed=4 * rows * columns, transcendentals=0),
         name="finish",
-    )(in_vmem(mine), in_vmem(theirs), in_vmem(inverse), in_vmem(turned), in_vmem(merged))
+    )(*(in_vmem(x) for x in (mine, theirs, inverse, turned, merged)))
 
 
 def exchange(blocks, axis):
@@ -197,9 +212,12 @@
     own = total(share(own.astype(BF16), "rep"))
     p_sum = share(own.astype(BF16), "col")
     raw = raw_factor(p_sum, merged)
-    inverse, turned = solve(p_sum)
-    raw = total([raw] + [swap(raw, "rep", mask) for mask in (1, 2, 3)]).astype(BF16)
-    return tuple(finish(raw, swap(raw, "rep", 6), inverse, turned, merged, replicas))
+    gram, turned = turn(p_sum)
+    near = [swap(raw, "rep", mask) for mask in (1, 2, 3)]
+    raw, gram, *near = lax.optimization_barrier((raw, gram, *near))
+    raw = total([raw, *near]).astype(BF16)
+    far, inverse = lax.optimization_barrier((swap(raw, "rep", 6), solve(gram)))
+    return tuple(finish(raw, far, inverse, turned, merged, replicas))
 
 
 def solution(mesh):

time: 66.6 us -> 66 us (level)
    pallas_call x1 -> x2, Pallas kernels: 3.16 us -> 3.4 us  [the longest x1 2.76 us: solve(): pl.pallas_call(solve_kernel, in_specs=[WHOLE], out_specs=WHOLE, out_shape...]
where the time goes in v11:
time: 66 us; the launch traced here: 65.1 us
  blocking collectives  46.5 us (70%)
  Pallas kernels  10.7 us (16%)
  starting transfers between devices  4.47 us (7%)
  waiting for transfers between devices  2.57 us (4%)
  between operations  0.67 us (1%)
    all_to_all x3, blocking collectives, exchange(): return lax.all_to_all(blocks, axis, 0, 0, tiled=True)  46.5 us
    ppermute x4, starting transfers between devices, swap(): lax.ppermute(block, axis, [(i, i ^ mask) for i in range(lax.axis_size(axi...  4.47 us
    pallas_call x1, Pallas kernels, merge(): pl.pallas_call(merge_kernel, in_specs=[ANYWHERE] * 3, out_specs=[WHOLE, W...  3.81 us
    pallas_call x1, Pallas kernels, solve(): pl.pallas_call(solve_kernel, in_specs=[WHOLE], out_specs=WHOLE, out_shape...  2.76 us
    pallas_call x1, Pallas kernels, finish(): pl.pallas_call(lambda *refs: finish_kernel(replicas, *refs), in_specs=[WH...  2.73 us
    ppermute x4, waiting for transfers between devices, swap(): lax.ppermute(block, axis, [(i, i ^ mask) for i in range(lax.axis_size(axi...  2.57 us
  transfers between devices with their start and end apart: 4, of which 3 were waited for; matrix products, arithmetic and copies ran while one was open for 0% of the time, Pallas kernels for 5%

profile of v11, /device:TPU:1, one launch (start us, length us, event | category | flops | bytes accessed | tf_op | source)
XLA Modules:
  0.0 65.1 jit_solution(16952125657092833294)
XLA Ops:
  0.6 3.8 %merge.1 = (bf16[4096,512]{1,0:T(8,128)(2,1)S(1)}, bf16[32,32,128]{2,1,0:T(8,128)(2,1)S(1)}) custom-call(bf16[1,4096,512]{2,1,0:T(8,128)(2,1)} %gradient.1, bf16[1,4096,512]{2,1,0:T(8,128)(2,1)} %error.1, bf16[32,512]{1,0:T(8,128)(2,1)} %warm.1), custom_call_target="tpu_custom_call" | custom-call | flops 134217728 | bytes 8388608 | tf_op jit(solution)/shard_map/merge/pallas_call | solution.py:56
  4.4 17.4 %all_to_all.15 = bf16[32,32,128]{2,1,0:T(8,128)(2,1)S(1)} all-to-all(bf16[32,32,128]{2,1,0:T(8,128)(2,1)S(1)} %get-tuple-element.13), channel_id=1, replica_groups=mesh['col'=32,'rep'=8] {'col'}, dimensions={0} | all-to-all | bytes 524288 | tf_op jit(solution)/shard_map/all_to_all | solution.py:190
  21.9 15.2 %all_to_all.16 = bf16[8,32,128]{2,1,0:T(8,128)(2,1)S(1)} all-to-all(bf16[8,32,128]{2,1,0:T(8,128)(2,1)S(1)} %broadcast_in_dim.17), channel_id=1, replica_groups=mesh['col'=32,'rep'=8] {'rep'}, dimensions={0} | all-to-all | bytes 131072 | tf_op jit(solution)/shard_map/all_to_all | solution.py:190
  37.1 13.9 %all_to_all.17.p_sum = bf16[32,32,128]{2,1,0:T(8,128)(2,1)S(1)} all-to-all(bf16[32,32,128]{2,1,0:T(8,128)(2,1)S(1)} %broadcast_in_dim.19), channel_id=1, replica_groups=mesh['col'=32,'rep'=8] {'col'}, dimensions={0} | all-to-all | bytes 524288 | tf_op jit(solution)/shard_map/all_to_all | solution.py:190
  51.0 0.8 %raw_factor.1 = bf16[32,512]{1,0:T(8,128)(2,1)S(1)} custom-call(bf16[32,32,128]{2,1,0:T(8,128)(2,1)S(1)} %all_to_all.17.p_sum, bf16[4096,512]{1,0:T(8,128)(2,1)S(1)} %get-tuple-element.14.merged.refs_4_), custom_call_target="tpu_custom_call" | custom-call | flops 134217728 | bytes 4194304 | tf_op jit(solution)/shard_map/raw_factor/pallas_call | solution.py:87
  51.9 0.2 collective-permute-start.2
  52.0 1.3 %collective-permute-start.1 = (bf16[32,512]{1,0:T(8,128)(2,1)S(1)}, bf16[32,512]{1,0:T(8,128)(2,1)S(1)}, u32[]{:S(2)}, u32[]{:S(2)}) collective-permute-start(bf16[32,512]{1,0:T(8,128)(2,1)S(1)} %raw_factor.1), channel_id=1, source_target_pairs={{0,2},{1,3},{2,0},{3,1},{4,6},{5,7},{6,4},{7,5},{8,10},{9,11},{10,... | collective-permute-start | bytes 98312 | tf_op jit(solution)/shard_map/ppermute | solution.py:205
  53.3 2.1 %collective-permute-start = (bf16[32,512]{1,0:T(8,128)(2,1)S(1)}, bf16[32,512]{1,0:T(8,128)(2,1)S(1)}, u32[]{:S(2)}, u32[]{:S(2)}) collective-permute-start(bf16[32,512]{1,0:T(8,128)(2,1)S(1)} %raw_factor.1), channel_id=1, source_target_pairs={{0,1},{1,0},{2,3},{3,2},{4,5},{5,4},{6,7},{7,6},{8,9},{9,8},{10,11... | collective-permute-start | bytes 98312 | tf_op jit(solution)/shard_map/ppermute | solution.py:205
  55.4 0.6 turn.1
  56.1 0.4 collective-permute-done.2
  56.5 0.0 collective-permute-done.1
  56.5 0.8 %collective-permute-done = bf16[32,512]{1,0:T(8,128)(2,1)S(1)} collective-permute-done((bf16[32,512]{1,0:T(8,128)(2,1)S(1)}, bf16[32,512]{1,0:T(8,128)(2,1)S(1)}, u32[]{:S(2)}, u32[]{:S(2)}) %collective-permute-start) | collective-permute-done | bytes 32800 | tf_op jit(solution)/shard_map/ppermute | solution.py:205
  57.3 0.9 %collective-permute-start.3 = (bf16[32,512]{1,0:T(8,128)(2,1)S(1)}, bf16[32,512]{1,0:T(8,128)(2,1)S(1)}, u32[]{:S(2)}, u32[]{:S(2)}) collective-permute-start(bf16[32,512]{1,0:T(8,128)(2,1)S(1)} %add_convert_fusion.refs_0_), channel_id=1, source_target_pairs={{0,6},{1,7},{2,4},{3,5},{4,2},{5,3},{6,0},{7,1},{8,14},{9,15},{10,... | collective-permute-start | bytes 98312 | tf_op jit(solution)/shard_map/ppermute | solution.py:205
  58.2 2.8 %solve.1.refs_2_ = f32[32,32]{1,0:T(8,128)S(1)} custom-call(f32[32,32]{1,0:T(8,128)S(1)} %get-tuple-element.20.gram), custom_call_target="tpu_custom_call" | custom-call | flops 8388608 | bytes 4194304 | tf_op jit(solution)/shard_map/solve/pallas_call | solution.py:136
  60.9 1.4 %collective-permute-done.3.refs_1_ = bf16[32,512]{1,0:T(8,128)(2,1)S(1)} collective-permute-done((bf16[32,512]{1,0:T(8,128)(2,1)S(1)}, bf16[32,512]{1,0:T(8,128)(2,1)S(1)}, u32[]{:S(2)}, u32[]{:S(2)}) %collective-permute-start.3) | collective-permute-done | bytes 32800 | tf_op jit(solution)/shard_map/ppermute | solution.py:205
  62.3 2.7 %finish.1 = (bf16[1,4096,512]{2,1,0:T(8,128)(2,1)}, f32[32,512]{1,0:T(8,128)}) custom-call(bf16[32,512]{1,0:T(8,128)(2,1)S(1)} %add_convert_fusion.refs_0_, bf16[32,512]{1,0:T(8,128)(2,1)S(1)} %collective-permute-done.3.refs_1_, f32[32,32]{1,0:T(8,128)S(1)} %solve.1.refs_2_, bf16[4096,64]{1,0:T(8,128)(2,1)S(1)} %get-tuple-element.23.refs_3_, ...), custom_call_target="tpu_custom_call" | custom-call | flops 268435456 | bytes 8388608 | tf_op jit(solution)/shard_map/finish/pallas_call | solution.py:172
  (5 shorter events, 0.1 us)
Async XLA Ops:
  51.9 4.6 %collective-permute-start.2 = (bf16[32,512]{1,0:T(8,128)(2,1)S(1)}, bf16[32,512]{1,0:T(8,128)(2,1)S(1)}, u32[]{:S(2)}, u32[]{:S(2)}) collective-permute-start(bf16[32,512]{1,0:T(8,128)(2,1)S(1)} %raw_factor.1), channel_id=1, source_target_pairs={{0,3},{1,2},{2,1},{3,0},{4,7},{5,6},{6,5},{7,4},{8,11},{9,10},{10,... | collective-permute-start | bytes 98312 | tf_op jit(solution)/shard_map/ppermute | solution.py:205
  52.0 4.5 %collective-permute-start.1 = (bf16[32,512]{1,0:T(8,128)(2,1)S(1)}, bf16[32,512]{1,0:T(8,128)(2,1)S(1)}, u32[]{:S(2)}, u32[]{:S(2)}) collective-permute-start(bf16[32,512]{1,0:T(8,128)(2,1)S(1)} %raw_factor.1), channel_id=1, source_target_pairs={{0,2},{1,3},{2,0},{3,1},{4,6},{5,7},{6,4},{7,5},{8,10},{9,11},{10,... | collective-permute-start | bytes 98312 | tf_op jit(solution)/shard_map/ppermute | solution.py:205
  53.3 3.9 %collective-permute-start = (bf16[32,512]{1,0:T(8,128)(2,1)S(1)}, bf16[32,512]{1,0:T(8,128)(2,1)S(1)}, u32[]{:S(2)}, u32[]{:S(2)}) collective-permute-start(bf16[32,512]{1,0:T(8,128)(2,1)S(1)} %raw_factor.1), channel_id=1, source_target_pairs={{0,1},{1,0},{2,3},{3,2},{4,5},{5,4},{6,7},{7,6},{8,9},{9,8},{10,11... | collective-permute-start | bytes 98312 | tf_op jit(solution)/shard_map/ppermute | solution.py:205
  57.3 5.1 %collective-permute-start.3 = (bf16[32,512]{1,0:T(8,128)(2,1)S(1)}, bf16[32,512]{1,0:T(8,128)(2,1)S(1)}, u32[]{:S(2)}, u32[]{:S(2)}) collective-permute-start(bf16[32,512]{1,0:T(8,128)(2,1)S(1)} %add_convert_fusion.refs_0_), channel_id=1, source_target_pairs={{0,6},{1,7},{2,4},{3,5},{4,2},{5,3},{6,0},{7,1},{8,14},{9,15},{10,... | collective-permute-start | bytes 98312 | tf_op jit(solution)/shard_map/ppermute | solution.py:205

commit v12 on v11

--- a/solution.py
+++ b/solution.py
@@ -7,6 +7,7 @@
 
 BF16, F32 = jnp.bfloat16, jnp.float32
 HIGHEST = lax.Precision.HIGHEST
+LATE = {"col": 21, "rep": 5}
 LANES = 128
 STEP = 512
 WHOLE = pl.BlockSpec(memory_space=pltpu.VMEM)
@@ -187,7 +188,9 @@
 
 
 def exchange(blocks, axis):
-    return lax.all_to_all(blocks, axis, 0, 0, tiled=True)
+    places = list(range(lax.axis_size(axis)))
+    first = LATE[axis]
+    return lax.all_to_all(blocks, axis, 0, 0, axis_index_groups=[places[first:] + places[:first]], tiled=True)
 
 
 def share(block, axis):

time: 66 us -> 59.4 us (0.900)
  blocking collectives: 46.5 us -> 38.4 us
  starting transfers between devices: 4.47 us -> 6.43 us
    all_to_all x3, blocking collectives: 46.5 us -> 38.4 us  [exchange(): lax.all_to_all(blocks, axis, 0, 0, axis_index_groups=[places[first:] + pl...]
    ppermute x4, starting transfers between devices: 4.47 us -> 6.43 us  [swap(): lax.ppermute(block, axis, [(i, i ^ mask) for i in range(lax.axis_size(axi...]
  transfers between devices with their start and end apart: 4 -> 4, of which waited for: 3 -> 2; matrix products, arithmetic and copies ran while one was open for 0% -> 0% of each run, Pallas kernels for 5% -> 6%
where the time goes in v12:
time: 59.4 us; the launch traced here: 58.3 us
  blocking collectives  38.4 us (65%)
  Pallas kernels  10.8 us (18%)
  starting transfers between devices  6.43 us (11%)
  waiting for transfers between devices  1.97 us (3%)
  between operations  0.67 us (1%)
    all_to_all x3, blocking collectives, exchange(): lax.all_to_all(blocks, axis, 0, 0, axis_index_groups=[places[first:] + pl...  38.4 us
    ppermute x4, starting transfers between devices, swap(): lax.ppermute(block, axis, [(i, i ^ mask) for i in range(lax.axis_size(axi...  6.43 us
    pallas_call x1, Pallas kernels, merge(): pl.pallas_call(merge_kernel, in_specs=[ANYWHERE] * 3, out_specs=[WHOLE, W...  3.81 us
    pallas_call x1, Pallas kernels, solve(): pl.pallas_call(solve_kernel, in_specs=[WHOLE], out_specs=WHOLE, out_shape...  2.76 us
    pallas_call x1, Pallas kernels, finish(): pl.pallas_call(lambda *refs: finish_kernel(replicas, *refs), in_specs=[WH...  2.74 us
    ppermute x4, waiting for transfers between devices, swap(): lax.ppermute(block, axis, [(i, i ^ mask) for i in range(lax.axis_size(axi...  1.97 us
  transfers between devices with their start and end apart: 4, of which 2 were waited for; matrix products, arithmetic and copies ran while one was open for 0% of the time, Pallas kernels for 6%

profile of v12, /device:TPU:1, one launch (start us, length us, event | category | flops | bytes accessed | tf_op | source)
XLA Modules:
  0.0 58.3 jit_solution(13486049684256301985)
XLA Ops:
  0.6 3.8 %merge.1 = (bf16[4096,512]{1,0:T(8,128)(2,1)S(1)}, bf16[32,32,128]{2,1,0:T(8,128)(2,1)S(1)}) custom-call(bf16[1,4096,512]{2,1,0:T(8,128)(2,1)} %gradient.1, bf16[1,4096,512]{2,1,0:T(8,128)(2,1)} %error.1, bf16[32,512]{1,0:T(8,128)(2,1)} %warm.1), custom_call_target="tpu_custom_call" | custom-call | flops 134217728 | bytes 8388608 | tf_op jit(solution)/shard_map/merge/pallas_call | solution.py:57
  4.4 13.8 %all_to_all.15 = bf16[32,32,128]{2,1,0:T(8,128)(2,1)S(1)} all-to-all(bf16[32,32,128]{2,1,0:T(8,128)(2,1)S(1)} %get-tuple-element.13), channel_id=1, replica_groups={{168,176,184,192,200,208,216,224,232,240,248,0,8,16,24,32,40,48,56,64,7..., dimensions={0} | all-to-all | bytes 524288 | tf_op jit(solution)/shard_map/all_to_all | solution.py:193
  18.3 11.6 %all_to_all.16 = bf16[8,32,128]{2,1,0:T(8,128)(2,1)S(1)} all-to-all(bf16[8,32,128]{2,1,0:T(8,128)(2,1)S(1)} %broadcast_in_dim.17), channel_id=1, replica_groups={{5,6,7,0,1,2,3,4},{13,14,15,8,9,10,11,12},{21,22,23,16,17,18,19,20},{29..., dimensions={0} | all-to-all | bytes 131072 | tf_op jit(solution)/shard_map/all_to_all | solution.py:193
  30.0 12.9 %all_to_all.17.p_sum = bf16[32,32,128]{2,1,0:T(8,128)(2,1)S(1)} all-to-all(bf16[32,32,128]{2,1,0:T(8,128)(2,1)S(1)} %broadcast_in_dim.19), channel_id=1, replica_groups={{168,176,184,192,200,208,216,224,232,240,248,0,8,16,24,32,40,48,56,64,7..., dimensions={0} | all-to-all | bytes 524288 | tf_op jit(solution)/shard_map/all_to_all | solution.py:193
  43.0 0.8 %raw_factor.1 = bf16[32,512]{1,0:T(8,128)(2,1)S(1)} custom-call(bf16[32,32,128]{2,1,0:T(8,128)(2,1)S(1)} %all_to_all.17.p_sum, bf16[4096,512]{1,0:T(8,128)(2,1)S(1)} %get-tuple-element.14.merged.refs_4_), custom_call_target="tpu_custom_call" | custom-call | flops 134217728 | bytes 4194304 | tf_op jit(solution)/shard_map/raw_factor/pallas_call | solution.py:88
  43.8 2.1 %collective-permute-start.2 = (bf16[32,512]{1,0:T(8,128)(2,1)S(1)}, bf16[32,512]{1,0:T(8,128)(2,1)S(1)}, u32[]{:S(2)}, u32[]{:S(2)}) collective-permute-start(bf16[32,512]{1,0:T(8,128)(2,1)S(1)} %raw_factor.1), channel_id=1, source_target_pairs={{0,3},{1,2},{2,1},{3,0},{4,7},{5,6},{6,5},{7,4},{8,11},{9,10},{10,... | collective-permute-start | bytes 98312 | tf_op jit(solution)/shard_map/ppermute | solution.py:208
  45.9 0.0 collective-permute-start.1
  45.9 1.5 %collective-permute-start = (bf16[32,512]{1,0:T(8,128)(2,1)S(1)}, bf16[32,512]{1,0:T(8,128)(2,1)S(1)}, u32[]{:S(2)}, u32[]{:S(2)}) collective-permute-start(bf16[32,512]{1,0:T(8,128)(2,1)S(1)} %raw_factor.1), channel_id=1, source_target_pairs={{0,1},{1,0},{2,3},{3,2},{4,5},{5,4},{6,7},{7,6},{8,9},{9,8},{10,11... | collective-permute-start | bytes 98312 | tf_op jit(solution)/shard_map/ppermute | solution.py:208
  47.3 0.6 %turn.1 = (f32[32,32]{1,0:T(8,128)S(1)}, bf16[4096,64]{1,0:T(8,128)(2,1)S(1)}) custom-call(bf16[32,32,128]{2,1,0:T(8,128)(2,1)S(1)} %all_to_all.17.p_sum), custom_call_target="tpu_custom_call" | custom-call | flops 33554432 | bytes 2097152 | tf_op jit(solution)/shard_map/turn/pallas_call | solution.py:110
  48.0 0.4 collective-permute-done.2
  48.4 1.6 %collective-permute-done.1 = bf16[32,512]{1,0:T(8,128)(2,1)S(1)} collective-permute-done((bf16[32,512]{1,0:T(8,128)(2,1)S(1)}, bf16[32,512]{1,0:T(8,128)(2,1)S(1)}, u32[]{:S(2)}, u32[]{:S(2)}) %collective-permute-start.1) | collective-permute-done | bytes 32800 | tf_op jit(solution)/shard_map/ppermute | solution.py:208
  49.9 0.0 collective-permute-done
  50.0 2.9 %collective-permute-start.3 = (bf16[32,512]{1,0:T(8,128)(2,1)S(1)}, bf16[32,512]{1,0:T(8,128)(2,1)S(1)}, u32[]{:S(2)}, u32[]{:S(2)}) collective-permute-start(bf16[32,512]{1,0:T(8,128)(2,1)S(1)} %add_convert_fusion.refs_0_), channel_id=1, source_target_pairs={{0,6},{1,7},{2,4},{3,5},{4,2},{5,3},{6,0},{7,1},{8,14},{9,15},{10,... | collective-permute-start | bytes 98312 | tf_op jit(solution)/shard_map/ppermute | solution.py:208
  52.8 2.8 %solve.1.refs_2_ = f32[32,32]{1,0:T(8,128)S(1)} custom-call(f32[32,32]{1,0:T(8,128)S(1)} %get-tuple-element.20.gram), custom_call_target="tpu_custom_call" | custom-call | flops 8388608 | bytes 4194304 | tf_op jit(solution)/shard_map/solve/pallas_call | solution.py:137
  55.6 0.0 collective-permute-done.3.refs_1_
  55.6 2.7 %finish.1 = (bf16[1,4096,512]{2,1,0:T(8,128)(2,1)}, f32[32,512]{1,0:T(8,128)}) custom-call(bf16[32,512]{1,0:T(8,128)(2,1)S(1)} %add_convert_fusion.refs_0_, bf16[32,512]{1,0:T(8,128)(2,1)S(1)} %collective-permute-done.3.refs_1_, f32[32,32]{1,0:T(8,128)S(1)} %solve.1.refs_2_, bf16[4096,64]{1,0:T(8,128)(2,1)S(1)} %get-tuple-element.23.refs_3_, ...), custom_call_target="tpu_custom_call" | custom-call | flops 268435456 | bytes 8388608 | tf_op jit(solution)/shard_map/finish/pallas_call | solution.py:173
  (5 shorter events, 0.1 us)
Async XLA Ops:
  43.8 4.6 %collective-permute-start.2 = (bf16[32,512]{1,0:T(8,128)(2,1)S(1)}, bf16[32,512]{1,0:T(8,128)(2,1)S(1)}, u32[]{:S(2)}, u32[]{:S(2)}) collective-permute-start(bf16[32,512]{1,0:T(8,128)(2,1)S(1)} %raw_factor.1), channel_id=1, source_target_pairs={{0,3},{1,2},{2,1},{3,0},{4,7},{5,6},{6,5},{7,4},{8,11},{9,10},{10,... | collective-permute-start | bytes 98312 | tf_op jit(solution)/shard_map/ppermute | solution.py:208
  45.9 4.1 %collective-permute-start.1 = (bf16[32,512]{1,0:T(8,128)(2,1)S(1)}, bf16[32,512]{1,0:T(8,128)(2,1)S(1)}, u32[]{:S(2)}, u32[]{:S(2)}) collective-permute-start(bf16[32,512]{1,0:T(8,128)(2,1)S(1)} %raw_factor.1), channel_id=1, source_target_pairs={{0,2},{1,3},{2,0},{3,1},{4,6},{5,7},{6,4},{7,5},{8,10},{9,11},{10,... | collective-permute-start | bytes 98312 | tf_op jit(solution)/shard_map/ppermute | solution.py:208
  45.9 4.1 %collective-permute-start = (bf16[32,512]{1,0:T(8,128)(2,1)S(1)}, bf16[32,512]{1,0:T(8,128)(2,1)S(1)}, u32[]{:S(2)}, u32[]{:S(2)}) collective-permute-start(bf16[32,512]{1,0:T(8,128)(2,1)S(1)} %raw_factor.1), channel_id=1, source_target_pairs={{0,1},{1,0},{2,3},{3,2},{4,5},{5,4},{6,7},{7,6},{8,9},{9,8},{10,11... | collective-permute-start | bytes 98312 | tf_op jit(solution)/shard_map/ppermute | solution.py:208
  50.0 5.6 %collective-permute-start.3 = (bf16[32,512]{1,0:T(8,128)(2,1)S(1)}, bf16[32,512]{1,0:T(8,128)(2,1)S(1)}, u32[]{:S(2)}, u32[]{:S(2)}) collective-permute-start(bf16[32,512]{1,0:T(8,128)(2,1)S(1)} %add_convert_fusion.refs_0_), channel_id=1, source_target_pairs={{0,6},{1,7},{2,4},{3,5},{4,2},{5,3},{6,0},{7,1},{8,14},{9,15},{10,... | collective-permute-start | bytes 98312 | tf_op jit(solution)/shard_map/ppermute | solution.py:208

commit v13 on v11

--- a/solution.py
+++ b/solution.py
@@ -1,3 +1,5 @@
+import math
+
 import jax
 import jax.numpy as jnp
 from jax import lax
@@ -7,6 +9,8 @@
 
 BF16, F32 = jnp.bfloat16, jnp.float32
 HIGHEST = lax.Precision.HIGHEST
+CORES = 2
+LATE = {"col": 21, "rep": 5}
 LANES = 128
 STEP = 512
 WHOLE = pl.BlockSpec(memory_space=pltpu.VMEM)
@@ -186,8 +190,19 @@
     )(*(in_vmem(x) for x in (mine, theirs, inverse, turned, merged)))
 
 
+def hops(axis, place):
+    first, size = LATE[axis], lax.axis_size(axis)
+    rings = [(place, first, size)]
+    if axis == "col":
+        along = math.isqrt(size // CORES)
+        rings = [(p // CORES // along, f // CORES // along, along) for p, f, _ in rings]
+        rings.append((place // CORES % along, first // CORES % along, along))
+    return sum(min((p - f) % n, (f - p) % n) for p, f, n in rings)
+
+
 def exchange(blocks, axis):
-    return lax.all_to_all(blocks, axis, 0, 0, tiled=True)
+    places = sorted(range(lax.axis_size(axis)), key=lambda p: (p != LATE[axis], hops(axis, p), -(p % CORES), p))
+    return lax.all_to_all(blocks, axis, 0, 0, axis_index_groups=[places], tiled=True)
 
 
 def share(block, axis):

time: 66 us -> 59.4 us (0.900)
  blocking collectives: 46.5 us -> 38.6 us
  starting transfers between devices: 4.47 us -> 6.12 us
    all_to_all x3, blocking collectives: 46.5 us -> 38.6 us  [exchange(): lax.all_to_all(blocks, axis, 0, 0, axis_index_groups=[places], tiled=True)]
    ppermute x4, starting transfers between devices: 4.47 us -> 6.12 us  [swap(): lax.ppermute(block, axis, [(i, i ^ mask) for i in range(lax.axis_size(axi...]
  transfers between devices with their start and end apart: 4 -> 4, of which waited for: 3 -> 2; matrix products, arithmetic and copies ran while one was open for 0% -> 0% of each run, Pallas kernels for 5% -> 6%
where the time goes in v13:
time: 59.4 us; the launch traced here: 58.4 us
  blocking collectives  38.6 us (65%)
  Pallas kernels  10.8 us (18%)
  starting transfers between devices  6.12 us (10%)
  waiting for transfers between devices  2.08 us (4%)
  between operations  0.67 us (1%)
    all_to_all x3, blocking collectives, exchange(): lax.all_to_all(blocks, axis, 0, 0, axis_index_groups=[places], tiled=True)  38.6 us
    ppermute x4, starting transfers between devices, swap(): lax.ppermute(block, axis, [(i, i ^ mask) for i in range(lax.axis_size(axi...  6.12 us
    pallas_call x1, Pallas kernels, merge(): pl.pallas_call(merge_kernel, in_specs=[ANYWHERE] * 3, out_specs=[WHOLE, W...  3.81 us
    pallas_call x1, Pallas kernels, solve(): pl.pallas_call(solve_kernel, in_specs=[WHOLE], out_specs=WHOLE, out_shape...  2.76 us
    pallas_call x1, Pallas kernels, finish(): pl.pallas_call(lambda *refs: finish_kernel(replicas, *refs), in_specs=[WH...  2.74 us
    ppermute x4, waiting for transfers between devices, swap(): lax.ppermute(block, axis, [(i, i ^ mask) for i in range(lax.axis_size(axi...  2.08 us
  transfers between devices with their start and end apart: 4, of which 2 were waited for; matrix products, arithmetic and copies ran while one was open for 0% of the time, Pallas kernels for 6%

profile of v13, /device:TPU:1, one launch (start us, length us, event | category | flops | bytes accessed | tf_op | source)
XLA Modules:
  0.0 58.4 jit_solution(2033320774858191840)
XLA Ops:
  0.6 3.8 %merge.1 = (bf16[4096,512]{1,0:T(8,128)(2,1)S(1)}, bf16[32,32,128]{2,1,0:T(8,128)(2,1)S(1)}) custom-call(bf16[1,4096,512]{2,1,0:T(8,128)(2,1)} %gradient.1, bf16[1,4096,512]{2,1,0:T(8,128)(2,1)} %error.1, bf16[32,512]{1,0:T(8,128)(2,1)} %warm.1), custom_call_target="tpu_custom_call" | custom-call | flops 134217728 | bytes 8388608 | tf_op jit(solution)/shard_map/merge/pallas_call | solution.py:60
  4.4 13.9 %all_to_all.15 = bf16[32,32,128]{2,1,0:T(8,128)(2,1)S(1)} all-to-all(bf16[32,32,128]{2,1,0:T(8,128)(2,1)S(1)} %get-tuple-element.13), channel_id=1, replica_groups={{168,160,104,152,184,232,96,144,176,224,40,88,120,136,216,248,32,80,112..., dimensions={0} | all-to-all | bytes 524288 | tf_op jit(solution)/shard_map/all_to_all | solution.py:205
  18.4 11.7 %all_to_all.16 = bf16[8,32,128]{2,1,0:T(8,128)(2,1)S(1)} all-to-all(bf16[8,32,128]{2,1,0:T(8,128)(2,1)S(1)} %broadcast_in_dim.17), channel_id=1, replica_groups={{5,4,6,3,7,0,2,1},{13,12,14,11,15,8,10,9},{21,20,22,19,23,16,18,17},{29..., dimensions={0} | all-to-all | bytes 131072 | tf_op jit(solution)/shard_map/all_to_all | solution.py:205
  30.2 13.0 %all_to_all.17.p_sum = bf16[32,32,128]{2,1,0:T(8,128)(2,1)S(1)} all-to-all(bf16[32,32,128]{2,1,0:T(8,128)(2,1)S(1)} %broadcast_in_dim.19), channel_id=1, replica_groups={{168,160,104,152,184,232,96,144,176,224,40,88,120,136,216,248,32,80,112..., dimensions={0} | all-to-all | bytes 524288 | tf_op jit(solution)/shard_map/all_to_all | solution.py:205
  43.2 0.8 %raw_factor.1 = bf16[32,512]{1,0:T(8,128)(2,1)S(1)} custom-call(bf16[32,32,128]{2,1,0:T(8,128)(2,1)S(1)} %all_to_all.17.p_sum, bf16[4096,512]{1,0:T(8,128)(2,1)S(1)} %get-tuple-element.14.merged.refs_4_), custom_call_target="tpu_custom_call" | custom-call | flops 134217728 | bytes 4194304 | tf_op jit(solution)/shard_map/raw_factor/pallas_call | solution.py:91
  44.0 1.9 %collective-permute-start.2 = (bf16[32,512]{1,0:T(8,128)(2,1)S(1)}, bf16[32,512]{1,0:T(8,128)(2,1)S(1)}, u32[]{:S(2)}, u32[]{:S(2)}) collective-permute-start(bf16[32,512]{1,0:T(8,128)(2,1)S(1)} %raw_factor.1), channel_id=1, source_target_pairs={{0,3},{1,2},{2,1},{3,0},{4,7},{5,6},{6,5},{7,4},{8,11},{9,10},{10,... | collective-permute-start | bytes 98312 | tf_op jit(solution)/shard_map/ppermute | solution.py:220
  45.9 0.0 collective-permute-start.1
  46.0 1.6 %collective-permute-start = (bf16[32,512]{1,0:T(8,128)(2,1)S(1)}, bf16[32,512]{1,0:T(8,128)(2,1)S(1)}, u32[]{:S(2)}, u32[]{:S(2)}) collective-permute-start(bf16[32,512]{1,0:T(8,128)(2,1)S(1)} %raw_factor.1), channel_id=1, source_target_pairs={{0,1},{1,0},{2,3},{3,2},{4,5},{5,4},{6,7},{7,6},{8,9},{9,8},{10,11... | collective-permute-start | bytes 98312 | tf_op jit(solution)/shard_map/ppermute | solution.py:220
  47.6 0.6 %turn.1 = (f32[32,32]{1,0:T(8,128)S(1)}, bf16[4096,64]{1,0:T(8,128)(2,1)S(1)}) custom-call(bf16[32,32,128]{2,1,0:T(8,128)(2,1)S(1)} %all_to_all.17.p_sum), custom_call_target="tpu_custom_call" | custom-call | flops 33554432 | bytes 2097152 | tf_op jit(solution)/shard_map/turn/pallas_call | solution.py:113
  48.2 0.4 collective-permute-done.2
  48.6 1.7 %collective-permute-done.1 = bf16[32,512]{1,0:T(8,128)(2,1)S(1)} collective-permute-done((bf16[32,512]{1,0:T(8,128)(2,1)S(1)}, bf16[32,512]{1,0:T(8,128)(2,1)S(1)}, u32[]{:S(2)}, u32[]{:S(2)}) %collective-permute-start.1) | collective-permute-done | bytes 32800 | tf_op jit(solution)/shard_map/ppermute | solution.py:220
  50.3 0.0 collective-permute-done
  50.3 2.6 %collective-permute-start.3 = (bf16[32,512]{1,0:T(8,128)(2,1)S(1)}, bf16[32,512]{1,0:T(8,128)(2,1)S(1)}, u32[]{:S(2)}, u32[]{:S(2)}) collective-permute-start(bf16[32,512]{1,0:T(8,128)(2,1)S(1)} %add_convert_fusion.refs_0_), channel_id=1, source_target_pairs={{0,6},{1,7},{2,4},{3,5},{4,2},{5,3},{6,0},{7,1},{8,14},{9,15},{10,... | collective-permute-start | bytes 98312 | tf_op jit(solution)/shard_map/ppermute | solution.py:220
  52.9 2.8 %solve.1.refs_2_ = f32[32,32]{1,0:T(8,128)S(1)} custom-call(f32[32,32]{1,0:T(8,128)S(1)} %get-tuple-element.20.gram), custom_call_target="tpu_custom_call" | custom-call | flops 8388608 | bytes 4194304 | tf_op jit(solution)/shard_map/solve/pallas_call | solution.py:140
  55.6 0.0 collective-permute-done.3.refs_1_
  55.6 2.7 %finish.1 = (bf16[1,4096,512]{2,1,0:T(8,128)(2,1)}, f32[32,512]{1,0:T(8,128)}) custom-call(bf16[32,512]{1,0:T(8,128)(2,1)S(1)} %add_convert_fusion.refs_0_, bf16[32,512]{1,0:T(8,128)(2,1)S(1)} %collective-permute-done.3.refs_1_, f32[32,32]{1,0:T(8,128)S(1)} %solve.1.refs_2_, bf16[4096,64]{1,0:T(8,128)(2,1)S(1)} %get-tuple-element.23.refs_3_, ...), custom_call_target="tpu_custom_call" | custom-call | flops 268435456 | bytes 8388608 | tf_op jit(solution)/shard_map/finish/pallas_call | solution.py:176
  (5 shorter events, 0.1 us)
Async XLA Ops:
  44.0 4.6 %collective-permute-start.2 = (bf16[32,512]{1,0:T(8,128)(2,1)S(1)}, bf16[32,512]{1,0:T(8,128)(2,1)S(1)}, u32[]{:S(2)}, u32[]{:S(2)}) collective-permute-start(bf16[32,512]{1,0:T(8,128)(2,1)S(1)} %raw_factor.1), channel_id=1, source_target_pairs={{0,3},{1,2},{2,1},{3,0},{4,7},{5,6},{6,5},{7,4},{8,11},{9,10},{10,... | collective-permute-start | bytes 98312 | tf_op jit(solution)/shard_map/ppermute | solution.py:220
  45.9 4.3 %collective-permute-start.1 = (bf16[32,512]{1,0:T(8,128)(2,1)S(1)}, bf16[32,512]{1,0:T(8,128)(2,1)S(1)}, u32[]{:S(2)}, u32[]{:S(2)}) collective-permute-start(bf16[32,512]{1,0:T(8,128)(2,1)S(1)} %raw_factor.1), channel_id=1, source_target_pairs={{0,2},{1,3},{2,0},{3,1},{4,6},{5,7},{6,4},{7,5},{8,10},{9,11},{10,... | collective-permute-start | bytes 98312 | tf_op jit(solution)/shard_map/ppermute | solution.py:220
  46.0 4.3 %collective-permute-start = (bf16[32,512]{1,0:T(8,128)(2,1)S(1)}, bf16[32,512]{1,0:T(8,128)(2,1)S(1)}, u32[]{:S(2)}, u32[]{:S(2)}) collective-permute-start(bf16[32,512]{1,0:T(8,128)(2,1)S(1)} %raw_factor.1), channel_id=1, source_target_pairs={{0,1},{1,0},{2,3},{3,2},{4,5},{5,4},{6,7},{7,6},{8,9},{9,8},{10,11... | collective-permute-start | bytes 98312 | tf_op jit(solution)/shard_map/ppermute | solution.py:220
  50.3 5.3 %collective-permute-start.3 = (bf16[32,512]{1,0:T(8,128)(2,1)S(1)}, bf16[32,512]{1,0:T(8,128)(2,1)S(1)}, u32[]{:S(2)}, u32[]{:S(2)}) collective-permute-start(bf16[32,512]{1,0:T(8,128)(2,1)S(1)} %add_convert_fusion.refs_0_), channel_id=1, source_target_pairs={{0,6},{1,7},{2,4},{3,5},{4,2},{5,3},{6,0},{7,1},{8,14},{9,15},{10,... | collective-permute-start | bytes 98312 | tf_op jit(solution)/shard_map/ppermute | solution.py:220

commit v14 on v13

--- a/solution.py
+++ b/solution.py
@@ -148,15 +148,26 @@
     )(in_vmem(gram))
 
 
+def terms_of(value, count):
+    terms = []
+    for _ in range(count):
+        terms.append(value.astype(BF16))
+        value = value - terms[-1].astype(F32)
+    return terms
+
+
 def finish_kernel(replicas, mine, theirs, inverse, turned, merged, new_error, q_factor, halves, result, factor_out, done):
-    raw = mine[...].astype(F32) + theirs[...].astype(F32)
-    factor = jnp.dot(inverse[...], raw, precision=HIGHEST, preferred_element_type=F32) * (1.0 / replicas)
+    raw = terms_of(mine[...].astype(F32) + theirs[...].astype(F32), 2)
+    lower = terms_of(inverse[...], 3)
+    factor = jnp.dot(jnp.concatenate(lower, axis=1), jnp.concatenate([raw[0]] * 3), preferred_element_type=F32)
+    factor += jnp.dot(jnp.concatenate(lower[:2], axis=1), jnp.concatenate([raw[1]] * 2), preferred_element_type=F32)
+    factor *= 1.0 / replicas
     factor_out[...] = factor
     copies = [pltpu.make_async_copy(factor_out, q_factor, done.at[merged.shape[0] // STEP])]
     copies[0].start()
-    rounded = factor.astype(BF16).astype(F32)
+    rounded = factor.astype(BF16)
     solved = lax.dot_general(
-        inverse[...], rounded, (((0,), (0,)), ((), ())), precision=HIGHEST, preferred_element_type=F32
+        jnp.concatenate(lower), jnp.concatenate([rounded] * 3), (((0,), (0,)), ((), ())), preferred_element_type=F32
     )
     high = solved.astype(BF16)
     halves[...] = jnp.concatenate([high, (solved - high.astype(F32)).astype(BF16)], axis=0)

time: 59.4 us -> 59.3 us (level)
  no operation moved by 1% of the time
where the time goes in v14:
time: 59.3 us; the launch traced here: 58.3 us
  blocking collectives  38.6 us (65%)
  Pallas kernels  10.7 us (18%)
  starting transfers between devices  6.12 us (10%)
  waiting for transfers between devices  2.08 us (4%)
  between operations  0.67 us (1%)
    all_to_all x3, blocking collectives, exchange(): lax.all_to_all(blocks, axis, 0, 0, axis_index_groups=[places], tiled=True)  38.6 us
    ppermute x4, starting transfers between devices, swap(): lax.ppermute(block, axis, [(i, i ^ mask) for i in range(lax.axis_size(axi...  6.12 us
    pallas_call x1, Pallas kernels, merge(): pl.pallas_call(merge_kernel, in_specs=[ANYWHERE] * 3, out_specs=[WHOLE, W...  3.81 us
    pallas_call x1, Pallas kernels, solve(): pl.pallas_call(solve_kernel, in_specs=[WHOLE], out_specs=WHOLE, out_shape...  2.76 us
    pallas_call x1, Pallas kernels, finish(): pl.pallas_call(lambda *refs: finish_kernel(replicas, *refs), in_specs=[WH...  2.7 us
    ppermute x4, waiting for transfers between devices, swap(): lax.ppermute(block, axis, [(i, i ^ mask) for i in range(lax.axis_size(axi...  2.08 us
  transfers between devices with their start and end apart: 4, of which 2 were waited for; matrix products, arithmetic and copies ran while one was open for 0% of the time, Pallas kernels for 6%

profile of v14, /device:TPU:1, one launch (start us, length us, event | category | flops | bytes accessed | tf_op | source)
XLA Modules:
  0.0 58.3 jit_solution(15765360915680244898)
XLA Ops:
  0.6 3.8 %merge.1 = (bf16[4096,512]{1,0:T(8,128)(2,1)S(1)}, bf16[32,32,128]{2,1,0:T(8,128)(2,1)S(1)}) custom-call(bf16[1,4096,512]{2,1,0:T(8,128)(2,1)} %gradient.1, bf16[1,4096,512]{2,1,0:T(8,128)(2,1)} %error.1, bf16[32,512]{1,0:T(8,128)(2,1)} %warm.1), custom_call_target="tpu_custom_call" | custom-call | flops 134217728 | bytes 8388608 | tf_op jit(solution)/shard_map/merge/pallas_call | solution.py:60
  4.4 13.9 %all_to_all.15 = bf16[32,32,128]{2,1,0:T(8,128)(2,1)S(1)} all-to-all(bf16[32,32,128]{2,1,0:T(8,128)(2,1)S(1)} %get-tuple-element.13), channel_id=1, replica_groups={{168,160,104,152,184,232,96,144,176,224,40,88,120,136,216,248,32,80,112..., dimensions={0} | all-to-all | bytes 524288 | tf_op jit(solution)/shard_map/all_to_all | solution.py:216
  18.4 11.7 %all_to_all.16 = bf16[8,32,128]{2,1,0:T(8,128)(2,1)S(1)} all-to-all(bf16[8,32,128]{2,1,0:T(8,128)(2,1)S(1)} %broadcast_in_dim.17), channel_id=1, replica_groups={{5,4,6,3,7,0,2,1},{13,12,14,11,15,8,10,9},{21,20,22,19,23,16,18,17},{29..., dimensions={0} | all-to-all | bytes 131072 | tf_op jit(solution)/shard_map/all_to_all | solution.py:216
  30.2 13.0 %all_to_all.17.p_sum = bf16[32,32,128]{2,1,0:T(8,128)(2,1)S(1)} all-to-all(bf16[32,32,128]{2,1,0:T(8,128)(2,1)S(1)} %broadcast_in_dim.19), channel_id=1, replica_groups={{168,160,104,152,184,232,96,144,176,224,40,88,120,136,216,248,32,80,112..., dimensions={0} | all-to-all | bytes 524288 | tf_op jit(solution)/shard_map/all_to_all | solution.py:216
  43.2 0.8 %raw_factor.1 = bf16[32,512]{1,0:T(8,128)(2,1)S(1)} custom-call(bf16[32,32,128]{2,1,0:T(8,128)(2,1)S(1)} %all_to_all.17.p_sum, bf16[4096,512]{1,0:T(8,128)(2,1)S(1)} %get-tuple-element.14.merged.refs_4_), custom_call_target="tpu_custom_call" | custom-call | flops 134217728 | bytes 4194304 | tf_op jit(solution)/shard_map/raw_factor/pallas_call | solution.py:91
  44.0 1.9 %collective-permute-start.2 = (bf16[32,512]{1,0:T(8,128)(2,1)S(1)}, bf16[32,512]{1,0:T(8,128)(2,1)S(1)}, u32[]{:S(2)}, u32[]{:S(2)}) collective-permute-start(bf16[32,512]{1,0:T(8,128)(2,1)S(1)} %raw_factor.1), channel_id=1, source_target_pairs={{0,3},{1,2},{2,1},{3,0},{4,7},{5,6},{6,5},{7,4},{8,11},{9,10},{10,... | collective-permute-start | bytes 98312 | tf_op jit(solution)/shard_map/ppermute | solution.py:231
  45.9 0.0 collective-permute-start.1
  46.0 1.6 %collective-permute-start = (bf16[32,512]{1,0:T(8,128)(2,1)S(1)}, bf16[32,512]{1,0:T(8,128)(2,1)S(1)}, u32[]{:S(2)}, u32[]{:S(2)}) collective-permute-start(bf16[32,512]{1,0:T(8,128)(2,1)S(1)} %raw_factor.1), channel_id=1, source_target_pairs={{0,1},{1,0},{2,3},{3,2},{4,5},{5,4},{6,7},{7,6},{8,9},{9,8},{10,11... | collective-permute-start | bytes 98312 | tf_op jit(solution)/shard_map/ppermute | solution.py:231
  47.6 0.6 %turn.1 = (f32[32,32]{1,0:T(8,128)S(1)}, bf16[4096,64]{1,0:T(8,128)(2,1)S(1)}) custom-call(bf16[32,32,128]{2,1,0:T(8,128)(2,1)S(1)} %all_to_all.17.p_sum), custom_call_target="tpu_custom_call" | custom-call | flops 33554432 | bytes 2097152 | tf_op jit(solution)/shard_map/turn/pallas_call | solution.py:113
  48.2 0.4 collective-permute-done.2
  48.6 1.7 %collective-permute-done.1 = bf16[32,512]{1,0:T(8,128)(2,1)S(1)} collective-permute-done((bf16[32,512]{1,0:T(8,128)(2,1)S(1)}, bf16[32,512]{1,0:T(8,128)(2,1)S(1)}, u32[]{:S(2)}, u32[]{:S(2)}) %collective-permute-start.1) | collective-permute-done | bytes 32800 | tf_op jit(solution)/shard_map/ppermute | solution.py:231
  50.3 0.0 collective-permute-done
  50.3 2.6 %collective-permute-start.3 = (bf16[32,512]{1,0:T(8,128)(2,1)S(1)}, bf16[32,512]{1,0:T(8,128)(2,1)S(1)}, u32[]{:S(2)}, u32[]{:S(2)}) collective-permute-start(bf16[32,512]{1,0:T(8,128)(2,1)S(1)} %add_convert_fusion.refs_0_), channel_id=1, source_target_pairs={{0,6},{1,7},{2,4},{3,5},{4,2},{5,3},{6,0},{7,1},{8,14},{9,15},{10,... | collective-permute-start | bytes 98312 | tf_op jit(solution)/shard_map/ppermute | solution.py:231
  52.9 2.8 %solve.1.refs_2_ = f32[32,32]{1,0:T(8,128)S(1)} custom-call(f32[32,32]{1,0:T(8,128)S(1)} %get-tuple-element.20.gram), custom_call_target="tpu_custom_call" | custom-call | flops 8388608 | bytes 4194304 | tf_op jit(solution)/shard_map/solve/pallas_call | solution.py:140
  55.6 0.0 collective-permute-done.3.refs_1_
  55.6 2.7 %finish.1 = (bf16[1,4096,512]{2,1,0:T(8,128)(2,1)}, f32[32,512]{1,0:T(8,128)}) custom-call(bf16[32,512]{1,0:T(8,128)(2,1)S(1)} %add_convert_fusion.refs_0_, bf16[32,512]{1,0:T(8,128)(2,1)S(1)} %collective-permute-done.3.refs_1_, f32[32,32]{1,0:T(8,128)S(1)} %solve.1.refs_2_, bf16[4096,64]{1,0:T(8,128)(2,1)S(1)} %get-tuple-element.23.refs_3_, ...), custom_call_target="tpu_custom_call" | custom-call | flops 268435456 | bytes 8388608 | tf_op jit(solution)/shard_map/finish/pallas_call | solution.py:187
  (5 shorter events, 0.1 us)
Async XLA Ops:
  44.0 4.6 %collective-permute-start.2 = (bf16[32,512]{1,0:T(8,128)(2,1)S(1)}, bf16[32,512]{1,0:T(8,128)(2,1)S(1)}, u32[]{:S(2)}, u32[]{:S(2)}) collective-permute-start(bf16[32,512]{1,0:T(8,128)(2,1)S(1)} %raw_factor.1), channel_id=1, source_target_pairs={{0,3},{1,2},{2,1},{3,0},{4,7},{5,6},{6,5},{7,4},{8,11},{9,10},{10,... | collective-permute-start | bytes 98312 | tf_op jit(solution)/shard_map/ppermute | solution.py:231
  45.9 4.3 %collective-permute-start.1 = (bf16[32,512]{1,0:T(8,128)(2,1)S(1)}, bf16[32,512]{1,0:T(8,128)(2,1)S(1)}, u32[]{:S(2)}, u32[]{:S(2)}) collective-permute-start(bf16[32,512]{1,0:T(8,128)(2,1)S(1)} %raw_factor.1), channel_id=1, source_target_pairs={{0,2},{1,3},{2,0},{3,1},{4,6},{5,7},{6,4},{7,5},{8,10},{9,11},{10,... | collective-permute-start | bytes 98312 | tf_op jit(solution)/shard_map/ppermute | solution.py:231
  46.0 4.3 %collective-permute-start = (bf16[32,512]{1,0:T(8,128)(2,1)S(1)}, bf16[32,512]{1,0:T(8,128)(2,1)S(1)}, u32[]{:S(2)}, u32[]{:S(2)}) collective-permute-start(bf16[32,512]{1,0:T(8,128)(2,1)S(1)} %raw_factor.1), channel_id=1, source_target_pairs={{0,1},{1,0},{2,3},{3,2},{4,5},{5,4},{6,7},{7,6},{8,9},{9,8},{10,11... | collective-permute-start | bytes 98312 | tf_op jit(solution)/shard_map/ppermute | solution.py:231
  50.3 5.3 %collective-permute-start.3 = (bf16[32,512]{1,0:T(8,128)(2,1)S(1)}, bf16[32,512]{1,0:T(8,128)(2,1)S(1)}, u32[]{:S(2)}, u32[]{:S(2)}) collective-permute-start(bf16[32,512]{1,0:T(8,128)(2,1)S(1)} %add_convert_fusion.refs_0_), channel_id=1, source_target_pairs={{0,6},{1,7},{2,4},{3,5},{4,2},{5,3},{6,0},{7,1},{8,14},{9,15},{10,... | collective-permute-start | bytes 98312 | tf_op jit(solution)/shard_map/ppermute | solution.py:231
